TPU v7x, 256 devices: a whole 4x4x8 slice. The times are simulated.
256 devices in a mesh: pipe: 16 (over x_hi, y, core), dp: 16 (over z, x_lo).
Axes of the slice: x: 4 (x_hi: 2, x_lo: 2; x = x_hi * 2 + x_lo), y: 4, z: 8, core: 2. Of those that a mesh axis runs over, the one named last changes fastest.
Arguments:
- fwd_in: bfloat16 [16, 1024, 3200], P('pipe', 'dp'), may hold values from -6 to 6
- fwd_ids: int32 [16, 1024], P('pipe', 'dp'), may hold values from 0 to 15, as said below
- fwd_lengths: int32 [16, 16], P('pipe', 'dp'), may hold values from 1 to 64
- bwd_in: bfloat16 [16, 1024, 3200], P('pipe', 'dp'), may hold values from -6 to 6
- bwd_grad: bfloat16 [16, 1024, 3200], P('pipe', 'dp'), may hold values from -6 to 6
- bwd_ids: int32 [16, 1024], P('pipe', 'dp'), may hold values from 0 to 15, as said below
- bwd_lengths: int32 [16, 16], P('pipe', 'dp'), may hold values from 1 to 64
- norm_gain: float32 [16, 3200], P('pipe'), may hold values from 0.1 to 1.9
- router: bfloat16 [16, 3200], P('pipe'), may hold values from -0.109375 to 0.109375
- w_gate: bfloat16 [16, 3200, 9216], P('pipe', None, 'dp'), may hold values from -0.109375 to 0.109375
- w_up: bfloat16 [16, 3200, 9216], P('pipe', None, 'dp'), may hold values from -0.109375 to 0.109375
- w_down: bfloat16 [16, 9216, 3200], P('pipe', 'dp'), may hold values from -0.0625 to 0.0625
Outputs:
- fwd_out: bfloat16 [16, 1024, 3200], P('pipe', 'dp')
- bwd_out: bfloat16 [16, 1024, 3200], P('pipe', 'dp')
Inputs may be any that keep to these rules, and one draw needn't show every extreme that they name: `fwd_ids`: expert 0 is the one held in this window. In the 64 tokens of one device at one section, between 1 and 8 tokens name expert 0; in every section some device has exactly 8, and in some section every device has 8. `bwd_ids`: like fwd_ids.
All inputs are finite; a program needn't handle non-finite values.
Results may differ from a plain program's by a relative error of at most 0.008.
Values may be sent and summed in bfloat16 or wider, within the bound.
No kernel may reach another device: no remote copies, remote signals or barrier semaphores. Data moves between devices by JAX's collectives and lax.ppermute only.
A program may use at most 64 MiB of HBM per device.

v0:
```python
import jax
import jax.numpy as jnp
from jax import lax
from jax.sharding import PartitionSpec as P

EXPERTS = 16


EPS = 1e-05


def shifted(value, axis, steps):
    count = lax.axis_size(axis)
    pairs = [(source, (source + steps) % count) for source in range(count)]
    return lax.ppermute(value, axis, pairs)


def normalize(tokens, norm_w):
    values = tokens.astype(jnp.float32)
    inv_scale = lax.rsqrt(jnp.mean(values * values, axis=-1, keepdims=True) + EPS)
    return (values, inv_scale, (values * inv_scale * norm_w).astype(jnp.bfloat16))


def placement_matrix(route_ids, capacity):
    chosen = (route_ids == 0).astype(jnp.int32)
    slot_rank = jnp.cumsum(chosen) - 1
    target = jnp.where(chosen == 1, slot_rank, capacity)
    return (target[None, :] == jnp.arange(capacity, dtype=jnp.int32)[:, None]).astype(jnp.bfloat16)


def pack_rows(placing, tok_rows):
    return jnp.dot(placing, tok_rows, preferred_element_type=jnp.float32).astype(jnp.bfloat16)


def unpack_rows(placing, buffer):
    return lax.dot_general(
        placing, buffer, (((0,), (0,)), ((), ())), preferred_element_type=jnp.float32
    )


def body(
    fwd_in,
    fwd_ids,
    fwd_lengths,
    bwd_in,
    bwd_grad,
    bwd_ids,
    bwd_lengths,
    norm_gain,
    router,
    w_gate,
    w_up,
    w_down,
):
    tok_count = fwd_in.shape[1]
    capacity = max(2, 2 * tok_count // EXPERTS)
    norm_w = norm_gain[0]
    router_w = router[0]
    gate_w = w_gate[0]
    up_w = w_up[0]
    down_w = w_down[0]
    positions = jnp.arange(tok_count, dtype=jnp.int32)

    def hidden_parts(slot_rows):
        gate_pre = jnp.dot(slot_rows, gate_w, preferred_element_type=jnp.float32)
        up_pre = jnp.dot(slot_rows, up_w, preferred_element_type=jnp.float32)
        hidden = (gate_pre * jax.nn.sigmoid(gate_pre) * up_pre).astype(jnp.bfloat16)
        return (gate_pre, up_pre, hidden)

    f_values, f_inv, f_normed = normalize(fwd_in[0], norm_w)
    f_place = placement_matrix(fwd_ids[0], capacity)
    f_mask = (positions < fwd_lengths[0, 0]).astype(jnp.float32)
    f_prob = jax.nn.sigmoid(jnp.dot(f_normed, router_w, preferred_element_type=jnp.float32))
    f_send = pack_rows(f_place, f_normed)
    b_values, b_inv, b_normed = normalize(bwd_in[0], norm_w)
    b_place = placement_matrix(bwd_ids[0], capacity)
    b_mask = (positions < bwd_lengths[0, 0]).astype(jnp.float32)
    b_prob = jax.nn.sigmoid(jnp.dot(b_normed, router_w, preferred_element_type=jnp.float32))
    grad32 = bwd_grad[0].astype(jnp.float32)
    scaled_grad = (grad32 * b_mask[:, None]).astype(jnp.bfloat16)
    b_send = pack_rows(b_place, b_normed)
    g_send = pack_rows(b_place, scaled_grad)
    f_hidden = hidden_parts(lax.all_gather(f_send, "dp", axis=0, tiled=True))[2]
    b_rows, g_rows = (
        lax.all_gather(b_send, "dp", axis=0, tiled=True),
        lax.all_gather(g_send, "dp", axis=0, tiled=True),
    )
    f_back = lax.psum_scatter(
        jnp.dot(f_hidden, down_w, preferred_element_type=jnp.float32).astype(jnp.bfloat16),
        "dp",
        scatter_dimension=0,
        tiled=True,
    )
    gate_pre, up_pre, hidden = hidden_parts(b_rows)
    d_hidden = lax.dot_general(
        g_rows, down_w, (((1,), (1,)), ((), ())), preferred_element_type=jnp.float32
    )
    dot_part = jnp.sum(hidden.astype(jnp.float32) * d_hidden, axis=1)
    gate_sig = jax.nn.sigmoid(gate_pre)
    d_gate = (d_hidden * up_pre * gate_sig * (1.0 + gate_pre * (1.0 - gate_sig))).astype(
        jnp.bfloat16
    )
    d_up = (d_hidden * gate_pre * gate_sig).astype(jnp.bfloat16)
    d_part = lax.dot_general(
        d_gate, gate_w, (((1,), (1,)), ((), ())), preferred_element_type=jnp.float32
    )
    d_part = d_part + lax.dot_general(
        d_up, up_w, (((1,), (1,)), ((), ())), preferred_element_type=jnp.float32
    )
    d_part, dot_part = (d_part, dot_part)
    d_own, dot_own = (
        lax.psum_scatter(d_part.astype(jnp.bfloat16), "dp", scatter_dimension=0, tiled=True).astype(
            jnp.float32
        ),
        lax.psum_scatter(
            dot_part.astype(jnp.bfloat16), "dp", scatter_dimension=0, tiled=True
        ).astype(jnp.float32),
    )
    layer_out = (f_values + (f_mask * f_prob)[:, None] * unpack_rows(f_place, f_back)).astype(
        jnp.bfloat16
    )
    d_tok = unpack_rows(b_place, d_own.astype(jnp.bfloat16))
    dot_tok = jnp.dot(dot_own, b_place.astype(jnp.float32), precision=lax.Precision.HIGHEST)
    d_logit = b_mask * dot_tok * b_prob * (1.0 - b_prob)
    d_normed = b_prob[:, None] * d_tok + d_logit[:, None] * router_w.astype(jnp.float32)[None, :]
    weighted = norm_w * d_normed
    inner = jnp.mean(weighted * b_values, axis=-1, keepdims=True)
    d_input = (grad32 + b_inv * weighted - b_values * b_inv * b_inv * b_inv * inner).astype(
        jnp.bfloat16
    )
    fwd_out = shifted(layer_out[None], "pipe", 1)
    bwd_out = shifted(d_input[None], "pipe", -1)
    return (fwd_out, bwd_out)


def solution(mesh):
    in_specs = (
        P("pipe", "dp", None),
        P("pipe", "dp"),
        P("pipe", "dp"),
        P("pipe", "dp", None),
        P("pipe", "dp", None),
        P("pipe", "dp"),
        P("pipe", "dp"),
        P("pipe", None),
        P("pipe", None),
        P("pipe", None, "dp"),
        P("pipe", None, "dp"),
        P("pipe", "dp", None),
    )
    out_specs = (P("pipe", "dp", None), P("pipe", "dp", None))
    return jax.shard_map(body, mesh=mesh, in_specs=in_specs, out_specs=out_specs, check_vma=False)
```

profile of v0, /device:TPU:4, one launch (start us, length us, event | category | flops | bytes accessed | tf_op | source)
XLA Modules:
  0.0 307.7 jit_solution(17471021301794332227)
XLA Ops:
  7.2 0.0 all-reduce.6.cloned.1.call-start
  7.2 0.7 compare_convert_fusion
  7.9 0.2 reduce-window_1_clone.1
  8.1 0.7 fusion.101
  8.8 1.2 fusion.55
  10.0 0.8 reduce
  10.7 0.0 copy-start
  10.7 1.4 convolution_convert_fusion.1
  12.2 41.0 %all_gather.11 = bf16[128,3200]{1,0:T(8,128)(2,1)S(1)} all-gather(bf16[8,3200]{1,0:T(8,128)(2,1)S(1)} %convolution_convert_fusion.1), channel_id=1, replica_groups=mesh['pipe'=16,'dp'=16] {'dp'}, dimensions={0}, use_global_device_ids=true | all-gather | bytes 870400 | tf_op jit(solution)/shard_map/all_gather | solution.py:85
  53.2 3.2 %fusion.16 = f32[128,576]{0,1:T(8,128)S(1)} fusion(bf16[128,3200]{1,0:T(8,128)(2,1)S(1)} %all_gather.11, bf16[1,3200,576]{1,2,0:T(8,128)(2,1)} %param.21), kind=kOutput, calls=%fused_computation.23 | convolution fusion | flops 471859200 | bytes 4800512 | tf_op jit(solution)/shard_map/dot_general | solution.py:65
  56.4 0.0 copy-start.2
  56.4 1.1 fusion.10
  57.6 0.0 copy-start.1
  58.4 0.0 copy-done.4
  58.4 0.2 convolution_convert_fusion.2
  58.6 34.8 %all_gather.10 = bf16[128,3200]{1,0:T(8,128)(2,1)S(1)} all-gather(bf16[8,3200]{1,0:T(8,128)(2,1)S(1)} %convolution_convert_fusion.2), channel_id=1, replica_groups=mesh['pipe'=16,'dp'=16] {'dp'}, dimensions={0}, use_global_device_ids=true | all-gather | bytes 870400 | tf_op jit(solution)/shard_map/all_gather | solution.py:86
  93.5 1.1 multiply_reduce_fusion
  94.6 0.0 copy-done.1
  94.6 0.9 fusion.14
  95.5 0.0 copy-start.7
  95.5 0.0 copy-start.5
  95.6 1.8 fusion
  97.3 0.2 reduce-window_clone.1
  97.6 0.2 fusion.50
  97.8 0.3 convolution_convert_fusion.3
  98.1 37.4 %all_gather.9 = bf16[128,3200]{1,0:T(8,128)(2,1)S(1)} all-gather(bf16[8,3200]{1,0:T(8,128)(2,1)S(1)} %convolution_convert_fusion.3), channel_id=1, replica_groups=mesh['pipe'=16,'dp'=16] {'dp'}, dimensions={0}, use_global_device_ids=true | all-gather | bytes 870400 | tf_op jit(solution)/shard_map/all_gather | solution.py:83
  135.5 3.1 %fusion.18 = f32[128,576]{0,1:T(8,128)S(1)} fusion(bf16[128,3200]{1,0:T(8,128)(2,1)S(1)} %all_gather.9, bf16[1,3200,576]{1,2,0:T(8,128)(2,1)} %param.21), kind=kOutput, calls=%fused_computation.25 | convolution fusion | flops 471859200 | bytes 4800512 | tf_op jit(solution)/shard_map/dot_general | solution.py:65
  138.7 0.0 copy-start.6
  138.7 0.0 copy-start.8
  138.7 0.0 copy-start.3
  138.7 7.2 %convolution_convert_fusion = bf16[128,3200]{1,0:T(8,128)(2,1)} fusion(bf16[1,576,3200]{2,1,0:T(8,128)(2,1)} %param.23, bf16[128,3200]{1,0:T(8,128)(2,1)S(1)} %all_gather.9, bf16[1,3200,576]{1,2,0:T(8,128)(2,1)} %param.22, f32[128,576]{0,1:T(8,128)S(1)} %fusion.18), kind=kOutput, calls=%fused_computation.2 | convolution fusion | flops 944570368 | bytes 9306112 | tf_op jit(solution)/shard_map/dot_general | solution.py:89
  145.9 0.0 all-reduce.6.cloned.1.call-update
  146.0 0.1 reduce.1
  146.7 0.6 dynamic-slice
  147.9 30.8 %all-reduce.2 = bf16[128]{0:T(256)(128)(2,1)S(1)} all-reduce(bf16[128]{0:T(256)(128)(2,1)S(1)} %get-tuple-element.4), channel_id=4, replica_groups=mesh['pipe'=16,'dp'=16] {'dp'}, use_global_device_ids=true, to_apply=%region_7.8.clone | all-reduce | flops 128 | bytes 512
  178.6 0.3 fusion.34
  178.9 0.2 fusion.37
  179.1 0.3 fusion.32
  179.4 106.0 %all-reduce.6.cloned.1.call-done = (bf16[128,3200]{1,0:T(8,128)(2,1)}, bf16[128,3200]{1,0:T(8,128)(2,1)}) async-done(((bf16[128,3200]{1,0:T(8,128)(2,1)}, bf16[128,3200]{1,0:T(8,128)(2,1)}), (bf16[128,3200]{1,0:T(8,128)(2,1)}, bf16[128,3200]{1,0:T(8,128)(2,1)})) %all-reduce.6.cloned.1.call-update) | async-done | bytes 1638416
  285.4 1.3 fusion.56
  286.7 0.3 fusion.68
  287.1 0.1 collective-permute-start.1
  287.2 1.1 fusion.5
  288.3 0.6 collective-permute-start
  288.9 3.8 %collective-permute-done.1 = bf16[1,64,3200]{2,1,0:T(8,128)(2,1)S(1)} collective-permute-done((bf16[1,64,3200]{2,1,0:T(8,128)(2,1)S(1)}, bf16[1,64,3200]{2,1,0:T(8,128)(2,1)S(1)}, u32[]{:S(2)}, u32[]{:S(2)}) %collective-permute-start.1) | collective-permute-done | bytes 409632 | tf_op jit(solution)/shard_map/ppermute | solution.py:15
  292.6 6.7 %collective-permute-done = bf16[1,64,3200]{2,1,0:T(8,128)(2,1)S(1)} collective-permute-done((bf16[1,64,3200]{2,1,0:T(8,128)(2,1)S(1)}, bf16[1,64,3200]{2,1,0:T(8,128)(2,1)S(1)}, u32[]{:S(2)}, u32[]{:S(2)}) %collective-permute-start) | collective-permute-done | bytes 409632 | tf_op jit(solution)/shard_map/ppermute | solution.py:15
  299.4 0.8 copy.20
  300.1 0.8 copy.21
  (15 shorter events, 0.1 us)
Async XLA Ops:
  7.2 278.3 %all-reduce.6.cloned.1.call-start = ((), (), s32[]{:S(2)}) async-start(), calls=%async_computation | async-start | bytes 3276800
  10.7 45.7 %copy-start = (bf16[1,3200,576]{1,2,0:T(8,128)(2,1)S(1)}, bf16[1,3200,576]{1,2,0:T(8,128)(2,1)}, u32[]{:S(2)}) copy-start(bf16[1,3200,576]{1,2,0:T(8,128)(2,1)} %param.22) | copy-start | bytes 11059204
  53.2 5.2 %copy-start.4 = (bf16[1,64,3200]{2,1,0:T(8,128)(2,1)S(1)}, bf16[1,64,3200]{2,1,0:T(8,128)(2,1)}, u32[]{:S(2)}) copy-start(bf16[1,64,3200]{2,1,0:T(8,128)(2,1)} %param.16) | copy-start | bytes 1228804
  56.4 37.1 %copy-start.2 = (bf16[1,576,3200]{2,1,0:T(8,128)(2,1)S(1)}, bf16[1,576,3200]{2,1,0:T(8,128)(2,1)}, u32[]{:S(2)}) copy-start(bf16[1,576,3200]{2,1,0:T(8,128)(2,1)} %param.23) | copy-start | bytes 11059204
  57.6 37.1 %copy-start.1 = (bf16[1,3200,576]{1,2,0:T(8,128)(2,1)S(1)}, bf16[1,3200,576]{1,2,0:T(8,128)(2,1)}, u32[]{:S(2)}) copy-start(bf16[1,3200,576]{1,2,0:T(8,128)(2,1)} %param.21) | copy-start | bytes 11059204
  95.5 1.8 copy-start.7
  95.5 2.1 copy-start.5
  138.7 7.3 %copy-start.6 = (bf16[1,3200]{1,0:T(2,128)(2,1)S(1)}, bf16[1,3200]{1,0:T(2,128)(2,1)}, u32[]{:S(2)}) copy-start(bf16[1,3200]{1,0:T(2,128)(2,1)} %param.20) | copy-start | bytes 19204
  138.7 8.0 %copy-start.8 = (u32[256]{0:T(256)S(1)}, u32[256]{0:T(256)}, u32[]{:S(2)}) copy-start(u32[256]{0:T(256)} %constant.41) | copy-start | bytes 3076
  138.7 40.0 %copy-start.3 = (bf16[1,64,3200]{2,1,0:T(8,128)(2,1)S(1)}, bf16[1,64,3200]{2,1,0:T(8,128)(2,1)}, u32[]{:S(2)}) copy-start(bf16[1,64,3200]{2,1,0:T(8,128)(2,1)} %param.15) | copy-start | bytes 1228804
  287.1 5.6 %collective-permute-start.1 = (bf16[1,64,3200]{2,1,0:T(8,128)(2,1)S(1)}, bf16[1,64,3200]{2,1,0:T(8,128)(2,1)S(1)}, u32[]{:S(2)}, u32[]{:S(2)}) collective-permute-start(bf16[1,64,3200]{2,1,0:T(8,128)(2,1)S(1)} %fusion.68), channel_id=1, source_target_pairs={{0,240},{16,0},{32,16},{48,32},{64,48},{80,64},{96,80},{112,96},{1... | collective-permute-start | bytes 1228808 | tf_op jit(solution)/shard_map/ppermute | solution.py:15
  288.3 11.1 %collective-permute-start = (bf16[1,64,3200]{2,1,0:T(8,128)(2,1)S(1)}, bf16[1,64,3200]{2,1,0:T(8,128)(2,1)S(1)}, u32[]{:S(2)}, u32[]{:S(2)}) collective-permute-start(bf16[1,64,3200]{2,1,0:T(8,128)(2,1)S(1)} %fusion.5), channel_id=1, source_target_pairs={{0,16},{16,32},{32,48},{48,64},{64,80},{80,96},{96,112},{112,128},... | collective-permute-start | bytes 1228808 | tf_op jit(solution)/shard_map/ppermute | solution.py:15
Sparse Core Ops, SparseCore 0:
  146.1 139.3 all-reduce.5
where the time goes:
time: 308 us
  blocking collectives  144 us (47%)
  waiting for transfers between devices  117 us (38%)
  matrix products  23.7 us (8%)
  between operations  16.3 us (5%)
  other arithmetic  4.34 us (1%)
    unnamed x2, waiting for transfers between devices  106 us
    all_gather x1, blocking collectives, body(): lax.all_gather(b_send, 'dp', axis=0, tiled=True)  41 us
    all_gather x1, blocking collectives, body(): f_hidden = hidden_parts(lax.all_gather(f_send, 'dp', axis=0, tiled=True))[2]  37.4 us
    all_gather x1, blocking collectives, body(): lax.all_gather(g_send, 'dp', axis=0, tiled=True)  34.8 us
    unnamed x1, blocking collectives  30.8 us
    ppermute x2, waiting for transfers between devices, shifted(): return lax.ppermute(value, axis, pairs)  10.5 us
    dot_general x1, matrix products, body(): jnp.dot(f_hidden, down_w, preferred_element_type=jnp.float32)  7.25 us
    dot_general x2, matrix products, hidden_parts(): gate_pre = jnp.dot(slot_rows, gate_w, preferred_element_type=jnp.float32)  6.36 us
  transfers between devices with their start and end apart: 3, of which 3 were waited for; matrix products, arithmetic and copies ran while one was open for 1% of the time, Pallas kernels for 0%

commit v1 on v0

v1 whole, which is shorter than its diff:
```python
import jax
import jax.numpy as jnp
from jax import lax
from jax.sharding import PartitionSpec as P

EXPERTS = 16


EPS = 1e-05


def shifted(value, axis, steps):
    count = lax.axis_size(axis)
    pairs = [(source, (source + steps) % count) for source in range(count)]
    return lax.ppermute(value, axis, pairs)


def slot_of(route_ids, capacity):
    chosen = (route_ids == 0).astype(jnp.int32)
    return jnp.where(chosen == 1, jnp.cumsum(chosen) - 1, capacity)


def placement_matrix(target, capacity):
    return (target[None, :] == jnp.arange(capacity, dtype=jnp.int32)[:, None]).astype(jnp.bfloat16)


def pack_rows(placing, tok_rows):
    return jnp.dot(placing, tok_rows, preferred_element_type=jnp.float32)


def overlay(placing, rows, tokens):
    placed = lax.dot_general(
        placing, rows, (((0,), (0,)), ((), ())), preferred_element_type=jnp.float32
    ).astype(jnp.bfloat16)
    chosen = jnp.sum(placing.astype(jnp.float32), axis=0) > 0
    return jnp.where(chosen[:, None], placed, tokens)


def normalize(values, norm_w):
    inv_scale = lax.rsqrt(jnp.mean(values * values, axis=-1, keepdims=True) + EPS)
    return (inv_scale, (values * inv_scale * norm_w).astype(jnp.bfloat16))


def exchange(blocks):
    return lax.all_to_all(blocks, "dp", 0, 0, tiled=False)


def body(
    fwd_in,
    fwd_ids,
    fwd_lengths,
    bwd_in,
    bwd_grad,
    bwd_ids,
    bwd_lengths,
    norm_gain,
    router,
    w_gate,
    w_up,
    w_down,
):
    tok_count, width = fwd_in.shape[1:]
    capacity = max(2, 2 * tok_count // EXPERTS)
    n_dp = lax.axis_size("dp")
    norm_w = norm_gain[0]
    router_w = router[0]
    gate_w = w_gate[0]
    up_w = w_up[0]
    down_w = w_down[0]
    positions = jnp.arange(tok_count, dtype=jnp.int32)

    def hidden_parts(slot_rows):
        gate_pre = jnp.dot(slot_rows, gate_w, preferred_element_type=jnp.float32)
        up_pre = jnp.dot(slot_rows, up_w, preferred_element_type=jnp.float32)
        hidden = (gate_pre * jax.nn.sigmoid(gate_pre) * up_pre).astype(jnp.bfloat16)
        return (gate_pre, up_pre, hidden)

    def slot_side(tokens, ids, length):
        placing = placement_matrix(slot_of(ids, capacity), capacity)
        mask = (positions < length).astype(jnp.float32)
        slot_mask = jnp.sum(placing.astype(jnp.float32) * mask[None, :], axis=1)
        values = pack_rows(placing, tokens)
        inv, normed = normalize(values, norm_w)
        logit = jnp.dot(normed, router_w, preferred_element_type=jnp.float32)
        return placing, slot_mask, values, inv, normed, jax.nn.sigmoid(logit)

    next_tokens = shifted(fwd_in[0], "pipe", 1)
    next_ids = shifted(fwd_ids, "pipe", 1)
    prev_grads = shifted(bwd_grad[0], "pipe", -1)
    prev_ids = shifted(bwd_ids, "pipe", -1)

    b_place, b_mask, b_values, b_inv, b_normed, b_prob = slot_side(
        bwd_in[0], bwd_ids[0], bwd_lengths[0, 0]
    )
    g_values = pack_rows(b_place, bwd_grad[0])
    g_send = (g_values * b_mask[:, None]).astype(jnp.bfloat16)
    f_place, f_mask, f_values, f_inv, f_normed, f_prob = slot_side(
        fwd_in[0], fwd_ids[0], fwd_lengths[0, 0]
    )

    def gathered(rows):
        return exchange(jnp.broadcast_to(rows[None], (n_dp,) + rows.shape))

    bg_rows = gathered(jnp.concatenate([b_normed, g_send], axis=0))
    b_rows = bg_rows[:, :capacity].reshape(n_dp * capacity, width)
    g_rows = bg_rows[:, capacity:].reshape(n_dp * capacity, width)
    f_rows = gathered(f_normed).reshape(n_dp * capacity, width)

    gate_pre, up_pre, hidden = hidden_parts(b_rows)
    d_hidden = lax.dot_general(
        g_rows, down_w, (((1,), (1,)), ((), ())), preferred_element_type=jnp.float32
    )
    dot_part = jnp.sum(hidden.astype(jnp.float32) * d_hidden, axis=1)
    gate_sig = jax.nn.sigmoid(gate_pre)
    d_gate = (d_hidden * up_pre * gate_sig * (1.0 + gate_pre * (1.0 - gate_sig))).astype(
        jnp.bfloat16
    )
    d_up = (d_hidden * gate_pre * gate_sig).astype(jnp.bfloat16)
    d_part = lax.dot_general(
        d_gate, gate_w, (((1,), (1,)), ((), ())), preferred_element_type=jnp.float32
    )
    d_part = d_part + lax.dot_general(
        d_up, up_w, (((1,), (1,)), ((), ())), preferred_element_type=jnp.float32
    )
    dot_high = dot_part.astype(jnp.bfloat16)
    dot_low = (dot_part - dot_high.astype(jnp.float32)).astype(jnp.bfloat16)
    lanes = jnp.arange(128)[None, :]
    dot_cols = jnp.where(
        lanes == 0, dot_high[:, None], jnp.where(lanes == 1, dot_low[:, None], 0)
    ).astype(jnp.bfloat16)
    d_send = jnp.concatenate([d_part.astype(jnp.bfloat16), dot_cols], axis=1)
    d_got = exchange(d_send.reshape(n_dp, capacity, width + 128))
    d_sum = jnp.sum(d_got.astype(jnp.float32), axis=0)

    f_hidden = hidden_parts(f_rows)[2]
    f_part = jnp.dot(f_hidden, down_w, preferred_element_type=jnp.float32).astype(jnp.bfloat16)
    f_got = exchange(f_part.reshape(n_dp, capacity, width))
    f_back = jnp.sum(f_got.astype(jnp.float32), axis=0).astype(jnp.bfloat16)

    d_rows = d_sum[:, :width].astype(jnp.bfloat16).astype(jnp.float32)
    row_dot = d_sum[:, width] + d_sum[:, width + 1]
    d_logit = b_mask * row_dot * b_prob * (1.0 - b_prob)
    d_normed = b_prob[:, None] * d_rows + d_logit[:, None] * router_w.astype(jnp.float32)[None, :]
    weighted = norm_w * d_normed
    inner = jnp.mean(weighted * b_values, axis=-1, keepdims=True)
    d_input = (g_values + b_inv * weighted - b_values * b_inv * b_inv * b_inv * inner).astype(
        jnp.bfloat16
    )
    d_moved = shifted(d_input, "pipe", -1)
    layer_rows = (f_values + (f_mask * f_prob)[:, None] * f_back.astype(jnp.float32)).astype(
        jnp.bfloat16
    )
    f_moved = shifted(layer_rows, "pipe", 1)

    next_place = placement_matrix(slot_of(next_ids[0], capacity), capacity)
    prev_place = placement_matrix(slot_of(prev_ids[0], capacity), capacity)
    bwd_out = overlay(prev_place, d_moved, prev_grads)
    fwd_out = overlay(next_place, f_moved, next_tokens)
    return (fwd_out[None], bwd_out[None])


def solution(mesh):
    in_specs = (
        P("pipe", "dp", None),
        P("pipe", "dp"),
        P("pipe", "dp"),
        P("pipe", "dp", None),
        P("pipe", "dp", None),
        P("pipe", "dp"),
        P("pipe", "dp"),
        P("pipe", None),
        P("pipe", None),
        P("pipe", None, "dp"),
        P("pipe", None, "dp"),
        P("pipe", "dp", None),
    )
    out_specs = (P("pipe", "dp", None), P("pipe", "dp", None))
    return jax.shard_map(body, mesh=mesh, in_specs=in_specs, out_specs=out_specs, check_vma=False)
```

time: 308 us -> 169 us (0.55)
  blocking collectives: 144 us -> 0 us
  starting transfers between devices: 0.69 us -> 33.1 us
  waiting for transfers between devices: 117 us -> 102 us
  between operations: 16.3 us -> 2.27 us
    all_gather x3 -> x0, blocking collectives: 113 us -> none  [the longest x1 41 us: body(): lax.all_gather(b_send, 'dp', axis=0, tiled=True)]
    unnamed x2 -> x0, waiting for transfers between devices: 106 us -> none
    all_to_all x0 -> x4, waiting for transfers between devices: none -> 96.2 us  [exchange(): return lax.all_to_all(blocks, 'dp', 0, 0, tiled=False)]
    unnamed x1 -> x0, blocking collectives: 30.8 us -> none
    all_to_all x0 -> x4, starting transfers between devices: none -> 20.2 us  [exchange(): return lax.all_to_all(blocks, 'dp', 0, 0, tiled=False)]
    ppermute x2 -> x6, starting transfers between devices: 0.65 us -> 12.9 us  [shifted(): return lax.ppermute(value, axis, pairs)]
    ppermute x2 -> x6, waiting for transfers between devices: 10.5 us -> 6.05 us  [shifted(): return lax.ppermute(value, axis, pairs)]
  transfers between devices with their start and end apart: 3 -> 10, of which waited for: 3 -> 5; matrix products, arithmetic and copies ran while one was open for 1% -> 8% of each run, Pallas kernels for 0% -> 0%
where the time goes in v1:
time: 169 us; the launch traced here: 168 us
  waiting for transfers between devices  102 us (60%)
  starting transfers between devices  33.1 us (20%)
  matrix products  21.8 us (13%)
  other arithmetic  5.53 us (3%)
  local copies, waits for them, and re-layouts  3.19 us (2%)
  between operations  2.27 us (1%)
    all_to_all x4, waiting for transfers between devices, exchange(): return lax.all_to_all(blocks, 'dp', 0, 0, tiled=False)  96.2 us
    all_to_all x4, starting transfers between devices, exchange(): return lax.all_to_all(blocks, 'dp', 0, 0, tiled=False)  20.2 us
    ppermute x6, starting transfers between devices, shifted(): return lax.ppermute(value, axis, pairs)  12.9 us
    dot_general x1, matrix products, body(): jnp.dot(f_hidden, down_w, preferred_element_type=jnp.float32)  7.19 us
    dot_general x2, matrix products, hidden_parts(): gate_pre = jnp.dot(slot_rows, gate_w, preferred_element_type=jnp.float32)  6.45 us
    ppermute x6, waiting for transfers between devices, shifted(): return lax.ppermute(value, axis, pairs)  6.05 us
  transfers between devices with their start and end apart: 10, of which 5 were waited for; matrix products, arithmetic and copies ran while one was open for 8% of the time, Pallas kernels for 0%

profile of v1, /device:TPU:4, one launch (start us, length us, event | category | flops | bytes accessed | tf_op | source)
XLA Modules:
  0.0 168.1 jit_solution(4349809100620675301)
XLA Ops:
  0.6 0.7 compare_convert_fusion.1
  1.4 0.2 reduce-window_3_clone.1
  1.6 0.7 fusion.68
  2.3 0.3 multiply_reduce_fusion.2
  3.2 0.1 multiply_reduce_fusion.4
  3.3 0.7 reduce.1
  4.1 1.2 multiply_convert_fusion.5
  5.3 0.1 multiply_convert_fusion.6
  5.4 1.3 broadcast_in_dim.102
  6.7 9.2 %all-to-all-start.2 = ((bf16[16,16,3200]{2,1,0:T(8,128)(2,1)}), bf16[16,16,3200]{2,1,0:T(8,128)(2,1)S(1)}, u32[]{:S(2)}, u32[]{:S(2)}) async-start(bf16[16,16,3200]{2,1,0:T(8,128)(2,1)} %broadcast_in_dim.102), calls=%async_computation.2 | async-start | bytes 3276800 | tf_op jit(solution)/shard_map/all_to_all | solution.py:45
  15.9 40.9 %all-to-all-done.2 = bf16[16,16,3200]{2,1,0:T(8,128)(2,1)S(1)} async-done(((bf16[16,16,3200]{2,1,0:T(8,128)(2,1)}), bf16[16,16,3200]{2,1,0:T(8,128)(2,1)S(1)}, u32[]{:S(2)}, u32[]{:S(2)}) %all-to-all-start.2) | async-done | bytes 1638432 | tf_op jit(solution)/shard_map/all_to_all | solution.py:45
  56.8 3.3 %fusion.16 = f32[128,576]{0,1:T(8,128)S(1)} fusion(bf16[1,3200,576]{1,2,0:T(8,128)(2,1)} %param.21, bf16[16,16,3200]{2,1,0:T(8,128)(2,1)S(1)} %all-to-all-done.2), kind=kOutput, calls=%fused_computation.20 | convolution fusion | flops 471859200 | bytes 4800512 | tf_op jit(solution)/shard_map/dot_general | solution.py:73
  60.2 1.1 fusion.10
  61.3 1.1 multiply_reduce_fusion
  62.4 0.9 copy-done.2
  63.3 0.9 fusion.14
  64.3 0.9 fusion
  65.2 0.1 select_select_fusion
  65.3 1.0 maximum_bitcast_fusion
  66.3 3.8 %all-to-all-start.3 = ((bf16[16,8,3328]{2,1,0:T(8,128)(2,1)}), bf16[16,8,3328]{2,1,0:T(8,128)(2,1)S(1)}, u32[]{:S(2)}, u32[]{:S(2)}) async-start(bf16[16,8,3328]{2,1,0:T(8,128)(2,1)} %maximum_bitcast_fusion), calls=%async_computation.3 | async-start | bytes 1703936 | tf_op jit(solution)/shard_map/all_to_all | solution.py:45
  70.1 0.2 reduce-window_1_clone.1
  70.4 0.3 multiply_reduce_fusion.3
  70.7 23.3 %all-to-all-done.3 = bf16[16,8,3328]{2,1,0:T(8,128)(2,1)S(1)} async-done(((bf16[16,8,3328]{2,1,0:T(8,128)(2,1)}), bf16[16,8,3328]{2,1,0:T(8,128)(2,1)S(1)}, u32[]{:S(2)}, u32[]{:S(2)}) %all-to-all-start.3) | async-done | bytes 852000 | tf_op jit(solution)/shard_map/all_to_all | solution.py:45
  94.0 0.1 convert_reduce_fusion
  94.1 0.2 fusion.53
  94.3 0.1 subtract_multiply_fusion
  94.4 0.2 multiply_reduce_fusion.1
  94.7 0.1 subtract_convert_fusion
  94.8 0.9 broadcast_in_dim.66
  95.8 3.6 %all-to-all-start = ((bf16[16,8,3200]{2,1,0:T(8,128)(2,1)}), bf16[16,8,3200]{2,1,0:T(8,128)(2,1)S(1)}, u32[]{:S(2)}, u32[]{:S(2)}) async-start(bf16[16,8,3200]{2,1,0:T(8,128)(2,1)} %broadcast_in_dim.66), calls=%async_computation | async-start | bytes 1638400 | tf_op jit(solution)/shard_map/all_to_all | solution.py:45
  99.4 0.1 collective-permute-start
  99.5 5.3 %collective-permute-start.3 = (s32[1,64]{1,0:T(1,128)S(1)}, s32[1,64]{1,0:T(1,128)S(1)}, u32[]{:S(2)}, u32[]{:S(2)}) collective-permute-start(s32[1,64]{1,0:T(1,128)S(1)} %copy-done.8), channel_id=1, source_target_pairs={{0,240},{16,0},{32,16},{48,32},{64,48},{80,64},{96,80},{112,96},{1... | collective-permute-start | bytes 776 | tf_op jit(solution)/shard_map/ppermute | solution.py:15
  104.8 5.4 %collective-permute-start.5 = (bf16[64,3200]{1,0:T(8,128)(2,1)S(1)}, bf16[64,3200]{1,0:T(8,128)(2,1)S(1)}, u32[]{:S(2)}, u32[]{:S(2)}) collective-permute-start(bf16[64,3200]{1,0:T(8,128)(2,1)S(1)} %bitcast.111), channel_id=1, source_target_pairs={{0,240},{16,0},{32,16},{48,32},{64,48},{80,64},{96,80},{112,96},{1... | collective-permute-start | bytes 1228808 | tf_op jit(solution)/shard_map/ppermute | solution.py:15
  110.9 0.1 multiply_reduce_fusion.5
  111.0 0.2 reduce-window_clone.1
  111.2 11.3 %all-to-all-done = bf16[16,8,3200]{2,1,0:T(8,128)(2,1)S(1)} async-done(((bf16[16,8,3200]{2,1,0:T(8,128)(2,1)}), bf16[16,8,3200]{2,1,0:T(8,128)(2,1)S(1)}, u32[]{:S(2)}, u32[]{:S(2)}) %all-to-all-start) | async-done | bytes 819232 | tf_op jit(solution)/shard_map/all_to_all | solution.py:45
  122.5 3.2 %fusion.18 = f32[128,576]{0,1:T(8,128)S(1)} fusion(bf16[1,3200,576]{1,2,0:T(8,128)(2,1)} %param.21, bf16[16,8,3200]{2,1,0:T(8,128)(2,1)S(1)} %all-to-all-done), kind=kOutput, calls=%fused_computation.22 | convolution fusion | flops 471859200 | bytes 4800512 | tf_op jit(solution)/shard_map/dot_general | solution.py:73
  125.7 7.2 %fusion.1 = bf16[16,8,3200]{2,1,0:T(8,128)(2,1)} fusion(bf16[1,576,3200]{2,1,0:T(8,128)(2,1)} %param.23, bf16[1,3200,576]{1,2,0:T(8,128)(2,1)} %param.22, bf16[16,8,3200]{2,1,0:T(8,128)(2,1)S(1)} %all-to-all-done, f32[128,576]{0,1:T(8,128)S(1)} %fusion.18), kind=kOutput, calls=%fused_computation.3 | convolution fusion | flops 944570368 | bytes 9306112 | tf_op jit(solution)/shard_map/dot_general | solution.py:136
  132.9 3.6 %all-to-all-start.1 = ((bf16[16,8,3200]{2,1,0:T(8,128)(2,1)}), bf16[16,8,3200]{2,1,0:T(8,128)(2,1)S(1)}, u32[]{:S(2)}, u32[]{:S(2)}) async-start(bf16[16,8,3200]{2,1,0:T(8,128)(2,1)} %fusion.1), calls=%async_computation.1 | async-start | bytes 1638400 | tf_op jit(solution)/shard_map/all_to_all | solution.py:45
  136.5 0.2 reduce-window_2_clone.1
  136.9 2.0 %collective-permute-start.4 = (bf16[8,3200]{1,0:T(8,128)(2,1)S(1)}, bf16[8,3200]{1,0:T(8,128)(2,1)S(1)}, u32[]{:S(2)}, u32[]{:S(2)}) collective-permute-start(bf16[8,3200]{1,0:T(8,128)(2,1)S(1)} %get-tuple-element.2), channel_id=1, source_target_pairs={{0,240},{16,0},{32,16},{48,32},{64,48},{80,64},{96,80},{112,96},{1... | collective-permute-start | bytes 153608 | tf_op jit(solution)/shard_map/ppermute | solution.py:15
  138.9 0.1 fusion.30
  139.0 20.6 %all-to-all-done.1 = bf16[16,8,3200]{2,1,0:T(8,128)(2,1)S(1)} async-done(((bf16[16,8,3200]{2,1,0:T(8,128)(2,1)}), bf16[16,8,3200]{2,1,0:T(8,128)(2,1)S(1)}, u32[]{:S(2)}, u32[]{:S(2)}) %all-to-all-start.1) | async-done | bytes 819232 | tf_op jit(solution)/shard_map/all_to_all | solution.py:45
  159.6 0.1 reduce_sum.96
  159.8 0.1 collective-permute-start.1
  160.0 1.1 fusion.4
  161.0 6.0 %collective-permute-done.1 = bf16[8,3200]{1,0:T(8,128)(2,1)S(1)} collective-permute-done((bf16[8,3200]{1,0:T(8,128)(2,1)S(1)}, bf16[8,3200]{1,0:T(8,128)(2,1)S(1)}, u32[]{:S(2)}, u32[]{:S(2)}) %collective-permute-start.1) | collective-permute-done | bytes 51232 | tf_op jit(solution)/shard_map/ppermute | solution.py:15
  167.1 1.1 fusion.5
  (44 shorter events, 0.3 us)
Async XLA Ops:
  0.6 1.6 copy-start
  6.7 50.2 %all-to-all-start.2 = ((bf16[16,16,3200]{2,1,0:T(8,128)(2,1)}), bf16[16,16,3200]{2,1,0:T(8,128)(2,1)S(1)}, u32[]{:S(2)}, u32[]{:S(2)}) async-start(bf16[16,16,3200]{2,1,0:T(8,128)(2,1)} %broadcast_in_dim.102), calls=%async_computation.2 | async-start | bytes 3276800 | tf_op jit(solution)/shard_map/all_to_all | solution.py:45
  56.8 3.3 %copy-start.1 = (bf16[1,3200,576]{1,2,0:T(8,128)(2,1)S(1)}, bf16[1,3200,576]{1,2,0:T(8,128)(2,1)}, u32[]{:S(2)}) copy-start(bf16[1,3200,576]{1,2,0:T(8,128)(2,1)} %param.22) | copy-start | bytes 11059204
  56.8 4.5 %copy-start.3 = (bf16[1,576,3200]{2,1,0:T(8,128)(2,1)S(1)}, bf16[1,576,3200]{2,1,0:T(8,128)(2,1)}, u32[]{:S(2)}) copy-start(bf16[1,576,3200]{2,1,0:T(8,128)(2,1)} %param.23) | copy-start | bytes 11059204
  61.3 2.0 %copy-start.2 = (bf16[1,3200,576]{1,2,0:T(8,128)(2,1)S(1)}, bf16[1,3200,576]{1,2,0:T(8,128)(2,1)}, u32[]{:S(2)}) copy-start(bf16[1,3200,576]{1,2,0:T(8,128)(2,1)} %param.21) | copy-start | bytes 11059204
  64.3 5.8 %copy-start.6 = (bf16[1,3200]{1,0:T(2,128)(2,1)S(1)}, bf16[1,3200]{1,0:T(2,128)(2,1)}, u32[]{:S(2)}) copy-start(bf16[1,3200]{1,0:T(2,128)(2,1)} %param.20) | copy-start | bytes 19204
  64.3 5.8 %copy-start.7 = (s32[1,64]{1,0:T(1,128)S(1)}, s32[1,64]{1,0:T(1,128)}, u32[]{:S(2)}) copy-start(s32[1,64]{1,0:T(1,128)} %param.13) | copy-start | bytes 772
  64.3 6.1 %copy-start.5 = (bf16[1,64,3200]{2,1,0:T(8,128)(2,1)S(1)}, bf16[1,64,3200]{2,1,0:T(8,128)(2,1)}, u32[]{:S(2)}) copy-start(bf16[1,64,3200]{2,1,0:T(8,128)(2,1)} %param.12) | copy-start | bytes 1228804
  66.3 33.2 %copy-start.8 = (s32[1,64]{1,0:T(1,128)S(1)}, s32[1,64]{1,0:T(1,128)}, u32[]{:S(2)}) copy-start(s32[1,64]{1,0:T(1,128)} %param.17) | copy-start | bytes 772
  66.3 38.6 %copy-start.4 = (bf16[1,64,3200]{2,1,0:T(8,128)(2,1)S(1)}, bf16[1,64,3200]{2,1,0:T(8,128)(2,1)}, u32[]{:S(2)}) copy-start(bf16[1,64,3200]{2,1,0:T(8,128)(2,1)} %param.16) | copy-start | bytes 1228804
  66.3 27.7 %all-to-all-start.3 = ((bf16[16,8,3328]{2,1,0:T(8,128)(2,1)}), bf16[16,8,3328]{2,1,0:T(8,128)(2,1)S(1)}, u32[]{:S(2)}, u32[]{:S(2)}) async-start(bf16[16,8,3328]{2,1,0:T(8,128)(2,1)} %maximum_bitcast_fusion), calls=%async_computation.3 | async-start | bytes 1703936 | tf_op jit(solution)/shard_map/all_to_all | solution.py:45
  95.8 26.8 %all-to-all-start = ((bf16[16,8,3200]{2,1,0:T(8,128)(2,1)}), bf16[16,8,3200]{2,1,0:T(8,128)(2,1)S(1)}, u32[]{:S(2)}, u32[]{:S(2)}) async-start(bf16[16,8,3200]{2,1,0:T(8,128)(2,1)} %broadcast_in_dim.66), calls=%async_computation | async-start | bytes 1638400 | tf_op jit(solution)/shard_map/all_to_all | solution.py:45
  99.4 11.6 %collective-permute-start = (s32[1,64]{1,0:T(1,128)S(1)}, s32[1,64]{1,0:T(1,128)S(1)}, u32[]{:S(2)}, u32[]{:S(2)}) collective-permute-start(s32[1,64]{1,0:T(1,128)S(1)} %copy-done.7), channel_id=1, source_target_pairs={{0,16},{16,32},{32,48},{48,64},{64,80},{80,96},{96,112},{112,128},... | collective-permute-start | bytes 776 | tf_op jit(solution)/shard_map/ppermute | solution.py:15
  99.5 37.0 %collective-permute-start.3 = (s32[1,64]{1,0:T(1,128)S(1)}, s32[1,64]{1,0:T(1,128)S(1)}, u32[]{:S(2)}, u32[]{:S(2)}) collective-permute-start(s32[1,64]{1,0:T(1,128)S(1)} %copy-done.8), channel_id=1, source_target_pairs={{0,240},{16,0},{32,16},{48,32},{64,48},{80,64},{96,80},{112,96},{1... | collective-permute-start | bytes 776 | tf_op jit(solution)/shard_map/ppermute | solution.py:15
  104.8 56.2 %collective-permute-start.2 = (bf16[64,3200]{1,0:T(8,128)(2,1)S(1)}, bf16[64,3200]{1,0:T(8,128)(2,1)S(1)}, u32[]{:S(2)}, u32[]{:S(2)}) collective-permute-start(bf16[64,3200]{1,0:T(8,128)(2,1)S(1)} %bitcast.112), channel_id=1, source_target_pairs={{0,16},{16,32},{32,48},{48,64},{64,80},{80,96},{96,112},{112,128},... | collective-permute-start | bytes 1228808 | tf_op jit(solution)/shard_map/ppermute | solution.py:15
  104.8 55.1 %collective-permute-start.5 = (bf16[64,3200]{1,0:T(8,128)(2,1)S(1)}, bf16[64,3200]{1,0:T(8,128)(2,1)S(1)}, u32[]{:S(2)}, u32[]{:S(2)}) collective-permute-start(bf16[64,3200]{1,0:T(8,128)(2,1)S(1)} %bitcast.111), channel_id=1, source_target_pairs={{0,240},{16,0},{32,16},{48,32},{64,48},{80,64},{96,80},{112,96},{1... | collective-permute-start | bytes 1228808 | tf_op jit(solution)/shard_map/ppermute | solution.py:15
  132.9 26.7 %all-to-all-start.1 = ((bf16[16,8,3200]{2,1,0:T(8,128)(2,1)}), bf16[16,8,3200]{2,1,0:T(8,128)(2,1)S(1)}, u32[]{:S(2)}, u32[]{:S(2)}) async-start(bf16[16,8,3200]{2,1,0:T(8,128)(2,1)} %fusion.1), calls=%async_computation.1 | async-start | bytes 1638400 | tf_op jit(solution)/shard_map/all_to_all | solution.py:45
  136.9 23.1 %collective-permute-start.4 = (bf16[8,3200]{1,0:T(8,128)(2,1)S(1)}, bf16[8,3200]{1,0:T(8,128)(2,1)S(1)}, u32[]{:S(2)}, u32[]{:S(2)}) collective-permute-start(bf16[8,3200]{1,0:T(8,128)(2,1)S(1)} %get-tuple-element.2), channel_id=1, source_target_pairs={{0,240},{16,0},{32,16},{48,32},{64,48},{80,64},{96,80},{112,96},{1... | collective-permute-start | bytes 153608 | tf_op jit(solution)/shard_map/ppermute | solution.py:15
  159.8 7.2 %collective-permute-start.1 = (bf16[8,3200]{1,0:T(8,128)(2,1)S(1)}, bf16[8,3200]{1,0:T(8,128)(2,1)S(1)}, u32[]{:S(2)}, u32[]{:S(2)}) collective-permute-start(bf16[8,3200]{1,0:T(8,128)(2,1)S(1)} %add_convert_fusion), channel_id=1, source_target_pairs={{0,16},{16,32},{32,48},{48,64},{64,80},{80,96},{96,112},{112,128},... | collective-permute-start | bytes 153608 | tf_op jit(solution)/shard_map/ppermute | solution.py:15

commit v2 on v1

--- a/solution.py
+++ b/solution.py
@@ -41,8 +41,50 @@
     return (inv_scale, (values * inv_scale * norm_w).astype(jnp.bfloat16))
 
 
-def exchange(blocks):
-    return lax.all_to_all(blocks, "dp", 0, 0, tiled=False)
+def along_z(value, steps):
+    count = lax.axis_size("dp")
+    pairs = [(source, (source + 2 * steps) % count) for source in range(count)]
+    return lax.ppermute(value, "dp", pairs)
+
+
+def swap_x(value):
+    count = lax.axis_size("dp")
+    return lax.ppermute(value, "dp", [(source, source ^ 1) for source in range(count)])
+
+
+def gather_column(own):
+    half = own.shape[1] // 256 * 128
+    below2 = along_z(own, 2)
+    above2 = along_z(own, -2)
+    below1 = along_z(own, 1)
+    above1 = along_z(own, -1)
+    near = jnp.stack([own, below1, above1, below2, above2])
+    below3 = along_z(below2, 1)
+    above3 = along_z(above2, -1)
+    far_low = along_z(below2[:, :half], 2)
+    far_high = along_z(above2[:, half:], -2)
+    far = jnp.stack([below3, above3, jnp.concatenate([far_low, far_high], axis=1)])
+    return near, far
+
+
+def sum_column(parts):
+    own, above1, below1, above2, below2, above3, below3, far = [
+        parts[step] for step in (0, 2, 1, 4, 3, 6, 5, 7)
+    ]
+    half = own.shape[1] // 256 * 128
+    got_up = along_z(jnp.stack([above1, above3]).astype(jnp.bfloat16), 1)
+    got_down = along_z(jnp.stack([below1, below3]).astype(jnp.bfloat16), -1)
+    far = far.astype(jnp.bfloat16)
+    far_low = along_z(far[:, :half], 2).astype(jnp.float32)
+    far_high = along_z(far[:, half:], -2).astype(jnp.float32)
+    above2 = above2 + got_up[1].astype(jnp.float32)
+    below2 = below2 + got_down[1].astype(jnp.float32)
+    above2 = jnp.concatenate([above2[:, :half] + far_low, above2[:, half:]], axis=1)
+    below2 = jnp.concatenate([below2[:, :half], below2[:, half:] + far_high], axis=1)
+    two_up = along_z(above2.astype(jnp.bfloat16), 2)
+    two_down = along_z(below2.astype(jnp.bfloat16), -2)
+    near = own + got_up[0].astype(jnp.float32) + got_down[0].astype(jnp.float32)
+    return near + two_up.astype(jnp.float32) + two_down.astype(jnp.float32)
 
 
 def body(
@@ -85,9 +127,7 @@
         return placing, slot_mask, values, inv, normed, jax.nn.sigmoid(logit)
 
     next_tokens = shifted(fwd_in[0], "pipe", 1)
-    next_ids = shifted(fwd_ids, "pipe", 1)
     prev_grads = shifted(bwd_grad[0], "pipe", -1)
-    prev_ids = shifted(bwd_ids, "pipe", -1)
 
     b_place, b_mask, b_values, b_inv, b_normed, b_prob = slot_side(
         bwd_in[0], bwd_ids[0], bwd_lengths[0, 0]
@@ -98,13 +138,13 @@
         fwd_in[0], fwd_ids[0], fwd_lengths[0, 0]
     )
 
-    def gathered(rows):
-        return exchange(jnp.broadcast_to(rows[None], (n_dp,) + rows.shape))
-
-    bg_rows = gathered(jnp.concatenate([b_normed, g_send], axis=0))
-    b_rows = bg_rows[:, :capacity].reshape(n_dp * capacity, width)
-    g_rows = bg_rows[:, capacity:].reshape(n_dp * capacity, width)
-    f_rows = gathered(f_normed).reshape(n_dp * capacity, width)
+    near, far = gather_column(jnp.concatenate([b_normed, g_send, f_normed], axis=0))
+    rows = jnp.concatenate([near, far, swap_x(near), swap_x(far)], axis=0)
+    b_rows, g_rows, f_rows = [
+        rows[:, part * capacity : (part + 1) * capacity].reshape(n_dp * capacity, width)
+        for part in range(3)
+    ]
+    column = n_dp // 2
 
     gate_pre, up_pre, hidden = hidden_parts(b_rows)
     d_hidden = lax.dot_general(
@@ -128,14 +168,23 @@
     dot_cols = jnp.where(
         lanes == 0, dot_high[:, None], jnp.where(lanes == 1, dot_low[:, None], 0)
     ).astype(jnp.bfloat16)
-    d_send = jnp.concatenate([d_part.astype(jnp.bfloat16), dot_cols], axis=1)
-    d_got = exchange(d_send.reshape(n_dp, capacity, width + 128))
-    d_sum = jnp.sum(d_got.astype(jnp.float32), axis=0)
+    d_parts = jnp.concatenate([d_part.astype(jnp.bfloat16), dot_cols], axis=1)
+    d_parts = d_parts.reshape(2, column, capacity, width + 128)
+    d_parts = d_parts[0].astype(jnp.float32) + swap_x(d_parts[1]).astype(jnp.float32)
 
     f_hidden = hidden_parts(f_rows)[2]
-    f_part = jnp.dot(f_hidden, down_w, preferred_element_type=jnp.float32).astype(jnp.bfloat16)
-    f_got = exchange(f_part.reshape(n_dp, capacity, width))
-    f_back = jnp.sum(f_got.astype(jnp.float32), axis=0).astype(jnp.bfloat16)
+    f_parts = jnp.dot(f_hidden, down_w, preferred_element_type=jnp.float32).astype(jnp.bfloat16)
+    f_parts = f_parts.reshape(2, column, capacity, width)
+    f_parts = f_parts[0].astype(jnp.float32) + swap_x(f_parts[1]).astype(jnp.float32)
+
+    both = sum_column(jnp.concatenate([d_parts, f_parts], axis=2))
+    d_sum = both[:, : width + 128]
+    f_back = both[:, width + 128 :].astype(jnp.bfloat16)
+
+    def with_place(rows, placing):
+        return jnp.concatenate(
+            [rows, jnp.pad(placing, ((0, 0), (0, 128 - tok_count)))], axis=1
+        )
 
     d_rows = d_sum[:, :width].astype(jnp.bfloat16).astype(jnp.float32)
     row_dot = d_sum[:, width] + d_sum[:, width + 1]
@@ -146,17 +195,16 @@
     d_input = (g_values + b_inv * weighted - b_values * b_inv * b_inv * b_inv * inner).astype(
         jnp.bfloat16
     )
-    d_moved = shifted(d_input, "pipe", -1)
+    d_moved = shifted(with_place(d_input, b_place), "pipe", -1)
     layer_rows = (f_values + (f_mask * f_prob)[:, None] * f_back.astype(jnp.float32)).astype(
         jnp.bfloat16
     )
-    f_moved = shifted(layer_rows, "pipe", 1)
-
-    next_place = placement_matrix(slot_of(next_ids[0], capacity), capacity)
-    prev_place = placement_matrix(slot_of(prev_ids[0], capacity), capacity)
-    bwd_out = overlay(prev_place, d_moved, prev_grads)
-    fwd_out = overlay(next_place, f_moved, next_tokens)
-    return (fwd_out[None], bwd_out[None])
+    f_moved = shifted(with_place(layer_rows, f_place), "pipe", 1)
+
+    def finished(moved, tokens):
+        return overlay(moved[:, width : width + tok_count], moved[:, :width], tokens)
+
+    return (finished(f_moved, next_tokens)[None], finished(d_moved, prev_grads)[None])
 
 
 def solution(mesh):

time: 169 us -> 131 us (0.78)
  waiting for transfers between devices: 102 us -> 51.5 us
  starting transfers between devices: 33.1 us -> 39.4 us
  matrix products: 21.8 us -> 25.5 us
  other arithmetic: 5.53 us -> 7.72 us
    all_to_all x4 -> x0, waiting for transfers between devices: 96.2 us -> none  [exchange(): return lax.all_to_all(blocks, 'dp', 0, 0, tiled=False)]
    ppermute x0 -> x18, waiting for transfers between devices: none -> 44.3 us  [the longest x4 26.1 us: swap_x(): lax.ppermute(value, 'dp', [(source, source ^ 1) for source in range(count)])]
    ppermute x0 -> x18, starting transfers between devices: none -> 36.3 us  [the longest x14 31.1 us: along_z(): return lax.ppermute(value, 'dp', pairs)]
    all_to_all x4 -> x0, starting transfers between devices: 20.2 us -> none  [exchange(): return lax.all_to_all(blocks, 'dp', 0, 0, tiled=False)]
    ppermute x6 -> x4, starting transfers between devices: 12.9 us -> 3.06 us  [shifted(): return lax.ppermute(value, axis, pairs)]
    dot_general x2, matrix products: 6.45 us -> 2.97 us  [hidden_parts(): gate_pre = jnp.dot(slot_rows, gate_w, preferred_element_type=jnp.float32)]
    broadcast_in_dim x2 -> x0, local copies, waits for them, and re-layouts: 2.25 us -> none  [gathered(): return exchange(jnp.broadcast_to(rows[None], (n_dp,) + rows.shape))]
    dot_general x1, matrix products: 1.14 us -> 3.21 us  [body(): lax.dot_general(g_rows, down_w, (((1,), (1,)), ((), ())), preferred_eleme...]
  transfers between devices with their start and end apart: 10 -> 22, of which waited for: 5 -> 13; matrix products, arithmetic and copies ran while one was open for 8% -> 20% of each run, Pallas kernels for 0% -> 0%
where the time goes in v2:
time: 131 us; the launch traced here: 130 us
  waiting for transfers between devices  51.5 us (39%)
  starting transfers between devices  39.4 us (30%)
  matrix products  25.5 us (19%)
  other arithmetic  7.72 us (6%)
  local copies, waits for them, and re-layouts  3.5 us (3%)
  between operations  2.43 us (2%)
    ppermute x14, starting transfers between devices, along_z(): return lax.ppermute(value, 'dp', pairs)  31.1 us
    ppermute x4, waiting for transfers between devices, swap_x(): lax.ppermute(value, 'dp', [(source, source ^ 1) for source in range(count)])  26.1 us
    ppermute x14, waiting for transfers between devices, along_z(): return lax.ppermute(value, 'dp', pairs)  18.3 us
    dot_general x1, matrix products, body(): jnp.dot(f_hidden, down_w, preferred_element_type=jnp.float32)  7.3 us
    ppermute x4, waiting for transfers between devices, shifted(): return lax.ppermute(value, axis, pairs)  7.14 us
    ppermute x4, starting transfers between devices, swap_x(): lax.ppermute(value, 'dp', [(source, source ^ 1) for source in range(count)])  5.21 us
    dot_general x2, matrix products, overlay(): lax.dot_general(placing, rows, (((0,), (0,)), ((), ())), preferred_elemen...  4.14 us
    dot_general x1, matrix products, body(): lax.dot_general(g_rows, down_w, (((1,), (1,)), ((), ())), preferred_eleme...  3.21 us
  transfers between devices with their start and end apart: 22, of which 13 were waited for; matrix products, arithmetic and copies ran while one was open for 20% of the time, Pallas kernels for 0%

profile of v2, /device:TPU:4, one launch (start us, length us, event | category | flops | bytes accessed | tf_op | source)
XLA Modules:
  0.0 130.0 jit_solution(11813683154309705400)
XLA Ops:
  0.7 0.7 compare_convert_fusion.1
  2.3 0.7 compare_convert_fusion.3
  4.9 1.3 multiply_reduce_fusion.3
  6.2 0.7 reduce
  7.0 1.2 multiply_convert_fusion.7
  8.3 2.0 %collective-permute-start = (bf16[24,3200]{1,0:T(8,128)(2,1)S(1)}, bf16[24,3200]{1,0:T(8,128)(2,1)S(1)}, u32[]{:S(2)}, u32[]{:S(2)}) collective-permute-start(bf16[24,3200]{1,0:T(8,128)(2,1)S(1)} %pad_maximum_fusion.5), channel_id=1, source_target_pairs={{0,2},{1,3},{2,4},{3,5},{4,6},{5,7},{6,8},{7,9},{8,10},{9,11},{10,... | collective-permute-start | bytes 460808 | tf_op jit(solution)/shard_map/ppermute | solution.py:47
  10.3 4.0 %collective-permute-start.1 = (bf16[24,3200]{1,0:T(8,128)(2,1)S(1)}, bf16[24,3200]{1,0:T(8,128)(2,1)S(1)}, u32[]{:S(2)}, u32[]{:S(2)}) collective-permute-start(bf16[24,3200]{1,0:T(8,128)(2,1)S(1)} %pad_maximum_fusion.5), channel_id=1, source_target_pairs={{0,14},{1,15},{2,0},{3,1},{4,2},{5,3},{6,4},{7,5},{8,6},{9,7},{10,... | collective-permute-start | bytes 460808 | tf_op jit(solution)/shard_map/ppermute | solution.py:47
  14.3 4.1 %collective-permute-start.3 = (bf16[24,3200]{1,0:T(8,128)(2,1)S(1)}, bf16[24,3200]{1,0:T(8,128)(2,1)S(1)}, u32[]{:S(2)}, u32[]{:S(2)}) collective-permute-start(bf16[24,3200]{1,0:T(8,128)(2,1)S(1)} %pad_maximum_fusion.5), channel_id=1, source_target_pairs={{0,12},{1,13},{2,14},{3,15},{4,0},{5,1},{6,2},{7,3},{8,4},{9,5},{1... | collective-permute-start | bytes 460808 | tf_op jit(solution)/shard_map/ppermute | solution.py:47
  18.4 1.6 %collective-permute-start.21 = (bf16[64,3200]{1,0:T(8,128)(2,1)}, bf16[64,3200]{1,0:T(8,128)(2,1)}, u32[]{:S(2)}, u32[]{:S(2)}) collective-permute-start(bf16[64,3200]{1,0:T(8,128)(2,1)} %bitcast.152), channel_id=1, source_target_pairs={{0,240},{16,0},{32,16},{48,32},{64,48},{80,64},{96,80},{112,96},{1... | collective-permute-start | bytes 1228808 | tf_op jit(solution)/shard_map/ppermute | solution.py:15
  20.8 0.8 fusion.20
  22.1 3.5 %collective-permute-done.3 = bf16[24,3200]{1,0:T(8,128)(2,1)S(1)} collective-permute-done((bf16[24,3200]{1,0:T(8,128)(2,1)S(1)}, bf16[24,3200]{1,0:T(8,128)(2,1)S(1)}, u32[]{:S(2)}, u32[]{:S(2)}) %collective-permute-start.3) | collective-permute-done | bytes 153632 | tf_op jit(solution)/shard_map/ppermute | solution.py:47
  25.7 3.2 %collective-permute-start.7 = (bf16[24,1664]{1,0:T(8,128)(2,1)S(1)}, bf16[24,1664]{1,0:T(8,128)(2,1)S(1)}, u32[]{:S(2)}, u32[]{:S(2)}) collective-permute-start(bf16[24,1664]{1,0:T(8,128)(2,1)S(1)} %slice.158), channel_id=1, source_target_pairs={{0,12},{1,13},{2,14},{3,15},{4,0},{5,1},{6,2},{7,3},{8,4},{9,5},{1... | collective-permute-start | bytes 239624 | tf_op jit(solution)/shard_map/ppermute | solution.py:47
  28.8 0.7 collective-permute-start.6
  29.7 1.3 collective-permute-start.8
  31.0 4.8 %collective-permute-done.6 = bf16[24,1536]{1,0:T(8,128)(2,1)S(1)} collective-permute-done((bf16[24,1536]{1,0:T(8,128)(2,1)S(1)}, bf16[24,1536]{1,0:T(8,128)(2,1)S(1)}, u32[]{:S(2)}, u32[]{:S(2)}) %collective-permute-start.6) | collective-permute-done | bytes 73760 | tf_op jit(solution)/shard_map/ppermute | solution.py:47
  35.8 3.2 %collective-permute-start.5 = (bf16[24,3200]{1,0:T(8,128)(2,1)S(1)}, bf16[24,3200]{1,0:T(8,128)(2,1)S(1)}, u32[]{:S(2)}, u32[]{:S(2)}) collective-permute-start(bf16[24,3200]{1,0:T(8,128)(2,1)S(1)} %collective-permute-done.3), channel_id=1, source_target_pairs={{0,14},{1,15},{2,0},{3,1},{4,2},{5,3},{6,4},{7,5},{8,6},{9,7},{10,... | collective-permute-start | bytes 460808 | tf_op jit(solution)/shard_map/ppermute | solution.py:47
  39.1 4.4 %collective-permute-done.4 = bf16[24,3200]{1,0:T(8,128)(2,1)S(1)} collective-permute-done((bf16[24,3200]{1,0:T(8,128)(2,1)S(1)}, bf16[24,3200]{1,0:T(8,128)(2,1)S(1)}, u32[]{:S(2)}, u32[]{:S(2)}) %collective-permute-start.4) | collective-permute-done | bytes 153632 | tf_op jit(solution)/shard_map/ppermute | solution.py:47
  43.5 1.5 %collective-permute-start.9 = (bf16[3,24,3200]{2,1,0:T(8,128)(2,1)S(1)}, bf16[3,24,3200]{2,1,0:T(8,128)(2,1)S(1)}, u32[]{:S(2)}, u32[]{:S(2)}) collective-permute-start(bf16[3,24,3200]{2,1,0:T(8,128)(2,1)S(1)} %pad_maximum_fusion.1), channel_id=1, source_target_pairs={{0,1},{1,0},{2,3},{3,2},{4,5},{5,4},{6,7},{7,6},{8,9},{9,8},{10,11... | collective-permute-start | bytes 1382408 | tf_op jit(solution)/shard_map/ppermute | solution.py:52
  45.1 4.4 %collective-permute-done.8 = bf16[5,24,3200]{2,1,0:T(8,128)(2,1)S(1)} collective-permute-done((bf16[5,24,3200]{2,1,0:T(8,128)(2,1)S(1)}, bf16[5,24,3200]{2,1,0:T(8,128)(2,1)S(1)}, u32[]{:S(2)}, u32[]{:S(2)}) %collective-permute-start.8) | collective-permute-done | bytes 768032 | tf_op jit(solution)/shard_map/ppermute | solution.py:52
  49.6 9.8 %collective-permute-done.9 = bf16[3,24,3200]{2,1,0:T(8,128)(2,1)S(1)} collective-permute-done((bf16[3,24,3200]{2,1,0:T(8,128)(2,1)S(1)}, bf16[3,24,3200]{2,1,0:T(8,128)(2,1)S(1)}, u32[]{:S(2)}, u32[]{:S(2)}) %collective-permute-start.9) | collective-permute-done | bytes 460832 | tf_op jit(solution)/shard_map/ppermute | solution.py:52
  59.4 1.8 %fusion.1 = f32[128,576]{0,1:T(8,128)} fusion(bf16[1,3200,576]{1,2,0:T(8,128)(2,1)S(1)} %copy-done.1, bf16[16,24,3200]{2,1,0:T(8,128)(2,1)S(1)} %constant_dynamic-update-slice_fusion), kind=kOutput, calls=%fused_computation.5 | convolution fusion | flops 471859200 | bytes 4800512 | tf_op jit(solution)/shard_map/dot_general | solution.py:115
  61.3 1.1 fusion.5
  62.4 0.9 copy-done.3
  63.3 1.8 %fusion.10 = f32[128,576]{0,1:T(8,128)} fusion(bf16[1,3200,576]{1,2,0:T(8,128)(2,1)S(1)} %copy-done.3, bf16[16,24,3200]{2,1,0:T(8,128)(2,1)S(1)} %constant_dynamic-update-slice_fusion), kind=kOutput, calls=%fused_computation.14 | convolution fusion | flops 471859200 | bytes 4800512 | tf_op jit(solution)/shard_map/dot_general | solution.py:116
  65.1 7.3 %convolution_convert_fusion = bf16[128,3200]{1,0:T(8,128)(2,1)} fusion(bf16[1,576,3200]{2,1,0:T(8,128)(2,1)} %param.23, f32[128,576]{0,1:T(8,128)} %fusion.1, bf16[1,3200,576]{1,2,0:T(8,128)(2,1)} %param.22, bf16[16,24,3200]{2,1,0:T(8,128)(2,1)S(1)} %constant_dynamic-update-slice_fusion), kind=kOutput, calls=%fused_computation.2 | convolution fusion | flops 944570368 | bytes 9306112 | tf_op jit(solution)/shard_map/dot_general | solution.py:176
  72.4 1.0 slice_bitcast_fusion.8
  73.5 1.3 collective-permute-start.11
  74.8 3.2 %multiply_reduce_fusion = (f32[128]{0:T(128)S(1)}, f32[128,576]{0,1:T(8,128)S(1)}) fusion(f32[128,576]{0,1:T(8,128)} %fusion.10, f32[128,576]{0,1:T(8,128)S(1)} %fusion.5, bf16[1,576,3200]{2,1,0:T(8,128)(2,1)} %param.23, bf16[16,24,3200]{2,1,0:T(8,128)(2,1)S(1)} %constant_dynamic-update-slice_fusion), kind=kOutput, calls=%fused_computation.57 | convolution fusion | flops 472522624 | bytes 5390848 | tf_op jit(solution)/shard_map/dot_general | solution.py:150
  78.0 0.9 fusion.3
  79.0 1.1 copy-done.4
  80.1 0.9 fusion
  81.1 1.2 collective-permute-start.10
  82.3 3.6 %collective-permute-done.11 = bf16[8,8,3200]{2,1,0:T(8,128)(2,1)S(1)} collective-permute-done((bf16[8,8,3200]{2,1,0:T(8,128)(2,1)S(1)}, bf16[8,8,3200]{2,1,0:T(8,128)(2,1)S(1)}, u32[]{:S(2)}, u32[]{:S(2)}) %collective-permute-start.11) | collective-permute-done | bytes 409632 | tf_op jit(solution)/shard_map/ppermute | solution.py:52
  86.0 8.3 %collective-permute-done.10 = bf16[8,8,3328]{2,1,0:T(8,128)(2,1)S(1)} collective-permute-done((bf16[8,8,3328]{2,1,0:T(8,128)(2,1)S(1)}, bf16[8,8,3328]{2,1,0:T(8,128)(2,1)S(1)}, u32[]{:S(2)}, u32[]{:S(2)}) %collective-permute-start.10) | collective-permute-done | bytes 426016 | tf_op jit(solution)/shard_map/ppermute | solution.py:52
  94.7 2.1 %collective-permute-start.12 = (bf16[2,8,6528]{2,1,0:T(8,128)(2,1)S(1)}, bf16[2,8,6528]{2,1,0:T(8,128)(2,1)S(1)}, u32[]{:S(2)}, u32[]{:S(2)}) collective-permute-start(bf16[2,8,6528]{2,1,0:T(8,128)(2,1)S(1)} %pad_maximum_fusion.3), channel_id=1, source_target_pairs={{0,2},{1,3},{2,4},{3,5},{4,6},{5,7},{6,8},{7,9},{8,10},{9,11},{10,... | collective-permute-start | bytes 626696 | tf_op jit(solution)/shard_map/ppermute | solution.py:47
  97.4 4.3 %collective-permute-start.14 = (bf16[8,3200]{1,0:T(8,128)(2,1)S(1)}, bf16[8,3200]{1,0:T(8,128)(2,1)S(1)}, u32[]{:S(2)}, u32[]{:S(2)}) collective-permute-start(bf16[8,3200]{1,0:T(8,128)(2,1)S(1)} %slice.179), channel_id=1, source_target_pairs={{0,4},{1,5},{2,6},{3,7},{4,8},{5,9},{6,10},{7,11},{8,12},{9,13},{1... | collective-permute-start | bytes 153608 | tf_op jit(solution)/shard_map/ppermute | solution.py:47
  101.7 2.9 %collective-permute-start.16 = (bf16[8,3328]{1,0:T(8,128)(2,1)S(1)}, bf16[8,3328]{1,0:T(8,128)(2,1)S(1)}, u32[]{:S(2)}, u32[]{:S(2)}) collective-permute-start(bf16[8,3328]{1,0:T(8,128)(2,1)S(1)} %slice.186), channel_id=1, source_target_pairs={{0,12},{1,13},{2,14},{3,15},{4,0},{5,1},{6,2},{7,3},{8,4},{9,5},{1... | collective-permute-start | bytes 159752 | tf_op jit(solution)/shard_map/ppermute | solution.py:47
  104.7 1.9 %collective-permute-done.14 = bf16[8,3200]{1,0:T(8,128)(2,1)S(1)} collective-permute-done((bf16[8,3200]{1,0:T(8,128)(2,1)S(1)}, bf16[8,3200]{1,0:T(8,128)(2,1)S(1)}, u32[]{:S(2)}, u32[]{:S(2)}) %collective-permute-start.14) | collective-permute-done | bytes 51232 | tf_op jit(solution)/shard_map/ppermute | solution.py:47
  107.4 3.9 %collective-permute-start.17 = (bf16[8,6528]{1,0:T(8,128)(2,1)S(1)}, bf16[8,6528]{1,0:T(8,128)(2,1)S(1)}, u32[]{:S(2)}, u32[]{:S(2)}) collective-permute-start(bf16[8,6528]{1,0:T(8,128)(2,1)S(1)} %pad_maximum_fusion.7), channel_id=1, source_target_pairs={{0,12},{1,13},{2,14},{3,15},{4,0},{5,1},{6,2},{7,3},{8,4},{9,5},{1... | collective-permute-start | bytes 313352 | tf_op jit(solution)/shard_map/ppermute | solution.py:47
  111.3 2.2 %collective-permute-done.15 = bf16[8,6528]{1,0:T(8,128)(2,1)S(1)} collective-permute-done((bf16[8,6528]{1,0:T(8,128)(2,1)S(1)}, bf16[8,6528]{1,0:T(8,128)(2,1)S(1)}, u32[]{:S(2)}, u32[]{:S(2)}) %collective-permute-start.15) | collective-permute-done | bytes 104480 | tf_op jit(solution)/shard_map/ppermute | solution.py:47
  113.5 1.2 collective-permute-done.17
  114.8 1.0 fusion.80
  115.9 0.8 subtract_multiply_fusion
  117.2 1.5 %collective-permute-start.20 = (bf16[8,3328]{1,0:T(8,128)(2,1)S(1)}, bf16[8,3328]{1,0:T(8,128)(2,1)S(1)}, u32[]{:S(2)}, u32[]{:S(2)}) collective-permute-start(bf16[8,3328]{1,0:T(8,128)(2,1)S(1)} %fusion.54), channel_id=1, source_target_pairs={{0,240},{16,0},{32,16},{48,32},{64,48},{80,64},{96,80},{112,96},{1... | collective-permute-start | bytes 159752 | tf_op jit(solution)/shard_map/ppermute | solution.py:15
  118.7 1.8 %collective-permute-done.20 = bf16[8,3328]{1,0:T(8,128)(2,1)S(1)} collective-permute-done((bf16[8,3328]{1,0:T(8,128)(2,1)S(1)}, bf16[8,3328]{1,0:T(8,128)(2,1)S(1)}, u32[]{:S(2)}, u32[]{:S(2)}) %collective-permute-start.20) | collective-permute-done | bytes 53280 | tf_op jit(solution)/shard_map/ppermute | solution.py:15
  120.5 5.4 %collective-permute-done.18 = bf16[8,3328]{1,0:T(8,128)(2,1)S(1)} collective-permute-done((bf16[8,3328]{1,0:T(8,128)(2,1)S(1)}, bf16[8,3328]{1,0:T(8,128)(2,1)S(1)}, u32[]{:S(2)}, u32[]{:S(2)}) %collective-permute-start.18) | collective-permute-done | bytes 53280 | tf_op jit(solution)/shard_map/ppermute | solution.py:15
  125.9 2.1 %select_bitcast_fusion = bf16[1,64,3200]{2,1,0:T(8,128)(2,1)} fusion(bf16[64,3200]{1,0:T(8,128)(2,1)} %collective-permute-done.21, pred[64]{0:T(512)(128)(4,1)S(1)} %broadcast_compare_fusion, bf16[8,3328]{1,0:T(8,128)(2,1)S(1)} %collective-permute-done.20), kind=kOutput, calls=%fused_computation.54 | convolution fusion | flops 3686400 | bytes 872512 | tf_op jit(solution)/shard_map/dot_general | solution.py:32
  128.0 2.1 %select_bitcast_fusion.1 = bf16[1,64,3200]{2,1,0:T(8,128)(2,1)} fusion(bf16[64,3200]{1,0:T(8,128)(2,1)} %collective-permute-done.19, pred[64]{0:T(512)(128)(4,1)S(1)} %broadcast_compare_fusion.1, bf16[8,3328]{1,0:T(8,128)(2,1)S(1)} %collective-permute-done.18), kind=kOutput, calls=%fused_computation.55 | convolution fusion | flops 3686400 | bytes 872512 | tf_op jit(solution)/shard_map/dot_general | solution.py:32
  (113 shorter events, 6.1 us)
Async XLA Ops:
  0.6 3.9 %copy-start = (bf16[1,64,3200]{2,1,0:T(8,128)(2,1)S(1)}, bf16[1,64,3200]{2,1,0:T(8,128)(2,1)}, u32[]{:S(2)}) copy-start(bf16[1,64,3200]{2,1,0:T(8,128)(2,1)} %param.15) | copy-start | bytes 1228804
  0.6 20.2 %copy-start.8 = (bf16[1,3200]{1,0:T(2,128)(2,1)S(1)}, bf16[1,3200]{1,0:T(2,128)(2,1)}, u32[]{:S(2)}) copy-start(bf16[1,3200]{1,0:T(2,128)(2,1)} %param.20) | copy-start | bytes 19204
  2.3 5.9 %copy-start.12 = (s32[64]{0:T(128)}, s32[64]{0:T(128)S(1)}, u32[]{:S(2)}) copy-start(s32[64]{0:T(128)S(1)} %fusion.74) | copy-start | bytes 772
  3.8 25.9 %copy-start.14 = (s32[64]{0:T(128)}, s32[64]{0:T(128)S(1)}, u32[]{:S(2)}) copy-start(s32[64]{0:T(128)S(1)} %fusion.73) | copy-start | bytes 772
  4.9 3.2 %copy-start.19 = (f32[8]{0:T(128)}, f32[8]{0:T(128)S(1)}, u32[]{:S(2)}) copy-start(f32[8]{0:T(128)S(1)} %multiply_reduce_fusion.4) | copy-start | bytes 100
  6.2 24.8 %copy-start.10 = (f32[8]{0:T(128)}, f32[8]{0:T(128)S(1)}, u32[]{:S(2)}) copy-start(f32[8]{0:T(128)S(1)} %get-tuple-element.37) | copy-start | bytes 100
  8.3 20.5 %collective-permute-start = (bf16[24,3200]{1,0:T(8,128)(2,1)S(1)}, bf16[24,3200]{1,0:T(8,128)(2,1)S(1)}, u32[]{:S(2)}, u32[]{:S(2)}) collective-permute-start(bf16[24,3200]{1,0:T(8,128)(2,1)S(1)} %pad_maximum_fusion.5), channel_id=1, source_target_pairs={{0,2},{1,3},{2,4},{3,5},{4,6},{5,7},{6,8},{7,9},{8,10},{9,11},{10,... | collective-permute-start | bytes 460808 | tf_op jit(solution)/shard_map/ppermute | solution.py:47
  10.3 19.3 %collective-permute-start.1 = (bf16[24,3200]{1,0:T(8,128)(2,1)S(1)}, bf16[24,3200]{1,0:T(8,128)(2,1)S(1)}, u32[]{:S(2)}, u32[]{:S(2)}) collective-permute-start(bf16[24,3200]{1,0:T(8,128)(2,1)S(1)} %pad_maximum_fusion.5), channel_id=1, source_target_pairs={{0,14},{1,15},{2,0},{3,1},{4,2},{5,3},{6,4},{7,5},{8,6},{9,7},{10,... | collective-permute-start | bytes 460808 | tf_op jit(solution)/shard_map/ppermute | solution.py:47
  14.3 11.3 %collective-permute-start.2 = (bf16[24,3200]{1,0:T(8,128)(2,1)S(1)}, bf16[24,3200]{1,0:T(8,128)(2,1)S(1)}, u32[]{:S(2)}, u32[]{:S(2)}) collective-permute-start(bf16[24,3200]{1,0:T(8,128)(2,1)S(1)} %pad_maximum_fusion.5), channel_id=1, source_target_pairs={{0,4},{1,5},{2,6},{3,7},{4,8},{5,9},{6,10},{7,11},{8,12},{9,13},{1... | collective-permute-start | bytes 460808 | tf_op jit(solution)/shard_map/ppermute | solution.py:47
  14.3 11.3 %collective-permute-start.3 = (bf16[24,3200]{1,0:T(8,128)(2,1)S(1)}, bf16[24,3200]{1,0:T(8,128)(2,1)S(1)}, u32[]{:S(2)}, u32[]{:S(2)}) collective-permute-start(bf16[24,3200]{1,0:T(8,128)(2,1)S(1)} %pad_maximum_fusion.5), channel_id=1, source_target_pairs={{0,12},{1,13},{2,14},{3,15},{4,0},{5,1},{6,2},{7,3},{8,4},{9,5},{1... | collective-permute-start | bytes 460808 | tf_op jit(solution)/shard_map/ppermute | solution.py:47
  18.4 107.5 %collective-permute-start.21 = (bf16[64,3200]{1,0:T(8,128)(2,1)}, bf16[64,3200]{1,0:T(8,128)(2,1)}, u32[]{:S(2)}, u32[]{:S(2)}) collective-permute-start(bf16[64,3200]{1,0:T(8,128)(2,1)} %bitcast.152), channel_id=1, source_target_pairs={{0,240},{16,0},{32,16},{48,32},{64,48},{80,64},{96,80},{112,96},{1... | collective-permute-start | bytes 1228808 | tf_op jit(solution)/shard_map/ppermute | solution.py:15
  25.6 102.3 %collective-permute-start.19 = (bf16[64,3200]{1,0:T(8,128)(2,1)}, bf16[64,3200]{1,0:T(8,128)(2,1)}, u32[]{:S(2)}, u32[]{:S(2)}) collective-permute-start(bf16[64,3200]{1,0:T(8,128)(2,1)} %bitcast.153), channel_id=1, source_target_pairs={{0,16},{16,32},{32,48},{48,64},{64,80},{80,96},{96,112},{112,128},... | collective-permute-start | bytes 1228808 | tf_op jit(solution)/shard_map/ppermute | solution.py:15
  25.7 10.2 %collective-permute-start.7 = (bf16[24,1664]{1,0:T(8,128)(2,1)S(1)}, bf16[24,1664]{1,0:T(8,128)(2,1)S(1)}, u32[]{:S(2)}, u32[]{:S(2)}) collective-permute-start(bf16[24,1664]{1,0:T(8,128)(2,1)S(1)} %slice.158), channel_id=1, source_target_pairs={{0,12},{1,13},{2,14},{3,15},{4,0},{5,1},{6,2},{7,3},{8,4},{9,5},{1... | collective-permute-start | bytes 239624 | tf_op jit(solution)/shard_map/ppermute | solution.py:47
  28.8 7.0 %collective-permute-start.6 = (bf16[24,1536]{1,0:T(8,128)(2,1)S(1)}, bf16[24,1536]{1,0:T(8,128)(2,1)S(1)}, u32[]{:S(2)}, u32[]{:S(2)}) collective-permute-start(bf16[24,1536]{1,0:T(8,128)(2,1)S(1)} %slice.157), channel_id=1, source_target_pairs={{0,4},{1,5},{2,6},{3,7},{4,8},{5,9},{6,10},{7,11},{8,12},{9,13},{1... | collective-permute-start | bytes 221192 | tf_op jit(solution)/shard_map/ppermute | solution.py:47
  29.7 29.7 %copy-start.1 = (bf16[1,3200,576]{1,2,0:T(8,128)(2,1)S(1)}, bf16[1,3200,576]{1,2,0:T(8,128)(2,1)}, u32[]{:S(2)}) copy-start(bf16[1,3200,576]{1,2,0:T(8,128)(2,1)} %param.21) | copy-start | bytes 11059204
  29.7 19.8 %collective-permute-start.8 = (bf16[5,24,3200]{2,1,0:T(8,128)(2,1)S(1)}, bf16[5,24,3200]{2,1,0:T(8,128)(2,1)S(1)}, u32[]{:S(2)}, u32[]{:S(2)}) collective-permute-start(bf16[5,24,3200]{2,1,0:T(8,128)(2,1)S(1)} %get-tuple-element.11), channel_id=1, source_target_pairs={{0,1},{1,0},{2,3},{3,2},{4,5},{5,4},{6,7},{7,6},{8,9},{9,8},{10,11... | collective-permute-start | bytes 2304008 | tf_op jit(solution)/shard_map/ppermute | solution.py:52
  35.8 7.7 %collective-permute-start.4 = (bf16[24,3200]{1,0:T(8,128)(2,1)S(1)}, bf16[24,3200]{1,0:T(8,128)(2,1)S(1)}, u32[]{:S(2)}, u32[]{:S(2)}) collective-permute-start(bf16[24,3200]{1,0:T(8,128)(2,1)S(1)} %collective-permute-done.2), channel_id=1, source_target_pairs={{0,2},{1,3},{2,4},{3,5},{4,6},{5,7},{6,8},{7,9},{8,10},{9,11},{10,... | collective-permute-start | bytes 460808 | tf_op jit(solution)/shard_map/ppermute | solution.py:47
  35.8 7.7 %collective-permute-start.5 = (bf16[24,3200]{1,0:T(8,128)(2,1)S(1)}, bf16[24,3200]{1,0:T(8,128)(2,1)S(1)}, u32[]{:S(2)}, u32[]{:S(2)}) collective-permute-start(bf16[24,3200]{1,0:T(8,128)(2,1)S(1)} %collective-permute-done.3), channel_id=1, source_target_pairs={{0,14},{1,15},{2,0},{3,1},{4,2},{5,3},{6,4},{7,5},{8,6},{9,7},{10,... | collective-permute-start | bytes 460808 | tf_op jit(solution)/shard_map/ppermute | solution.py:47
  43.5 15.8 %collective-permute-start.9 = (bf16[3,24,3200]{2,1,0:T(8,128)(2,1)S(1)}, bf16[3,24,3200]{2,1,0:T(8,128)(2,1)S(1)}, u32[]{:S(2)}, u32[]{:S(2)}) collective-permute-start(bf16[3,24,3200]{2,1,0:T(8,128)(2,1)S(1)} %pad_maximum_fusion.1), channel_id=1, source_target_pairs={{0,1},{1,0},{2,3},{3,2},{4,5},{5,4},{6,7},{7,6},{8,9},{9,8},{10,11... | collective-permute-start | bytes 1382408 | tf_op jit(solution)/shard_map/ppermute | solution.py:52
  61.3 2.0 %copy-start.3 = (bf16[1,3200,576]{1,2,0:T(8,128)(2,1)S(1)}, bf16[1,3200,576]{1,2,0:T(8,128)(2,1)}, u32[]{:S(2)}) copy-start(bf16[1,3200,576]{1,2,0:T(8,128)(2,1)} %param.22) | copy-start | bytes 11059204
  73.5 4.5 %copy-start.2 = (bf16[1,3200,576]{1,2,0:T(8,128)(2,1)S(1)}, bf16[1,3200,576]{1,2,0:T(8,128)(2,1)}, u32[]{:S(2)}) copy-start(bf16[1,3200,576]{1,2,0:T(8,128)(2,1)} %param.21) | copy-start | bytes 11059204
  73.5 4.5 %copy-start.6 = (f32[128,576]{0,1:T(8,128)S(1)}, f32[128,576]{0,1:T(8,128)}, u32[]{:S(2)}) copy-start(f32[128,576]{0,1:T(8,128)} %fusion.10) | copy-start | bytes 884740
  73.5 12.4 %collective-permute-start.11 = (bf16[8,8,3200]{2,1,0:T(8,128)(2,1)S(1)}, bf16[8,8,3200]{2,1,0:T(8,128)(2,1)S(1)}, u32[]{:S(2)}, u32[]{:S(2)}) collective-permute-start(bf16[8,8,3200]{2,1,0:T(8,128)(2,1)S(1)} %slice_bitcast_fusion.8), channel_id=1, source_target_pairs={{0,1},{1,0},{2,3},{3,2},{4,5},{5,4},{6,7},{7,6},{8,9},{9,8},{10,11... | collective-permute-start | bytes 1228808 | tf_op jit(solution)/shard_map/ppermute | solution.py:52
  78.0 2.0 %copy-start.4 = (bf16[1,3200,576]{1,2,0:T(8,128)(2,1)S(1)}, bf16[1,3200,576]{1,2,0:T(8,128)(2,1)}, u32[]{:S(2)}) copy-start(bf16[1,3200,576]{1,2,0:T(8,128)(2,1)} %param.22) | copy-start | bytes 11059204
  80.1 0.9 copy-start.17
  80.1 0.9 copy-start.18
  80.1 5.8 %copy-start.5 = (bf16[128,3200]{1,0:T(8,128)(2,1)S(1)}, bf16[128,3200]{1,0:T(8,128)(2,1)}, u32[]{:S(2)}) copy-start(bf16[128,3200]{1,0:T(8,128)(2,1)} %convolution_convert_fusion) | copy-start | bytes 2457604
  81.1 13.1 %collective-permute-start.10 = (bf16[8,8,3328]{2,1,0:T(8,128)(2,1)S(1)}, bf16[8,8,3328]{2,1,0:T(8,128)(2,1)S(1)}, u32[]{:S(2)}, u32[]{:S(2)}) collective-permute-start(bf16[8,8,3328]{2,1,0:T(8,128)(2,1)S(1)} %fusion.27), channel_id=1, source_target_pairs={{0,1},{1,0},{2,3},{3,2},{4,5},{5,4},{6,7},{7,6},{8,9},{9,8},{10,11... | collective-permute-start | bytes 1277960 | tf_op jit(solution)/shard_map/ppermute | solution.py:52
  94.4 2.4 %copy-start.13 = (s32[64]{0:T(128)S(1)}, s32[64]{0:T(128)}, u32[]{:S(2)}) copy-start(s32[64]{0:T(128)} %copy-done.12) | copy-start | bytes 772
  94.5 16.7 %copy-start.15 = (s32[64]{0:T(128)S(1)}, s32[64]{0:T(128)}, u32[]{:S(2)}) copy-start(s32[64]{0:T(128)} %copy-done.14) | copy-start | bytes 772
  94.6 7.1 %collective-permute-start.13 = (bf16[2,8,6528]{2,1,0:T(8,128)(2,1)S(1)}, bf16[2,8,6528]{2,1,0:T(8,128)(2,1)S(1)}, u32[]{:S(2)}, u32[]{:S(2)}) collective-permute-start(bf16[2,8,6528]{2,1,0:T(8,128)(2,1)S(1)} %pad_maximum_fusion.4), channel_id=1, source_target_pairs={{0,14},{1,15},{2,0},{3,1},{4,2},{5,3},{6,4},{7,5},{8,6},{9,7},{10,... | collective-permute-start | bytes 626696 | tf_op jit(solution)/shard_map/ppermute | solution.py:47
  94.7 9.9 %collective-permute-start.12 = (bf16[2,8,6528]{2,1,0:T(8,128)(2,1)S(1)}, bf16[2,8,6528]{2,1,0:T(8,128)(2,1)S(1)}, u32[]{:S(2)}, u32[]{:S(2)}) collective-permute-start(bf16[2,8,6528]{2,1,0:T(8,128)(2,1)S(1)} %pad_maximum_fusion.3), channel_id=1, source_target_pairs={{0,2},{1,3},{2,4},{3,5},{4,6},{5,7},{6,8},{7,9},{8,10},{9,11},{10,... | collective-permute-start | bytes 626696 | tf_op jit(solution)/shard_map/ppermute | solution.py:47
  97.4 9.3 %collective-permute-start.14 = (bf16[8,3200]{1,0:T(8,128)(2,1)S(1)}, bf16[8,3200]{1,0:T(8,128)(2,1)S(1)}, u32[]{:S(2)}, u32[]{:S(2)}) collective-permute-start(bf16[8,3200]{1,0:T(8,128)(2,1)S(1)} %slice.179), channel_id=1, source_target_pairs={{0,4},{1,5},{2,6},{3,7},{4,8},{5,9},{6,10},{7,11},{8,12},{9,13},{1... | collective-permute-start | bytes 153608 | tf_op jit(solution)/shard_map/ppermute | solution.py:47
  101.7 5.6 %collective-permute-start.16 = (bf16[8,3328]{1,0:T(8,128)(2,1)S(1)}, bf16[8,3328]{1,0:T(8,128)(2,1)S(1)}, u32[]{:S(2)}, u32[]{:S(2)}) collective-permute-start(bf16[8,3328]{1,0:T(8,128)(2,1)S(1)} %slice.186), channel_id=1, source_target_pairs={{0,12},{1,13},{2,14},{3,15},{4,0},{5,1},{6,2},{7,3},{8,4},{9,5},{1... | collective-permute-start | bytes 159752 | tf_op jit(solution)/shard_map/ppermute | solution.py:47
  104.6 2.8 %copy-start.7 = (bf16[2,8,6528]{2,1,0:T(8,128)(2,1)}, bf16[2,8,6528]{2,1,0:T(8,128)(2,1)S(1)}, u32[]{:S(2)}) copy-start(bf16[2,8,6528]{2,1,0:T(8,128)(2,1)S(1)} %collective-permute-done.12) | copy-start | bytes 626692
  104.7 12.3 %copy-start.11 = (f32[8]{0:T(128)S(1)}, f32[8]{0:T(128)}, u32[]{:S(2)}) copy-start(f32[8]{0:T(128)} %copy-done.10) | copy-start | bytes 100
  104.7 12.3 %copy-start.16 = (f32[8]{0:T(128)S(1)}, f32[8]{0:T(128)}, u32[]{:S(2)}) copy-start(f32[8]{0:T(128)} %fusion.20) | copy-start | bytes 100
  104.7 12.5 %copy-start.9 = (bf16[8,64]{1,0:T(8,128)(2,1)S(1)}, bf16[8,64]{1,0:T(8,128)(2,1)}, u32[]{:S(2)}) copy-start(bf16[8,64]{1,0:T(8,128)(2,1)} %fusion.64) | copy-start | bytes 3076
  106.7 6.9 %collective-permute-start.15 = (bf16[8,6528]{1,0:T(8,128)(2,1)S(1)}, bf16[8,6528]{1,0:T(8,128)(2,1)S(1)}, u32[]{:S(2)}, u32[]{:S(2)}) collective-permute-start(bf16[8,6528]{1,0:T(8,128)(2,1)S(1)} %pad_maximum_fusion.6), channel_id=1, source_target_pairs={{0,4},{1,5},{2,6},{3,7},{4,8},{5,9},{6,10},{7,11},{8,12},{9,13},{1... | collective-permute-start | bytes 313352 | tf_op jit(solution)/shard_map/ppermute | solution.py:47
  107.4 7.4 %collective-permute-start.17 = (bf16[8,6528]{1,0:T(8,128)(2,1)S(1)}, bf16[8,6528]{1,0:T(8,128)(2,1)S(1)}, u32[]{:S(2)}, u32[]{:S(2)}) collective-permute-start(bf16[8,6528]{1,0:T(8,128)(2,1)S(1)} %pad_maximum_fusion.7), channel_id=1, source_target_pairs={{0,12},{1,13},{2,14},{3,15},{4,0},{5,1},{6,2},{7,3},{8,4},{9,5},{1... | collective-permute-start | bytes 313352 | tf_op jit(solution)/shard_map/ppermute | solution.py:47
  117.2 3.3 %collective-permute-start.20 = (bf16[8,3328]{1,0:T(8,128)(2,1)S(1)}, bf16[8,3328]{1,0:T(8,128)(2,1)S(1)}, u32[]{:S(2)}, u32[]{:S(2)}) collective-permute-start(bf16[8,3328]{1,0:T(8,128)(2,1)S(1)} %fusion.54), channel_id=1, source_target_pairs={{0,240},{16,0},{32,16},{48,32},{64,48},{80,64},{96,80},{112,96},{1... | collective-permute-start | bytes 159752 | tf_op jit(solution)/shard_map/ppermute | solution.py:15
  118.7 7.2 %collective-permute-start.18 = (bf16[8,3328]{1,0:T(8,128)(2,1)S(1)}, bf16[8,3328]{1,0:T(8,128)(2,1)S(1)}, u32[]{:S(2)}, u32[]{:S(2)}) collective-permute-start(bf16[8,3328]{1,0:T(8,128)(2,1)S(1)} %fusion.53), channel_id=1, source_target_pairs={{0,16},{16,32},{32,48},{48,64},{64,80},{80,96},{96,112},{112,128},... | collective-permute-start | bytes 159752 | tf_op jit(solution)/shard_map/ppermute | solution.py:15

commit v3 on v0

v3 whole, which is shorter than its diff:
```python
import jax
import jax.numpy as jnp
from jax import lax
from jax.experimental import pallas as pl
from jax.experimental.pallas import tpu as pltpu
from jax.sharding import PartitionSpec as P

EXPERTS = 16
EPS = 1e-05
LANES = 128
CHUNKS = 3
VMEM_LIMIT = 20 * 1024 * 1024
VMEM = pl.BlockSpec(memory_space=pltpu.VMEM)
SMEM = pl.BlockSpec(memory_space=pltpu.SMEM)
NT = (((1,), (1,)), ((), ()))
TN = (((0,), (0,)), ((), ()))


def along_z(value, steps):
    count = lax.axis_size("dp")
    pairs = [(source, (source + 2 * steps) % count) for source in range(count)]
    return lax.ppermute(value, "dp", pairs)


def swap_x(value):
    count = lax.axis_size("dp")
    return lax.ppermute(value, "dp", [(source, source ^ 1) for source in range(count)])


def across(value, stages, steps):
    n_pipe, n_dp = lax.axis_size("pipe"), lax.axis_size("dp")
    pairs = [
        (p * n_dp + d, (p + stages) % n_pipe * n_dp + (d + 2 * steps) % n_dp)
        for p in range(n_pipe)
        for d in range(n_dp)
    ]
    return lax.ppermute(value, ("pipe", "dp"), pairs)


def split3(value):
    high = value.astype(jnp.bfloat16)
    rest = value - high.astype(jnp.float32)
    middle = rest.astype(jnp.bfloat16)
    low = (rest - middle.astype(jnp.float32)).astype(jnp.bfloat16)
    return [part.astype(jnp.float32) for part in (high, middle, low)]


def columns(parts, rows):
    lane = lax.broadcasted_iota(jnp.int32, (rows, LANES), 1)
    out = jnp.zeros((rows, LANES), jnp.float32)
    for at, part in parts:
        out = jnp.where(lane == at, part, out)
    return out


def head_kernel(capacity, f_ids, b_ids, f_len, b_len, f_in, b_in, grad, gain, router, rows, f_pack, b_pack):
    tok_count = f_in.shape[0]

    def place(ids):
        chosen = jnp.where(ids[...] == 0, 1.0, 0.0)
        chosen = jnp.broadcast_to(chosen, (capacity, tok_count))
        before = lax.broadcasted_iota(jnp.int32, (tok_count, tok_count), 0)
        after = lax.broadcasted_iota(jnp.int32, (tok_count, tok_count), 1)
        upto = jnp.where(before <= after, 1.0, 0.0).astype(jnp.bfloat16)
        rank = jnp.dot(chosen.astype(jnp.bfloat16), upto, preferred_element_type=jnp.float32)
        slot = lax.broadcasted_iota(jnp.int32, (capacity, tok_count), 0).astype(jnp.float32)
        return jnp.where((rank - 1.0 == slot) & (chosen > 0.0), 1.0, 0.0)

    def side(ids, length, tokens):
        placing = place(ids)
        position = lax.broadcasted_iota(jnp.int32, (capacity, tok_count), 1)
        mask = jnp.sum(jnp.where(position < length[0, 0], placing, 0.0), axis=1, keepdims=True)
        values = jnp.dot(
            placing.astype(jnp.bfloat16), tokens[...], preferred_element_type=jnp.float32
        )
        inv = lax.rsqrt(jnp.mean(values * values, axis=1, keepdims=True) + EPS)
        normed = (values * inv * gain[...]).astype(jnp.bfloat16).astype(jnp.float32)
        logit = jnp.sum(normed * router[...].astype(jnp.float32), axis=1, keepdims=True)
        prob = 1.0 / (1.0 + jnp.exp(-logit))
        return placing, mask, values, inv, normed, prob

    def lanes_of(placing, scalars):
        parts = []
        for at, scalar in enumerate(scalars):
            parts += [(tok_count + 3 * at + i, part) for i, part in enumerate(split3(scalar))]
        wide = jnp.concatenate([placing, jnp.zeros((capacity, LANES - tok_count), jnp.float32)], axis=1)
        return wide + columns(parts, capacity)

    placing, mask, values, inv, normed, prob = side(b_ids, b_len, b_in)
    grads = jnp.dot(placing.astype(jnp.bfloat16), grad[...], preferred_element_type=jnp.float32)
    gain_parts = split3(gain[...])
    router32 = router[...].astype(jnp.float32)
    width = values.shape[1]
    meta = jnp.concatenate([values] + gain_parts + [router32, jnp.zeros((4, width), jnp.float32)], axis=0)
    b_lanes = lanes_of(placing, (prob, inv, mask * prob * (1.0 - prob)))
    b_pack[:tok_count, :width] = grad[...]
    b_pack[tok_count:, :width] = meta.astype(jnp.bfloat16)
    b_pack[:tok_count, width:] = jnp.zeros((tok_count, LANES), jnp.bfloat16)
    b_pack[tok_count:, width:] = jnp.concatenate([b_lanes, jnp.zeros_like(b_lanes)], axis=0).astype(jnp.bfloat16)
    f_placing, f_mask, f_values, f_inv, f_normed, f_prob = side(f_ids, f_len, f_in)
    rows[...] = jnp.concatenate([normed, grads * mask, f_normed], axis=0).astype(jnp.bfloat16)
    f_lanes = lanes_of(f_placing, (f_mask * f_prob,))
    f_pack[:, :width] = f_in[...]
    f_pack[:, width:] = jnp.concatenate(
        [f_lanes, jnp.zeros((tok_count - capacity, LANES), jnp.float32)], axis=0
    ).astype(jnp.bfloat16)


def head(capacity, f_ids, b_ids, f_len, b_len, f_in, b_in, grad, gain, router):
    tok_count, width = f_in.shape
    return pl.pallas_call(
        lambda *refs: head_kernel(capacity, *refs),
        out_shape=(
            jax.ShapeDtypeStruct((3 * capacity, width), jnp.bfloat16),
            jax.ShapeDtypeStruct((tok_count, width + LANES), jnp.bfloat16),
            jax.ShapeDtypeStruct((tok_count + 2 * capacity, width + LANES), jnp.bfloat16),
        ),
        in_specs=[VMEM, VMEM, SMEM, SMEM] + [VMEM] * 5,
        out_specs=(VMEM,) * 3,
        compiler_params=pltpu.CompilerParams(vmem_limit_bytes=8 * 1024 * 1024),
        name="head",
    )(f_ids, b_ids, f_len, b_len, f_in, b_in, grad, gain, router)


def sigmoid(value):
    return 1.0 / (1.0 + jnp.exp(-value))


def dot_t(left, right):
    return lax.dot_general(left, right, NT, preferred_element_type=jnp.float32)


def dot(left, right):
    return jnp.dot(left, right, preferred_element_type=jnp.float32)


def chunk_of(step, weights):
    part = weights[0].shape[0] // CHUNKS
    return [weight[step * part : (step + 1) * part] for weight in weights]


def forward_kernel(own, other, after, gate_w, up_w, down_w, mine, theirs, rows, total):
    half = own.shape[0]
    rows[:half] = own[...]
    rows[half:] = other[...]
    for step in range(CHUNKS):
        gate, up, down = chunk_of(step, (gate_w, up_w, down_w))
        gate_pre = dot_t(rows[...], gate)
        up_pre = dot_t(rows[...], up)
        hidden = (gate_pre * sigmoid(gate_pre) * up_pre).astype(jnp.bfloat16)
        if step == 0:
            total[...] = dot(hidden, down)
        elif step < CHUNKS - 1:
            total[...] += dot(hidden, down)
        else:
            part = total[...] + dot(hidden, down)
            mine[...] = part[:half]
            theirs[...] = part[half:].astype(jnp.bfloat16)


def backward_kernel(capacity, groups, after, gate_w, up_w, down_w, mine, theirs, rows, grads, total):
    half, width = mine.shape[0], rows.shape[1]
    pair = 2 * capacity
    blocks = [(ref, at) for ref in groups for at in range(0, ref.shape[0], pair)]
    for at in range(0, len(blocks), 2):
        low, high = [ref[start : start + pair].astype(jnp.float32) for ref, start in blocks[at : at + 2]]
        place = slice(at * capacity, at * capacity + pair)
        rows[place] = jnp.concatenate([low[:capacity], high[:capacity]], axis=0).astype(jnp.bfloat16)
        grads[place] = jnp.concatenate([low[capacity:], high[capacity:]], axis=0).astype(jnp.bfloat16)

    dots = jnp.zeros((2 * half, 1), jnp.float32)
    for step in range(CHUNKS):
        gate, up, down = chunk_of(step, (gate_w, up_w, down_w))
        gate_pre = dot_t(rows[...], gate)
        up_pre = dot_t(rows[...], up)
        d_hidden = dot_t(grads[...], down)
        gate_sig = sigmoid(gate_pre)
        silu = gate_pre * gate_sig
        hidden = (silu * up_pre).astype(jnp.bfloat16).astype(jnp.float32)
        dots += jnp.sum(hidden * d_hidden, axis=1, keepdims=True)
        d_gate = (d_hidden * up_pre * gate_sig * (1.0 + gate_pre * (1.0 - gate_sig))).astype(jnp.bfloat16)
        d_up = (d_hidden * silu).astype(jnp.bfloat16)
        part = dot(d_gate, gate) + dot(d_up, up)
        if step == 0:
            total[...] = part
        elif step < CHUNKS - 1:
            total[...] += part
        else:
            part += total[...]
            mine[:, :width] = part[:half]
            theirs[:, :width] = part[half:].astype(jnp.bfloat16)
    high = dots.astype(jnp.bfloat16).astype(jnp.float32)
    tail = columns([(0, high), (1, dots - high)], 2 * half)
    mine[:, width:] = tail[:half]
    theirs[:, width:] = tail[half:].astype(jnp.bfloat16)


def expert_call(kernel, name, operands, weights, extra, count, spaces, products, scratch):
    hidden, width = weights[0].shape
    half = count // 2
    return pl.pallas_call(
        kernel,
        out_shape=(
            jax.ShapeDtypeStruct((half, width + extra), jnp.float32),
            jax.ShapeDtypeStruct((half, width + extra), jnp.bfloat16),
        ),
        in_specs=spaces + [VMEM] * 3,
        out_specs=(VMEM, VMEM),
        scratch_shapes=[pltpu.VMEM((count, width), jnp.bfloat16)] * scratch
        + [pltpu.VMEM((count, width), jnp.float32)],
        compiler_params=pltpu.CompilerParams(vmem_limit_bytes=VMEM_LIMIT),
        cost_estimate=pl.CostEstimate(
            flops=products * 2 * count * hidden * width, bytes_accessed=6 * hidden * width, transcendentals=0
        ),
        name=name,
    )(*operands, *weights)


def hold(after, weights):
    def kernel(after, gate_w, up_w, down_w, held):
        held[...] = jnp.zeros_like(held)

    return pl.pallas_call(
        kernel,
        out_shape=jax.ShapeDtypeStruct((8, LANES), jnp.float32),
        in_specs=[pl.BlockSpec(memory_space=pl.ANY)] + [VMEM] * 3,
        out_specs=VMEM,
        compiler_params=pltpu.CompilerParams(vmem_limit_bytes=2 * 1024 * 1024),
        cost_estimate=pl.CostEstimate(
            flops=0, bytes_accessed=6 * weights[0].shape[0] * weights[0].shape[1], transcendentals=0
        ),
        name="hold",
    )(after, *weights)


def forward_expert(own, other, after, weights):
    spaces = [VMEM, VMEM, pl.BlockSpec(memory_space=pl.ANY)]
    return expert_call(
        forward_kernel, "forward_expert", (own, other, after), weights, 0, 2 * own.shape[0], spaces, 3, 1
    )


def backward_expert(capacity, groups, after, weights):
    count = sum(group.shape[0] for group in groups) // 2

    def kernel(*refs):
        backward_kernel(capacity, refs[: len(groups)], *refs[len(groups) :])

    return expert_call(
        kernel,
        "backward_expert",
        groups + [after],
        weights,
        LANES,
        count,
        [VMEM] * len(groups) + [pl.BlockSpec(memory_space=pl.ANY)],
        5,
        2,
    )


def scalar_of(lanes, tok_count, at):
    first = tok_count + 3 * at
    return lanes[:, first : first + 1] + lanes[:, first + 1 : first + 2] + lanes[:, first + 2 : first + 3]


def overlay(placing, rows, tokens, out):
    place16 = placing.astype(jnp.bfloat16)
    placed = lax.dot_general(place16, rows.astype(jnp.bfloat16), TN, preferred_element_type=jnp.float32)
    ones = jnp.ones((placing.shape[0], LANES), jnp.bfloat16)
    chosen = lax.dot_general(place16, ones, TN, preferred_element_type=jnp.float32)
    out[...] = jnp.where(chosen[:, :1] > 0.0, placed, tokens[...].astype(jnp.float32)).astype(jnp.bfloat16)


def forward_finish_kernel(capacity, sums, pack, out):
    tok_count, width = out.shape
    lanes = pack[:, width:].astype(jnp.float32)[:capacity]
    placing = lanes[:, :tok_count]
    tokens = pack[:, :width]
    values = dot(placing.astype(jnp.bfloat16), tokens)
    result = sums[...].astype(jnp.bfloat16).astype(jnp.float32)
    overlay(placing, values + scalar_of(lanes, tok_count, 0) * result, tokens, out)


def backward_finish_kernel(capacity, sums, pack, out):
    tok_count, width = out.shape
    lanes = pack[tok_count:, width:].astype(jnp.float32)[:capacity]
    wide = pack[tok_count:, :width].astype(jnp.float32)
    tokens = pack[:tok_count, :width]
    values = wide[:capacity]
    gain = wide[capacity : capacity + 1] + wide[capacity + 1 : capacity + 2] + wide[capacity + 2 : capacity + 3]
    router = wide[capacity + 3 : capacity + 4]
    placing = lanes[:, :tok_count]
    prob, inv, slope = [scalar_of(lanes, tok_count, at) for at in range(3)]
    grads = dot(placing.astype(jnp.bfloat16), tokens)
    d_rows = sums[:, :width].astype(jnp.bfloat16).astype(jnp.float32)
    row_dot = sums[:, width : width + 1] + sums[:, width + 1 : width + 2]
    weighted = gain * (prob * d_rows + (slope * row_dot) * router)
    inner = jnp.mean(weighted * values, axis=1, keepdims=True)
    overlay(placing, grads + inv * weighted - values * inv * inv * inv * inner, tokens, out)


def finish(kernel, name, capacity, sums, pack, tok_count):
    return pl.pallas_call(
        lambda *refs: kernel(capacity, *refs),
        out_shape=jax.ShapeDtypeStruct((tok_count, pack.shape[1] - LANES), pack.dtype),
        in_specs=[VMEM, VMEM],
        out_specs=VMEM,
        compiler_params=pltpu.CompilerParams(vmem_limit_bytes=8 * 1024 * 1024),
        name=name,
    )(sums, pack)


def gather_column(own):
    half = own.shape[1] // (2 * LANES) * LANES
    below2 = along_z(own, 2)
    above2 = along_z(own, -2)
    below1 = along_z(own, 1)
    above1 = along_z(own, -1)
    below3 = along_z(below2, 1)
    above3 = along_z(above2, -1)
    far_low = along_z(below2[:, :half], 2)
    far_high = along_z(above2[:, half:], -2)
    far = jnp.concatenate([far_low, far_high], axis=1)
    return [own], [below1, above1, below2, above2], [below3, above3, far]


def sum_columns(b_total, f_total, capacity):
    width = b_total.shape[1]
    low, full = jnp.bfloat16, jnp.float32
    total = jnp.concatenate([b_total, f_total], axis=1)
    own, below1, above1, below2, above2, below3, above3, far = [
        total[at * capacity : (at + 1) * capacity] for at in range(total.shape[0] // capacity)
    ]
    up = along_z(jnp.concatenate([above1, above3], axis=0).astype(low), 1).astype(full)
    down = along_z(jnp.concatenate([below1, below3], axis=0).astype(low), -1).astype(full)
    far_b = along_z(far[:, :width].astype(low), 2).astype(full)
    far_f = along_z(far[:, width:].astype(low), -2).astype(full)
    above2 = above2 + up[capacity:]
    below2 = below2 + down[capacity:]
    near = own + up[:capacity] + down[:capacity]
    b_up = across((above2[:, :width] + far_b).astype(low), -1, 2)
    b_down = across(below2[:, :width].astype(low), -1, -2)
    f_up = across(above2[:, width:].astype(low), 1, 2)
    f_down = across((below2[:, width:] + far_f).astype(low), 1, -2)
    b_near = across(near[:, :width].astype(low), -1, 0)
    f_near = across(near[:, width:].astype(low), 1, 0)

    def add(parts):
        return sum(part.astype(full) for part in parts)

    return add((b_near, b_up, b_down)), add((f_near, f_up, f_down))


def body(
    fwd_in,
    fwd_ids,
    fwd_lengths,
    bwd_in,
    bwd_grad,
    bwd_ids,
    bwd_lengths,
    norm_gain,
    router,
    w_gate,
    w_up,
    w_down,
):
    tok_count = fwd_in.shape[1]
    capacity = max(2, 2 * tok_count // EXPERTS)
    weights = (w_gate[0].T, w_up[0].T, w_down[0])

    rows, f_pack, b_pack = head(
        capacity, fwd_ids, bwd_ids, fwd_lengths, bwd_lengths, fwd_in[0], bwd_in[0], bwd_grad[0], norm_gain, router
    )
    f_pack = across(f_pack, 1, 0)
    b_pack = across(b_pack, -1, 0)
    own, near, far = gather_column(rows)
    pair = 2 * capacity
    groups = [jnp.concatenate([block[:pair] for block in group], axis=0) for group in (own, near, far)]
    f_own = jnp.concatenate([block[pair:] for block in own + near + far], axis=0)
    others = [swap_x(group) for group in groups]
    f_own, others[2] = lax.optimization_barrier((f_own, others[2]))
    f_other = swap_x(f_own)

    b_mine, b_theirs = backward_expert(capacity, groups + others, hold(groups[2], weights), weights)
    f_mine, f_theirs = forward_expert(f_own, f_other, b_theirs, weights)
    b_total = b_mine + swap_x(b_theirs).astype(jnp.float32)
    f_total = f_mine + swap_x(f_theirs).astype(jnp.float32)
    b_sums, f_sums = sum_columns(b_total, f_total, capacity)
    bwd_out = finish(backward_finish_kernel, "backward_finish", capacity, b_sums, b_pack, tok_count)
    fwd_out = finish(forward_finish_kernel, "forward_finish", capacity, f_sums, f_pack, tok_count)
    return (fwd_out[None], bwd_out[None])


def solution(mesh):
    in_specs = (
        P("pipe", "dp", None),
        P("pipe", "dp"),
        P("pipe", "dp"),
        P("pipe", "dp", None),
        P("pipe", "dp", None),
        P("pipe", "dp"),
        P("pipe", "dp"),
        P("pipe", None),
        P("pipe", None),
        P("pipe", None, "dp"),
        P("pipe", None, "dp"),
        P("pipe", "dp", None),
    )
    out_specs = (P("pipe", "dp", None), P("pipe", "dp", None))
    return jax.shard_map(body, mesh=mesh, in_specs=in_specs, out_specs=out_specs, check_vma=False)
```

time: 308 us -> 113 us (0.37)
  the two profiles are of different devices: /device:TPU:4 before, /device:TPU:1 now
where the time goes in v3:
time: 113 us; the launch traced here: 112 us
  starting transfers between devices  49.7 us (44%)
  waiting for transfers between devices  36.4 us (32%)
  Pallas kernels  13.2 us (12%)
  local copies, waits for them, and re-layouts  10.1 us (9%)
  between operations  2.21 us (2%)
    ppermute x12, starting transfers between devices, along_z(): return lax.ppermute(value, 'dp', pairs)  23 us
    ppermute x8, starting transfers between devices, across(): return lax.ppermute(value, ('pipe', 'dp'), pairs)  19.2 us
    ppermute x6, waiting for transfers between devices, swap_x(): lax.ppermute(value, 'dp', [(source, source ^ 1) for source in range(count)])  17.7 us
    ppermute x12, waiting for transfers between devices, along_z(): return lax.ppermute(value, 'dp', pairs)  11.5 us
    unnamed x32, local copies, waits for them, and re-layouts  9.89 us
    pallas_call x2, Pallas kernels, expert_call(): pl.pallas_call(kernel, out_shape=(jax.ShapeDtypeStruct((half, width + ext...  9.72 us
    ppermute x6, starting transfers between devices, swap_x(): lax.ppermute(value, 'dp', [(source, source ^ 1) for source in range(count)])  7.48 us
    ppermute x8, waiting for transfers between devices, across(): return lax.ppermute(value, ('pipe', 'dp'), pairs)  7.11 us
  transfers between devices with their start and end apart: 26, of which 15 were waited for; matrix products, arithmetic and copies ran while one was open for 1% of the time, Pallas kernels for 10%

profile of v3, /device:TPU:1, one launch (start us, length us, event | category | flops | bytes accessed | tf_op | source)
XLA Modules:
  0.0 112.2 jit_solution(17760316526157249781)
XLA Ops:
  1.9 1.0 copy-done.5
  2.9 1.0 copy-done.6
  3.9 1.0 copy-done.7
  4.9 0.7 copy-done.8
  5.6 0.7 copy-done.9
  6.3 0.7 copy-done.10
  7.0 0.7 copy-done.11
  7.7 0.8 head.1
  8.4 2.5 %collective-permute-start = (bf16[24,3200]{1,0:T(8,128)(2,1)S(1)}, bf16[24,3200]{1,0:T(8,128)(2,1)S(1)}, u32[]{:S(2)}, u32[]{:S(2)}) collective-permute-start(bf16[24,3200]{1,0:T(8,128)(2,1)S(1)} %get-tuple-element.11), channel_id=1, source_target_pairs={{0,2},{1,3},{2,4},{3,5},{4,6},{5,7},{6,8},{7,9},{8,10},{9,11},{10,... | collective-permute-start | bytes 460808 | tf_op jit(solution)/shard_map/ppermute | solution.py:22
  11.0 4.0 %collective-permute-start.1 = (bf16[24,3200]{1,0:T(8,128)(2,1)S(1)}, bf16[24,3200]{1,0:T(8,128)(2,1)S(1)}, u32[]{:S(2)}, u32[]{:S(2)}) collective-permute-start(bf16[24,3200]{1,0:T(8,128)(2,1)S(1)} %get-tuple-element.11), channel_id=1, source_target_pairs={{0,14},{1,15},{2,0},{3,1},{4,2},{5,3},{6,4},{7,5},{8,6},{9,7},{10,... | collective-permute-start | bytes 460808 | tf_op jit(solution)/shard_map/ppermute | solution.py:22
  15.0 3.6 %collective-permute-start.3 = (bf16[24,3200]{1,0:T(8,128)(2,1)S(1)}, bf16[24,3200]{1,0:T(8,128)(2,1)S(1)}, u32[]{:S(2)}, u32[]{:S(2)}) collective-permute-start(bf16[24,3200]{1,0:T(8,128)(2,1)S(1)} %get-tuple-element.11), channel_id=1, source_target_pairs={{0,12},{1,13},{2,14},{3,15},{4,0},{5,1},{6,2},{7,3},{8,4},{9,5},{1... | collective-permute-start | bytes 460808 | tf_op jit(solution)/shard_map/ppermute | solution.py:22
  18.6 1.3 %collective-permute-start.8 = (bf16[16,3200]{1,0:T(8,128)(2,1)S(1)}, bf16[16,3200]{1,0:T(8,128)(2,1)S(1)}, u32[]{:S(2)}, u32[]{:S(2)}) collective-permute-start(bf16[16,3200]{1,0:T(8,128)(2,1)S(1)} %slice.126.refs_0_), channel_id=1, source_target_pairs={{0,1},{1,0},{2,3},{3,2},{4,5},{5,4},{6,7},{7,6},{8,9},{9,8},{10,11... | collective-permute-start | bytes 307208 | tf_op jit(solution)/shard_map/ppermute | solution.py:27
  19.9 4.6 %collective-permute-done.2 = bf16[24,3200]{1,0:T(8,128)(2,1)S(1)} collective-permute-done((bf16[24,3200]{1,0:T(8,128)(2,1)S(1)}, bf16[24,3200]{1,0:T(8,128)(2,1)S(1)}, u32[]{:S(2)}, u32[]{:S(2)}) %collective-permute-start.2) | collective-permute-done | bytes 153632 | tf_op jit(solution)/shard_map/ppermute | solution.py:22
  24.5 0.6 collective-permute-start.6
  25.1 0.8 collective-permute-done.3
  26.0 2.9 %collective-permute-start.7 = (bf16[24,1664]{1,0:T(8,128)(2,1)S(1)}, bf16[24,1664]{1,0:T(8,128)(2,1)S(1)}, u32[]{:S(2)}, u32[]{:S(2)}) collective-permute-start(bf16[24,1664]{1,0:T(8,128)(2,1)S(1)} %slice.170), channel_id=1, source_target_pairs={{0,12},{1,13},{2,14},{3,15},{4,0},{5,1},{6,2},{7,3},{8,4},{9,5},{1... | collective-permute-start | bytes 239624 | tf_op jit(solution)/shard_map/ppermute | solution.py:22
  29.0 1.3 %collective-permute-start.9 = (bf16[64,3200]{1,0:T(8,128)(2,1)S(1)}, bf16[64,3200]{1,0:T(8,128)(2,1)S(1)}, u32[]{:S(2)}, u32[]{:S(2)}) collective-permute-start(bf16[64,3200]{1,0:T(8,128)(2,1)S(1)} %pad_maximum_fusion.1.refs_1_), channel_id=1, source_target_pairs={{0,1},{1,0},{2,3},{3,2},{4,5},{5,4},{6,7},{7,6},{8,9},{9,8},{10,11... | collective-permute-start | bytes 1228808 | tf_op jit(solution)/shard_map/ppermute | solution.py:27
  30.6 2.6 %collective-permute-start.5 = (bf16[24,3200]{1,0:T(8,128)(2,1)S(1)}, bf16[24,3200]{1,0:T(8,128)(2,1)S(1)}, u32[]{:S(2)}, u32[]{:S(2)}) collective-permute-start(bf16[24,3200]{1,0:T(8,128)(2,1)S(1)} %collective-permute-done.3), channel_id=1, source_target_pairs={{0,14},{1,15},{2,0},{3,1},{4,2},{5,3},{6,4},{7,5},{8,6},{9,7},{10,... | collective-permute-start | bytes 460808 | tf_op jit(solution)/shard_map/ppermute | solution.py:22
  33.2 0.4 collective-permute-done.7
  33.6 2.0 %collective-permute-done.4 = bf16[24,3200]{1,0:T(8,128)(2,1)S(1)} collective-permute-done((bf16[24,3200]{1,0:T(8,128)(2,1)S(1)}, bf16[24,3200]{1,0:T(8,128)(2,1)S(1)}, u32[]{:S(2)}, u32[]{:S(2)}) %collective-permute-start.4) | collective-permute-done | bytes 153632 | tf_op jit(solution)/shard_map/ppermute | solution.py:22
  35.6 0.9 collective-permute-done.5
  36.5 1.3 %collective-permute-start.10 = (bf16[48,3200]{1,0:T(8,128)(2,1)S(1)}, bf16[48,3200]{1,0:T(8,128)(2,1)S(1)}, u32[]{:S(2)}, u32[]{:S(2)}) collective-permute-start(bf16[48,3200]{1,0:T(8,128)(2,1)S(1)} %pad_maximum_fusion.2.after.refs_2_), channel_id=1, source_target_pairs={{0,1},{1,0},{2,3},{3,2},{4,5},{5,4},{6,7},{7,6},{8,9},{9,8},{10,11... | collective-permute-start | bytes 921608 | tf_op jit(solution)/shard_map/ppermute | solution.py:27
  37.9 2.0 %copy-done.1 = bf16[1,3200,576]{1,2,0:T(8,128)(2,1)S(1)} copy-done((bf16[1,3200,576]{1,2,0:T(8,128)(2,1)S(1)}, bf16[1,3200,576]{1,2,0:T(8,128)(2,1)}, u32[]{:S(2)}) %copy-start.1) | copy-done | bytes 3686424
  39.9 2.0 %copy-done.3 = bf16[1,576,3200]{2,1,0:T(8,128)(2,1)S(1)} copy-done((bf16[1,576,3200]{2,1,0:T(8,128)(2,1)S(1)}, bf16[1,576,3200]{2,1,0:T(8,128)(2,1)}, u32[]{:S(2)}) %copy-start.3) | copy-done | bytes 3686424
  42.0 3.3 %collective-permute-done.10.refs_5_ = bf16[48,3200]{1,0:T(8,128)(2,1)S(1)} collective-permute-done((bf16[48,3200]{1,0:T(8,128)(2,1)S(1)}, bf16[48,3200]{1,0:T(8,128)(2,1)S(1)}, u32[]{:S(2)}, u32[]{:S(2)}) %collective-permute-start.10) | collective-permute-done | bytes 307232 | tf_op jit(solution)/shard_map/ppermute | solution.py:27
  45.3 1.7 %collective-permute-start.12 = (bf16[64,3200]{1,0:T(8,128)(2,1)S(1)}, bf16[64,3200]{1,0:T(8,128)(2,1)S(1)}, u32[]{:S(2)}, u32[]{:S(2)}) collective-permute-start(bf16[64,3200]{1,0:T(8,128)(2,1)S(1)} %slice_dynamic-update-slice_fusion.own), channel_id=1, source_target_pairs={{0,1},{1,0},{2,3},{3,2},{4,5},{5,4},{6,7},{7,6},{8,9},{9,8},{10,11... | collective-permute-start | bytes 1228808 | tf_op jit(solution)/shard_map/ppermute | solution.py:27
  47.0 6.3 %backward_expert.1 = (f32[64,3328]{1,0:T(8,128)S(1)}, bf16[64,3328]{1,0:T(8,128)(2,1)S(1)}) custom-call(bf16[16,3200]{1,0:T(8,128)(2,1)S(1)} %slice.126.refs_0_, bf16[64,3200]{1,0:T(8,128)(2,1)S(1)} %pad_maximum_fusion.1.refs_1_, bf16[48,3200]{1,0:T(8,128)(2,1)S(1)} %pad_maximum_fusion.2.after.refs_2_, bf16[16,3200]{1,0:T(8,128)(2,1)S(1)} %collective-permute-done.8.refs_3_, ...), custom_call_target="tpu_custom_call" | custom-call | flops 2359296000 | bytes 11059200 | tf_op jit(solution)/shard_map/backward_expert/pallas_call | solution.py:201
  53.4 1.0 collective-permute-done.12.other
  54.4 3.4 %forward_expert.1 = (f32[64,3200]{1,0:T(8,128)S(1)}, bf16[64,3200]{1,0:T(8,128)(2,1)S(1)}) custom-call(bf16[64,3200]{1,0:T(8,128)(2,1)S(1)} %slice_dynamic-update-slice_fusion.own, bf16[64,3200]{1,0:T(8,128)(2,1)S(1)} %collective-permute-done.12.other, bf16[64,3328]{1,0:T(8,128)(2,1)S(1)} %get-tuple-element.14.after, bf16[576,3200]{1,0:T(8,128)(2,1)S(1)} %bitcast.14, ...), custom_call_target="tpu_custom_call" | custom-call | flops 1415577600 | bytes 11059200 | tf_op jit(solution)/shard_map/forward_expert/pallas_call | solution.py:201
  57.8 1.8 %collective-permute-start.13 = (bf16[64,3200]{1,0:T(8,128)(2,1)S(1)}, bf16[64,3200]{1,0:T(8,128)(2,1)S(1)}, u32[]{:S(2)}, u32[]{:S(2)}) collective-permute-start(bf16[64,3200]{1,0:T(8,128)(2,1)S(1)} %get-tuple-element.17), channel_id=1, source_target_pairs={{0,1},{1,0},{2,3},{3,2},{4,5},{5,4},{6,7},{7,6},{8,9},{9,8},{10,11... | collective-permute-start | bytes 1228808 | tf_op jit(solution)/shard_map/ppermute | solution.py:27
  59.6 4.8 %collective-permute-done.11 = bf16[64,3328]{1,0:T(8,128)(2,1)S(1)} collective-permute-done((bf16[64,3328]{1,0:T(8,128)(2,1)S(1)}, bf16[64,3328]{1,0:T(8,128)(2,1)S(1)}, u32[]{:S(2)}, u32[]{:S(2)}) %collective-permute-start.11) | collective-permute-done | bytes 426016 | tf_op jit(solution)/shard_map/ppermute | solution.py:27
  64.5 8.7 %collective-permute-done.13 = bf16[64,3200]{1,0:T(8,128)(2,1)S(1)} collective-permute-done((bf16[64,3200]{1,0:T(8,128)(2,1)S(1)}, bf16[64,3200]{1,0:T(8,128)(2,1)S(1)}, u32[]{:S(2)}, u32[]{:S(2)}) %collective-permute-start.13) | collective-permute-done | bytes 409632 | tf_op jit(solution)/shard_map/ppermute | solution.py:27
  73.5 2.7 %collective-permute-start.15 = (bf16[16,6528]{1,0:T(8,128)(2,1)S(1)}, bf16[16,6528]{1,0:T(8,128)(2,1)S(1)}, u32[]{:S(2)}, u32[]{:S(2)}) collective-permute-start(bf16[16,6528]{1,0:T(8,128)(2,1)S(1)} %pad_maximum_fusion.4), channel_id=1, source_target_pairs={{0,14},{1,15},{2,0},{3,1},{4,2},{5,3},{6,4},{7,5},{8,6},{9,7},{10,... | collective-permute-start | bytes 626696 | tf_op jit(solution)/shard_map/ppermute | solution.py:22
  76.3 2.7 %collective-permute-start.25 = (bf16[80,3328]{1,0:T(8,128)(2,1)S(1)}, bf16[80,3328]{1,0:T(8,128)(2,1)S(1)}, u32[]{:S(2)}, u32[]{:S(2)}) collective-permute-start(bf16[80,3328]{1,0:T(8,128)(2,1)S(1)} %get-tuple-element.19), channel_id=1, source_target_pairs={{0,240},{1,241},{2,242},{3,243},{4,244},{5,245},{6,246},{7,247},{8... | collective-permute-start | bytes 1597448 | tf_op jit(solution)/shard_map/ppermute | solution.py:37
  79.0 1.2 %collective-permute-start.20 = (bf16[64,3328]{1,0:T(8,128)(2,1)S(1)}, bf16[64,3328]{1,0:T(8,128)(2,1)S(1)}, u32[]{:S(2)}, u32[]{:S(2)}) collective-permute-start(bf16[64,3328]{1,0:T(8,128)(2,1)S(1)} %get-tuple-element.18), channel_id=1, source_target_pairs={{0,16},{1,17},{2,18},{3,19},{4,20},{5,21},{6,22},{7,23},{8,24},{9,... | collective-permute-start | bytes 1277960 | tf_op jit(solution)/shard_map/ppermute | solution.py:37
  80.1 0.3 collective-permute-start.22
  80.4 3.7 %collective-permute-start.18 = (bf16[8,3200]{1,0:T(8,128)(2,1)S(1)}, bf16[8,3200]{1,0:T(8,128)(2,1)S(1)}, u32[]{:S(2)}, u32[]{:S(2)}) collective-permute-start(bf16[8,3200]{1,0:T(8,128)(2,1)S(1)} %slice.253), channel_id=1, source_target_pairs={{0,12},{1,13},{2,14},{3,15},{4,0},{5,1},{6,2},{7,3},{8,4},{9,5},{1... | collective-permute-start | bytes 153608 | tf_op jit(solution)/shard_map/ppermute | solution.py:22
  84.3 2.6 %collective-permute-done.18 = bf16[8,3200]{1,0:T(8,128)(2,1)S(1)} collective-permute-done((bf16[8,3200]{1,0:T(8,128)(2,1)S(1)}, bf16[8,3200]{1,0:T(8,128)(2,1)S(1)}, u32[]{:S(2)}, u32[]{:S(2)}) %collective-permute-start.18) | collective-permute-done | bytes 51232 | tf_op jit(solution)/shard_map/ppermute | solution.py:22
  86.8 4.5 %collective-permute-start.19 = (bf16[8,3200]{1,0:T(8,128)(2,1)S(1)}, bf16[8,3200]{1,0:T(8,128)(2,1)S(1)}, u32[]{:S(2)}, u32[]{:S(2)}) collective-permute-start(bf16[8,3200]{1,0:T(8,128)(2,1)S(1)} %fusion.10), channel_id=1, source_target_pairs={{0,28},{1,29},{2,30},{3,31},{4,16},{5,17},{6,18},{7,19},{8,20},{9,... | collective-permute-start | bytes 153608 | tf_op jit(solution)/shard_map/ppermute | solution.py:37
  91.4 0.2 collective-permute-start.16
  91.6 1.6 %collective-permute-start.17 = (bf16[8,3200]{1,0:T(8,128)(2,1)S(1)}, bf16[8,3200]{1,0:T(8,128)(2,1)S(1)}, u32[]{:S(2)}, u32[]{:S(2)}) collective-permute-start(bf16[8,3200]{1,0:T(8,128)(2,1)S(1)} %slice.254), channel_id=1, source_target_pairs={{0,20},{1,21},{2,22},{3,23},{4,24},{5,25},{6,26},{7,27},{8,28},{9,... | collective-permute-start | bytes 153608 | tf_op jit(solution)/shard_map/ppermute | solution.py:37
  93.2 2.2 %collective-permute-done.19 = bf16[8,3200]{1,0:T(8,128)(2,1)S(1)} collective-permute-done((bf16[8,3200]{1,0:T(8,128)(2,1)S(1)}, bf16[8,3200]{1,0:T(8,128)(2,1)S(1)}, u32[]{:S(2)}, u32[]{:S(2)}) %collective-permute-start.19) | collective-permute-done | bytes 51232 | tf_op jit(solution)/shard_map/ppermute | solution.py:37
  95.4 9.0 %collective-permute-start.23 = (bf16[8,3328]{1,0:T(8,128)(2,1)S(1)}, bf16[8,3328]{1,0:T(8,128)(2,1)S(1)}, u32[]{:S(2)}, u32[]{:S(2)}) collective-permute-start(bf16[8,3328]{1,0:T(8,128)(2,1)S(1)} %fusion.9), channel_id=1, source_target_pairs={{0,244},{1,245},{2,246},{3,247},{4,248},{5,249},{6,250},{7,251},{8... | collective-permute-start | bytes 159752 | tf_op jit(solution)/shard_map/ppermute | solution.py:37
  104.5 1.3 %forward_finish.1 = bf16[64,3200]{1,0:T(8,128)(2,1)} custom-call(f32[8,3200]{1,0:T(8,128)S(1)} %convert_add_fusion.3.refs_0_, bf16[64,3328]{1,0:T(8,128)(2,1)S(1)} %collective-permute-done.20.refs_1_), custom_call_target="tpu_custom_call" | custom-call | tf_op jit(solution)/shard_map/forward_finish/pallas_call | solution.py:304
  105.8 0.2 collective-permute-done.23
  106.0 2.2 %collective-permute-done.21 = bf16[8,3328]{1,0:T(8,128)(2,1)S(1)} collective-permute-done((bf16[8,3328]{1,0:T(8,128)(2,1)S(1)}, bf16[8,3328]{1,0:T(8,128)(2,1)S(1)}, u32[]{:S(2)}, u32[]{:S(2)}) %collective-permute-start.21) | collective-permute-done | bytes 53280 | tf_op jit(solution)/shard_map/ppermute | solution.py:37
  108.2 2.5 %collective-permute-done.24 = bf16[8,3328]{1,0:T(8,128)(2,1)S(1)} collective-permute-done((bf16[8,3328]{1,0:T(8,128)(2,1)S(1)}, bf16[8,3328]{1,0:T(8,128)(2,1)S(1)}, u32[]{:S(2)}, u32[]{:S(2)}) %collective-permute-start.24) | collective-permute-done | bytes 53280 | tf_op jit(solution)/shard_map/ppermute | solution.py:37
  110.7 1.4 %backward_finish.1 = bf16[64,3200]{1,0:T(8,128)(2,1)} custom-call(f32[8,3328]{1,0:T(8,128)S(1)} %convert_add_fusion.2.refs_0_, bf16[80,3328]{1,0:T(8,128)(2,1)S(1)} %collective-permute-done.25.refs_1_), custom_call_target="tpu_custom_call" | custom-call | tf_op jit(solution)/shard_map/backward_finish/pallas_call | solution.py:304
  (75 shorter events, 1.4 us)
Async XLA Ops:
  1.9 1.0 copy-start.5
  2.9 1.0 copy-start.6
  3.9 1.0 copy-start.7
  4.9 0.7 copy-start.8
  5.6 0.7 copy-start.9
  6.3 0.7 copy-start.10
  7.0 0.7 copy-start.11
  8.4 20.5 %collective-permute-start = (bf16[24,3200]{1,0:T(8,128)(2,1)S(1)}, bf16[24,3200]{1,0:T(8,128)(2,1)S(1)}, u32[]{:S(2)}, u32[]{:S(2)}) collective-permute-start(bf16[24,3200]{1,0:T(8,128)(2,1)S(1)} %get-tuple-element.11), channel_id=1, source_target_pairs={{0,2},{1,3},{2,4},{3,5},{4,6},{5,7},{6,8},{7,9},{8,10},{9,11},{10,... | collective-permute-start | bytes 460808 | tf_op jit(solution)/shard_map/ppermute | solution.py:22
  11.0 18.0 %collective-permute-start.1 = (bf16[24,3200]{1,0:T(8,128)(2,1)S(1)}, bf16[24,3200]{1,0:T(8,128)(2,1)S(1)}, u32[]{:S(2)}, u32[]{:S(2)}) collective-permute-start(bf16[24,3200]{1,0:T(8,128)(2,1)S(1)} %get-tuple-element.11), channel_id=1, source_target_pairs={{0,14},{1,15},{2,0},{3,1},{4,2},{5,3},{6,4},{7,5},{8,6},{9,7},{10,... | collective-permute-start | bytes 460808 | tf_op jit(solution)/shard_map/ppermute | solution.py:22
  15.0 9.5 %collective-permute-start.2 = (bf16[24,3200]{1,0:T(8,128)(2,1)S(1)}, bf16[24,3200]{1,0:T(8,128)(2,1)S(1)}, u32[]{:S(2)}, u32[]{:S(2)}) collective-permute-start(bf16[24,3200]{1,0:T(8,128)(2,1)S(1)} %get-tuple-element.11), channel_id=1, source_target_pairs={{0,4},{1,5},{2,6},{3,7},{4,8},{5,9},{6,10},{7,11},{8,12},{9,13},{1... | collective-permute-start | bytes 460808 | tf_op jit(solution)/shard_map/ppermute | solution.py:22
  15.0 11.0 %collective-permute-start.3 = (bf16[24,3200]{1,0:T(8,128)(2,1)S(1)}, bf16[24,3200]{1,0:T(8,128)(2,1)S(1)}, u32[]{:S(2)}, u32[]{:S(2)}) collective-permute-start(bf16[24,3200]{1,0:T(8,128)(2,1)S(1)} %get-tuple-element.11), channel_id=1, source_target_pairs={{0,12},{1,13},{2,14},{3,15},{4,0},{5,1},{6,2},{7,3},{8,4},{9,5},{1... | collective-permute-start | bytes 460808 | tf_op jit(solution)/shard_map/ppermute | solution.py:22
  18.6 28.4 %collective-permute-start.8 = (bf16[16,3200]{1,0:T(8,128)(2,1)S(1)}, bf16[16,3200]{1,0:T(8,128)(2,1)S(1)}, u32[]{:S(2)}, u32[]{:S(2)}) collective-permute-start(bf16[16,3200]{1,0:T(8,128)(2,1)S(1)} %slice.126.refs_0_), channel_id=1, source_target_pairs={{0,1},{1,0},{2,3},{3,2},{4,5},{5,4},{6,7},{7,6},{8,9},{9,8},{10,11... | collective-permute-start | bytes 307208 | tf_op jit(solution)/shard_map/ppermute | solution.py:27
  24.5 6.1 %collective-permute-start.6 = (bf16[24,1536]{1,0:T(8,128)(2,1)S(1)}, bf16[24,1536]{1,0:T(8,128)(2,1)S(1)}, u32[]{:S(2)}, u32[]{:S(2)}) collective-permute-start(bf16[24,1536]{1,0:T(8,128)(2,1)S(1)} %slice.169), channel_id=1, source_target_pairs={{0,4},{1,5},{2,6},{3,7},{4,8},{5,9},{6,10},{7,11},{8,12},{9,13},{1... | collective-permute-start | bytes 221192 | tf_op jit(solution)/shard_map/ppermute | solution.py:22
  26.0 7.6 %collective-permute-start.7 = (bf16[24,1664]{1,0:T(8,128)(2,1)S(1)}, bf16[24,1664]{1,0:T(8,128)(2,1)S(1)}, u32[]{:S(2)}, u32[]{:S(2)}) collective-permute-start(bf16[24,1664]{1,0:T(8,128)(2,1)S(1)} %slice.170), channel_id=1, source_target_pairs={{0,12},{1,13},{2,14},{3,15},{4,0},{5,1},{6,2},{7,3},{8,4},{9,5},{1... | collective-permute-start | bytes 239624 | tf_op jit(solution)/shard_map/ppermute | solution.py:22
  28.9 8.9 %copy-start = (bf16[1,3200,576]{1,2,0:T(8,128)(2,1)S(1)}, bf16[1,3200,576]{1,2,0:T(8,128)(2,1)}, u32[]{:S(2)}) copy-start(bf16[1,3200,576]{1,2,0:T(8,128)(2,1)} %param.21) | copy-start | bytes 11059204
  29.0 17.9 %collective-permute-start.9 = (bf16[64,3200]{1,0:T(8,128)(2,1)S(1)}, bf16[64,3200]{1,0:T(8,128)(2,1)S(1)}, u32[]{:S(2)}, u32[]{:S(2)}) collective-permute-start(bf16[64,3200]{1,0:T(8,128)(2,1)S(1)} %pad_maximum_fusion.1.refs_1_), channel_id=1, source_target_pairs={{0,1},{1,0},{2,3},{3,2},{4,5},{5,4},{6,7},{7,6},{8,9},{9,8},{10,11... | collective-permute-start | bytes 1228808 | tf_op jit(solution)/shard_map/ppermute | solution.py:27
  30.3 5.3 %collective-permute-start.4 = (bf16[24,3200]{1,0:T(8,128)(2,1)S(1)}, bf16[24,3200]{1,0:T(8,128)(2,1)S(1)}, u32[]{:S(2)}, u32[]{:S(2)}) collective-permute-start(bf16[24,3200]{1,0:T(8,128)(2,1)S(1)} %collective-permute-done.2), channel_id=1, source_target_pairs={{0,2},{1,3},{2,4},{3,5},{4,6},{5,7},{6,8},{7,9},{8,10},{9,11},{10,... | collective-permute-start | bytes 460808 | tf_op jit(solution)/shard_map/ppermute | solution.py:22
  30.6 5.9 %collective-permute-start.5 = (bf16[24,3200]{1,0:T(8,128)(2,1)S(1)}, bf16[24,3200]{1,0:T(8,128)(2,1)S(1)}, u32[]{:S(2)}, u32[]{:S(2)}) collective-permute-start(bf16[24,3200]{1,0:T(8,128)(2,1)S(1)} %collective-permute-done.3), channel_id=1, source_target_pairs={{0,14},{1,15},{2,0},{3,1},{4,2},{5,3},{6,4},{7,5},{8,6},{9,7},{10,... | collective-permute-start | bytes 460808 | tf_op jit(solution)/shard_map/ppermute | solution.py:22
  36.5 8.7 %collective-permute-start.10 = (bf16[48,3200]{1,0:T(8,128)(2,1)S(1)}, bf16[48,3200]{1,0:T(8,128)(2,1)S(1)}, u32[]{:S(2)}, u32[]{:S(2)}) collective-permute-start(bf16[48,3200]{1,0:T(8,128)(2,1)S(1)} %pad_maximum_fusion.2.after.refs_2_), channel_id=1, source_target_pairs={{0,1},{1,0},{2,3},{3,2},{4,5},{5,4},{6,7},{7,6},{8,9},{9,8},{10,11... | collective-permute-start | bytes 921608 | tf_op jit(solution)/shard_map/ppermute | solution.py:27
  37.9 2.0 %copy-start.1 = (bf16[1,3200,576]{1,2,0:T(8,128)(2,1)S(1)}, bf16[1,3200,576]{1,2,0:T(8,128)(2,1)}, u32[]{:S(2)}) copy-start(bf16[1,3200,576]{1,2,0:T(8,128)(2,1)} %param.22) | copy-start | bytes 11059204
  39.9 2.0 %copy-start.3 = (bf16[1,576,3200]{2,1,0:T(8,128)(2,1)S(1)}, bf16[1,576,3200]{2,1,0:T(8,128)(2,1)}, u32[]{:S(2)}) copy-start(bf16[1,576,3200]{2,1,0:T(8,128)(2,1)} %param.23) | copy-start | bytes 11059204
  42.0 5.0 %copy-start.2 = (bf16[1,3200,576]{1,2,0:T(8,128)(2,1)S(1)}, bf16[1,3200,576]{1,2,0:T(8,128)(2,1)}, u32[]{:S(2)}) copy-start(bf16[1,3200,576]{1,2,0:T(8,128)(2,1)} %param.22) | copy-start | bytes 11059204
  42.0 5.0 %copy-start.4 = (bf16[1,576,3200]{2,1,0:T(8,128)(2,1)S(1)}, bf16[1,576,3200]{2,1,0:T(8,128)(2,1)}, u32[]{:S(2)}) copy-start(bf16[1,576,3200]{2,1,0:T(8,128)(2,1)} %param.23) | copy-start | bytes 11059204
  45.3 9.1 %collective-permute-start.12 = (bf16[64,3200]{1,0:T(8,128)(2,1)S(1)}, bf16[64,3200]{1,0:T(8,128)(2,1)S(1)}, u32[]{:S(2)}, u32[]{:S(2)}) collective-permute-start(bf16[64,3200]{1,0:T(8,128)(2,1)S(1)} %slice_dynamic-update-slice_fusion.own), channel_id=1, source_target_pairs={{0,1},{1,0},{2,3},{3,2},{4,5},{5,4},{6,7},{7,6},{8,9},{9,8},{10,11... | collective-permute-start | bytes 1228808 | tf_op jit(solution)/shard_map/ppermute | solution.py:27
  53.3 11.1 %collective-permute-start.11 = (bf16[64,3328]{1,0:T(8,128)(2,1)S(1)}, bf16[64,3328]{1,0:T(8,128)(2,1)S(1)}, u32[]{:S(2)}, u32[]{:S(2)}) collective-permute-start(bf16[64,3328]{1,0:T(8,128)(2,1)S(1)} %get-tuple-element.14.after), channel_id=1, source_target_pairs={{0,1},{1,0},{2,3},{3,2},{4,5},{5,4},{6,7},{7,6},{8,9},{9,8},{10,11... | collective-permute-start | bytes 1277960 | tf_op jit(solution)/shard_map/ppermute | solution.py:27
  57.8 15.4 %collective-permute-start.13 = (bf16[64,3200]{1,0:T(8,128)(2,1)S(1)}, bf16[64,3200]{1,0:T(8,128)(2,1)S(1)}, u32[]{:S(2)}, u32[]{:S(2)}) collective-permute-start(bf16[64,3200]{1,0:T(8,128)(2,1)S(1)} %get-tuple-element.17), channel_id=1, source_target_pairs={{0,1},{1,0},{2,3},{3,2},{4,5},{5,4},{6,7},{7,6},{8,9},{9,8},{10,11... | collective-permute-start | bytes 1228808 | tf_op jit(solution)/shard_map/ppermute | solution.py:27
  73.4 7.0 %collective-permute-start.14 = (bf16[16,6528]{1,0:T(8,128)(2,1)S(1)}, bf16[16,6528]{1,0:T(8,128)(2,1)S(1)}, u32[]{:S(2)}, u32[]{:S(2)}) collective-permute-start(bf16[16,6528]{1,0:T(8,128)(2,1)S(1)} %pad_maximum_fusion.3), channel_id=1, source_target_pairs={{0,2},{1,3},{2,4},{3,5},{4,6},{5,7},{6,8},{7,9},{8,10},{9,11},{10,... | collective-permute-start | bytes 626696 | tf_op jit(solution)/shard_map/ppermute | solution.py:22
  73.5 10.6 %collective-permute-start.15 = (bf16[16,6528]{1,0:T(8,128)(2,1)S(1)}, bf16[16,6528]{1,0:T(8,128)(2,1)S(1)}, u32[]{:S(2)}, u32[]{:S(2)}) collective-permute-start(bf16[16,6528]{1,0:T(8,128)(2,1)S(1)} %pad_maximum_fusion.4), channel_id=1, source_target_pairs={{0,14},{1,15},{2,0},{3,1},{4,2},{5,3},{6,4},{7,5},{8,6},{9,7},{10,... | collective-permute-start | bytes 626696 | tf_op jit(solution)/shard_map/ppermute | solution.py:22
  76.3 34.5 %collective-permute-start.25 = (bf16[80,3328]{1,0:T(8,128)(2,1)S(1)}, bf16[80,3328]{1,0:T(8,128)(2,1)S(1)}, u32[]{:S(2)}, u32[]{:S(2)}) collective-permute-start(bf16[80,3328]{1,0:T(8,128)(2,1)S(1)} %get-tuple-element.19), channel_id=1, source_target_pairs={{0,240},{1,241},{2,242},{3,243},{4,244},{5,245},{6,246},{7,247},{8... | collective-permute-start | bytes 1597448 | tf_op jit(solution)/shard_map/ppermute | solution.py:37
  79.0 25.5 %collective-permute-start.20 = (bf16[64,3328]{1,0:T(8,128)(2,1)S(1)}, bf16[64,3328]{1,0:T(8,128)(2,1)S(1)}, u32[]{:S(2)}, u32[]{:S(2)}) collective-permute-start(bf16[64,3328]{1,0:T(8,128)(2,1)S(1)} %get-tuple-element.18), channel_id=1, source_target_pairs={{0,16},{1,17},{2,18},{3,19},{4,20},{5,21},{6,22},{7,23},{8,24},{9,... | collective-permute-start | bytes 1277960 | tf_op jit(solution)/shard_map/ppermute | solution.py:37
  80.1 11.5 %collective-permute-start.22 = (bf16[8,3328]{1,0:T(8,128)(2,1)S(1)}, bf16[8,3328]{1,0:T(8,128)(2,1)S(1)}, u32[]{:S(2)}, u32[]{:S(2)}) collective-permute-start(bf16[8,3328]{1,0:T(8,128)(2,1)S(1)} %slice.252), channel_id=1, source_target_pairs={{0,4},{1,5},{2,6},{3,7},{4,8},{5,9},{6,10},{7,11},{8,12},{9,13},{1... | collective-permute-start | bytes 159752 | tf_op jit(solution)/shard_map/ppermute | solution.py:22
  80.4 6.4 %collective-permute-start.18 = (bf16[8,3200]{1,0:T(8,128)(2,1)S(1)}, bf16[8,3200]{1,0:T(8,128)(2,1)S(1)}, u32[]{:S(2)}, u32[]{:S(2)}) collective-permute-start(bf16[8,3200]{1,0:T(8,128)(2,1)S(1)} %slice.253), channel_id=1, source_target_pairs={{0,12},{1,13},{2,14},{3,15},{4,0},{5,1},{6,2},{7,3},{8,4},{9,5},{1... | collective-permute-start | bytes 153608 | tf_op jit(solution)/shard_map/ppermute | solution.py:22
  86.8 8.5 %collective-permute-start.19 = (bf16[8,3200]{1,0:T(8,128)(2,1)S(1)}, bf16[8,3200]{1,0:T(8,128)(2,1)S(1)}, u32[]{:S(2)}, u32[]{:S(2)}) collective-permute-start(bf16[8,3200]{1,0:T(8,128)(2,1)S(1)} %fusion.10), channel_id=1, source_target_pairs={{0,28},{1,29},{2,30},{3,31},{4,16},{5,17},{6,18},{7,19},{8,20},{9,... | collective-permute-start | bytes 153608 | tf_op jit(solution)/shard_map/ppermute | solution.py:37
  91.4 13.0 %collective-permute-start.16 = (bf16[8,3200]{1,0:T(8,128)(2,1)S(1)}, bf16[8,3200]{1,0:T(8,128)(2,1)S(1)}, u32[]{:S(2)}, u32[]{:S(2)}) collective-permute-start(bf16[8,3200]{1,0:T(8,128)(2,1)S(1)} %slice.187), channel_id=1, source_target_pairs={{0,16},{1,17},{2,18},{3,19},{4,20},{5,21},{6,22},{7,23},{8,24},{9,... | collective-permute-start | bytes 153608 | tf_op jit(solution)/shard_map/ppermute | solution.py:37
  91.6 12.7 %collective-permute-start.17 = (bf16[8,3200]{1,0:T(8,128)(2,1)S(1)}, bf16[8,3200]{1,0:T(8,128)(2,1)S(1)}, u32[]{:S(2)}, u32[]{:S(2)}) collective-permute-start(bf16[8,3200]{1,0:T(8,128)(2,1)S(1)} %slice.254), channel_id=1, source_target_pairs={{0,20},{1,21},{2,22},{3,23},{4,24},{5,25},{6,26},{7,27},{8,28},{9,... | collective-permute-start | bytes 153608 | tf_op jit(solution)/shard_map/ppermute | solution.py:37
  95.4 10.6 %collective-permute-start.23 = (bf16[8,3328]{1,0:T(8,128)(2,1)S(1)}, bf16[8,3328]{1,0:T(8,128)(2,1)S(1)}, u32[]{:S(2)}, u32[]{:S(2)}) collective-permute-start(bf16[8,3328]{1,0:T(8,128)(2,1)S(1)} %fusion.9), channel_id=1, source_target_pairs={{0,244},{1,245},{2,246},{3,247},{4,248},{5,249},{6,250},{7,251},{8... | collective-permute-start | bytes 159752 | tf_op jit(solution)/shard_map/ppermute | solution.py:37
  104.3 3.9 %collective-permute-start.21 = (bf16[8,3328]{1,0:T(8,128)(2,1)S(1)}, bf16[8,3328]{1,0:T(8,128)(2,1)S(1)}, u32[]{:S(2)}, u32[]{:S(2)}) collective-permute-start(bf16[8,3328]{1,0:T(8,128)(2,1)S(1)} %slice.197), channel_id=1, source_target_pairs={{0,240},{1,241},{2,242},{3,243},{4,244},{5,245},{6,246},{7,247},{8... | collective-permute-start | bytes 159752 | tf_op jit(solution)/shard_map/ppermute | solution.py:37
  104.3 6.3 %collective-permute-start.24 = (bf16[8,3328]{1,0:T(8,128)(2,1)S(1)}, bf16[8,3328]{1,0:T(8,128)(2,1)S(1)}, u32[]{:S(2)}, u32[]{:S(2)}) collective-permute-start(bf16[8,3328]{1,0:T(8,128)(2,1)S(1)} %slice.251), channel_id=1, source_target_pairs={{0,252},{1,253},{2,254},{3,255},{4,240},{5,241},{6,242},{7,243},{8... | collective-permute-start | bytes 159752 | tf_op jit(solution)/shard_map/ppermute | solution.py:37

commit v4 on v3

--- a/solution.py
+++ b/solution.py
@@ -106,20 +106,38 @@
     ).astype(jnp.bfloat16)
 
 
+def fetched_head_kernel(capacity, f_len, b_len, *refs):
+    count = 7
+    sources, outs, held, arrived = refs[:count], refs[count : count + 3], refs[count + 3 : -1], refs[-1]
+    copies = [
+        pltpu.make_async_copy(source, target, arrived.at[at])
+        for at, (source, target) in enumerate(zip(sources, held))
+    ]
+    for copy in copies:
+        copy.start()
+    for copy in copies:
+        copy.wait()
+    f_ids, b_ids, *tokens = held
+    head_kernel(capacity, f_ids, b_ids, f_len, b_len, *tokens, *outs)
+
+
 def head(capacity, f_ids, b_ids, f_len, b_len, f_in, b_in, grad, gain, router):
     tok_count, width = f_in.shape
+    sources = (f_ids, b_ids, f_in, b_in, grad, gain, router)
     return pl.pallas_call(
-        lambda *refs: head_kernel(capacity, *refs),
+        lambda *refs: fetched_head_kernel(capacity, *refs),
         out_shape=(
             jax.ShapeDtypeStruct((3 * capacity, width), jnp.bfloat16),
             jax.ShapeDtypeStruct((tok_count, width + LANES), jnp.bfloat16),
             jax.ShapeDtypeStruct((tok_count + 2 * capacity, width + LANES), jnp.bfloat16),
         ),
-        in_specs=[VMEM, VMEM, SMEM, SMEM] + [VMEM] * 5,
+        in_specs=[SMEM, SMEM] + [pl.BlockSpec(memory_space=pl.ANY)] * len(sources),
         out_specs=(VMEM,) * 3,
-        compiler_params=pltpu.CompilerParams(vmem_limit_bytes=8 * 1024 * 1024),
+        scratch_shapes=[pltpu.VMEM(source.shape, source.dtype) for source in sources]
+        + [pltpu.SemaphoreType.DMA((len(sources),))],
+        compiler_params=pltpu.CompilerParams(vmem_limit_bytes=56 * 1024 * 1024),
         name="head",
-    )(f_ids, b_ids, f_len, b_len, f_in, b_in, grad, gain, router)
+    )(f_len, b_len, *sources)
 
 
 def sigmoid(value):
@@ -217,20 +235,21 @@
 
 
 def hold(after, weights):
-    def kernel(after, gate_w, up_w, down_w, held):
+    def kernel(*refs):
+        held = refs[-1]
         held[...] = jnp.zeros_like(held)
 
     return pl.pallas_call(
         kernel,
         out_shape=jax.ShapeDtypeStruct((8, LANES), jnp.float32),
-        in_specs=[pl.BlockSpec(memory_space=pl.ANY)] + [VMEM] * 3,
+        in_specs=[pl.BlockSpec(memory_space=pl.ANY)] * len(after) + [VMEM] * 3,
         out_specs=VMEM,
         compiler_params=pltpu.CompilerParams(vmem_limit_bytes=2 * 1024 * 1024),
         cost_estimate=pl.CostEstimate(
             flops=0, bytes_accessed=6 * weights[0].shape[0] * weights[0].shape[1], transcendentals=0
         ),
         name="hold",
-    )(after, *weights)
+    )(*after, *weights)
 
 
 def forward_expert(own, other, after, weights):
@@ -322,7 +341,7 @@
     far_low = along_z(below2[:, :half], 2)
     far_high = along_z(above2[:, half:], -2)
     far = jnp.concatenate([far_low, far_high], axis=1)
-    return [own], [below1, above1, below2, above2], [below3, above3, far]
+    return [own], [below1, above1], [below2, above2], [below3, above3, far]
 
 
 def sum_columns(b_total, f_total, capacity):
@@ -332,17 +351,16 @@
     own, below1, above1, below2, above2, below3, above3, far = [
         total[at * capacity : (at + 1) * capacity] for at in range(total.shape[0] // capacity)
     ]
-    up = along_z(jnp.concatenate([above1, above3], axis=0).astype(low), 1).astype(full)
-    down = along_z(jnp.concatenate([below1, below3], axis=0).astype(low), -1).astype(full)
-    far_b = along_z(far[:, :width].astype(low), 2).astype(full)
-    far_f = along_z(far[:, width:].astype(low), -2).astype(full)
-    above2 = above2 + up[capacity:]
-    below2 = below2 + down[capacity:]
-    near = own + up[:capacity] + down[:capacity]
-    b_up = across((above2[:, :width] + far_b).astype(low), -1, 2)
-    b_down = across(below2[:, :width].astype(low), -1, -2)
-    f_up = across(above2[:, width:].astype(low), 1, 2)
-    f_down = across((below2[:, width:] + far_f).astype(low), 1, -2)
+    both = total.shape[1]
+    up = along_z(jnp.concatenate([above1, below2, far[:, :width]], axis=1).astype(low), 1).astype(full)
+    down = along_z(jnp.concatenate([below1, above2, far[:, width:]], axis=1).astype(low), -1).astype(full)
+    near = own + up[:, :both] + down[:, :both]
+    above3 = above3 + down[:, both : 2 * both]
+    below3 = below3 + up[:, both : 2 * both]
+    b_up = across((above3[:, :width] + up[:, 2 * both :]).astype(low), -1, 3)
+    b_down = across(below3[:, :width].astype(low), -1, -3)
+    f_up = across(above3[:, width:].astype(low), 1, 3)
+    f_down = across((below3[:, width:] + down[:, 2 * both :]).astype(low), 1, -3)
     b_near = across(near[:, :width].astype(low), -1, 0)
     f_near = across(near[:, width:].astype(low), 1, 0)
 
@@ -375,15 +393,26 @@
     )
     f_pack = across(f_pack, 1, 0)
     b_pack = across(b_pack, -1, 0)
-    own, near, far = gather_column(rows)
+    column = gather_column(rows)
+    other = swap_x(rows)
+    other_near = [along_z(other, 1), along_z(other, -1)]
     pair = 2 * capacity
-    groups = [jnp.concatenate([block[:pair] for block in group], axis=0) for group in (own, near, far)]
-    f_own = jnp.concatenate([block[pair:] for block in own + near + far], axis=0)
-    others = [swap_x(group) for group in groups]
-    f_own, others[2] = lax.optimization_barrier((f_own, others[2]))
-    f_other = swap_x(f_own)
-
-    b_mine, b_theirs = backward_expert(capacity, groups + others, hold(groups[2], weights), weights)
+
+    def of_backward(blocks):
+        return jnp.concatenate([block[:pair] for block in blocks], axis=0)
+
+    def of_forward(blocks):
+        return jnp.concatenate([block[pair:] for block in blocks], axis=0)
+
+    own, near, two, far = column
+    groups = [of_backward(blocks) for blocks in column]
+    others = [of_backward([other]), of_backward(other_near), swap_x(groups[2]), swap_x(groups[3])]
+    f_own = of_forward(own + near + two + far)
+    loaded = hold((groups[3],), weights)
+    f_rest, others[3], loaded = lax.optimization_barrier((of_forward(two + far), others[3], loaded))
+    f_other = jnp.concatenate([of_forward([other] + other_near), swap_x(f_rest)], axis=0)
+
+    b_mine, b_theirs = backward_expert(capacity, groups + others, loaded, weights)
     f_mine, f_theirs = forward_expert(f_own, f_other, b_theirs, weights)
     b_total = b_mine + swap_x(b_theirs).astype(jnp.float32)
     f_total = f_mine + swap_x(f_theirs).astype(jnp.float32)

time: 113 us -> 104 us (0.920)
  the two profiles are of different devices: /device:TPU:1 before, /device:TPU:89 now
where the time goes in v4:
time: 104 us
  starting transfers between devices  47.1 us (45%)
  waiting for transfers between devices  30.6 us (29%)
  Pallas kernels  15.5 us (15%)
  local copies, waits for them, and re-layouts  7.43 us (7%)
  between operations  2.34 us (2%)
    ppermute x8, starting transfers between devices, across(): return lax.ppermute(value, ('pipe', 'dp'), pairs)  22.5 us
    ppermute x12, starting transfers between devices, along_z(): return lax.ppermute(value, 'dp', pairs)  18.7 us
    ppermute x6, waiting for transfers between devices, swap_x(): lax.ppermute(value, 'dp', [(source, source ^ 1) for source in range(count)])  13.9 us
    ppermute x8, waiting for transfers between devices, across(): return lax.ppermute(value, ('pipe', 'dp'), pairs)  10.3 us
    pallas_call x2, Pallas kernels, expert_call(): pl.pallas_call(kernel, out_shape=(jax.ShapeDtypeStruct((half, width + ext...  9.72 us
    ppermute x12, waiting for transfers between devices, along_z(): return lax.ppermute(value, 'dp', pairs)  6.49 us
    unnamed x22, local copies, waits for them, and re-layouts  6.31 us
    ppermute x6, starting transfers between devices, swap_x(): lax.ppermute(value, 'dp', [(source, source ^ 1) for source in range(count)])  5.96 us
  transfers between devices with their start and end apart: 26, of which 10 were waited for; matrix products, arithmetic and copies ran while one was open for 2% of the time, Pallas kernels for 11%

profile of v4, /device:TPU:89, one launch (start us, length us, event | category | flops | bytes accessed | tf_op | source)
XLA Modules:
  0.0 103.7 jit_solution(18044355250500849447)
XLA Ops:
  1.9 3.0 %head.1 = (bf16[24,3200]{1,0:T(8,128)(2,1)}, bf16[64,3328]{1,0:T(8,128)(2,1)}, bf16[80,3328]{1,0:T(8,128)(2,1)}) custom-call(s32[1,1]{1,0:T(1,128)S(6)} %copy.26.refs_0_, s32[1,1]{1,0:T(1,128)S(6)} %copy.27.refs_1_, s32[1,64]{1,0:T(1,128)} %refs_2_.1, s32[1,64]{1,0:T(1,128)} %refs_3_.1, bf16[64,3200]{1,0:T(8,128)(2,1)} %bitcast.23, ...), custom_call_target="tpu_custom_call" | custom-call | tf_op jit(solution)/shard_map/head/pallas_call | solution.py:127
  5.0 4.3 %collective-permute-start.2 = (bf16[24,3200]{1,0:T(8,128)(2,1)}, bf16[24,3200]{1,0:T(8,128)(2,1)S(1)}, u32[]{:S(2)}, u32[]{:S(2)}) collective-permute-start(bf16[24,3200]{1,0:T(8,128)(2,1)} %get-tuple-element.12), channel_id=1, source_target_pairs={{0,4},{1,5},{2,6},{3,7},{4,8},{5,9},{6,10},{7,11},{8,12},{9,13},{1... | collective-permute-start | bytes 460808 | tf_op jit(solution)/shard_map/ppermute | solution.py:22
  9.3 0.7 collective-permute-start
  10.0 0.7 collective-permute-start.1
  10.7 1.2 %collective-permute-start.8 = (bf16[24,3200]{1,0:T(8,128)(2,1)}, bf16[24,3200]{1,0:T(8,128)(2,1)S(1)}, u32[]{:S(2)}, u32[]{:S(2)}) collective-permute-start(bf16[24,3200]{1,0:T(8,128)(2,1)} %get-tuple-element.12), channel_id=1, source_target_pairs={{0,1},{1,0},{2,3},{3,2},{4,5},{5,4},{6,7},{7,6},{8,9},{9,8},{10,11... | collective-permute-start | bytes 460808 | tf_op jit(solution)/shard_map/ppermute | solution.py:27
  11.9 0.8 slice_dynamic-update-slice_fusion.2
  12.8 0.9 slice.155.refs_0_
  13.7 2.5 %collective-permute-done.2 = bf16[24,3200]{1,0:T(8,128)(2,1)S(1)} collective-permute-done((bf16[24,3200]{1,0:T(8,128)(2,1)}, bf16[24,3200]{1,0:T(8,128)(2,1)S(1)}, u32[]{:S(2)}, u32[]{:S(2)}) %collective-permute-start.2) | collective-permute-done | bytes 153632 | tf_op jit(solution)/shard_map/ppermute | solution.py:22
  16.2 4.2 %collective-permute-start.6 = (bf16[24,1536]{1,0:T(8,128)(2,1)S(1)}, bf16[24,1536]{1,0:T(8,128)(2,1)S(1)}, u32[]{:S(2)}, u32[]{:S(2)}) collective-permute-start(bf16[24,1536]{1,0:T(8,128)(2,1)S(1)} %slice.206), channel_id=1, source_target_pairs={{0,4},{1,5},{2,6},{3,7},{4,8},{5,9},{6,10},{7,11},{8,12},{9,13},{1... | collective-permute-start | bytes 221192 | tf_op jit(solution)/shard_map/ppermute | solution.py:22
  20.4 0.8 collective-permute-done.3
  21.1 0.4 collective-permute-start.7
  21.6 1.3 %collective-permute-start.11 = (bf16[32,3200]{1,0:T(8,128)(2,1)S(1)}, bf16[32,3200]{1,0:T(8,128)(2,1)S(1)}, u32[]{:S(2)}, u32[]{:S(2)}) collective-permute-start(bf16[32,3200]{1,0:T(8,128)(2,1)S(1)} %pad_maximum_fusion.6.refs_2_), channel_id=1, source_target_pairs={{0,1},{1,0},{2,3},{3,2},{4,5},{5,4},{6,7},{7,6},{8,9},{9,8},{10,11... | collective-permute-start | bytes 614408 | tf_op jit(solution)/shard_map/ppermute | solution.py:27
  22.9 1.0 collective-permute-start.4
  24.0 0.6 collective-permute-start.5
  24.7 0.6 collective-permute-start.10
  25.3 1.4 %collective-permute-done.7 = bf16[24,1664]{1,0:T(8,128)(2,1)S(1)} collective-permute-done((bf16[24,1664]{1,0:T(8,128)(2,1)S(1)}, bf16[24,1664]{1,0:T(8,128)(2,1)S(1)}, u32[]{:S(2)}, u32[]{:S(2)}) %collective-permute-start.7) | collective-permute-done | bytes 79904 | tf_op jit(solution)/shard_map/ppermute | solution.py:22
  26.7 1.1 %collective-permute-start.9 = (bf16[24,3200]{1,0:T(8,128)(2,1)S(1)}, bf16[24,3200]{1,0:T(8,128)(2,1)S(1)}, u32[]{:S(2)}, u32[]{:S(2)}) collective-permute-start(bf16[24,3200]{1,0:T(8,128)(2,1)S(1)} %collective-permute-done.8), channel_id=1, source_target_pairs={{0,2},{1,3},{2,4},{3,5},{4,6},{5,7},{6,8},{7,9},{8,10},{9,11},{10,... | collective-permute-start | bytes 460808 | tf_op jit(solution)/shard_map/ppermute | solution.py:22
  27.8 1.8 %collective-permute-done.5 = bf16[24,3200]{1,0:T(8,128)(2,1)S(1)} collective-permute-done((bf16[24,3200]{1,0:T(8,128)(2,1)S(1)}, bf16[24,3200]{1,0:T(8,128)(2,1)S(1)}, u32[]{:S(2)}, u32[]{:S(2)}) %collective-permute-start.5) | collective-permute-done | bytes 153632 | tf_op jit(solution)/shard_map/ppermute | solution.py:22
  29.7 1.0 collective-permute-start.12
  30.7 2.0 %copy-done.1 = bf16[1,3200,576]{1,2,0:T(8,128)(2,1)S(1)} copy-done((bf16[1,3200,576]{1,2,0:T(8,128)(2,1)S(1)}, bf16[1,3200,576]{1,2,0:T(8,128)(2,1)}, u32[]{:S(2)}) %copy-start.1) | copy-done | bytes 3686424
  32.8 2.0 %copy-done.3 = bf16[1,576,3200]{2,1,0:T(8,128)(2,1)S(1)} copy-done((bf16[1,576,3200]{2,1,0:T(8,128)(2,1)S(1)}, bf16[1,576,3200]{2,1,0:T(8,128)(2,1)}, u32[]{:S(2)}) %copy-start.3) | copy-done | bytes 3686424
  34.9 0.9 collective-permute-done.12.refs_7_
  35.8 0.8 collective-permute-start.14
  36.7 0.2 copy-done.2
  36.9 1.1 %copy-done.4 = bf16[1,576,3200]{2,1,0:T(8,128)(2,1)S(1)} copy-done((bf16[1,576,3200]{2,1,0:T(8,128)(2,1)S(1)}, bf16[1,576,3200]{2,1,0:T(8,128)(2,1)}, u32[]{:S(2)}) %copy-start.4) | copy-done | bytes 3686424
  38.0 6.3 %backward_expert.1 = (f32[64,3328]{1,0:T(8,128)S(1)}, bf16[64,3328]{1,0:T(8,128)(2,1)S(1)}) custom-call(bf16[16,3200]{1,0:T(8,128)(2,1)S(1)} %slice.155.refs_0_, bf16[32,3200]{1,0:T(8,128)(2,1)S(1)} %pad_maximum_fusion.5.refs_1_, bf16[32,3200]{1,0:T(8,128)(2,1)S(1)} %pad_maximum_fusion.6.refs_2_, bf16[48,3200]{1,0:T(8,128)(2,1)S(1)} %pad_maximum_fusion.2.refs_0_.refs_3_, ...), custom_call_target="tpu_custom_call" | custom-call | flops 2359296000 | bytes 11059200 | tf_op jit(solution)/shard_map/backward_expert/pallas_call | solution.py:219
  44.3 0.7 collective-permute-start.13
  45.0 3.4 %forward_expert.1 = (f32[64,3200]{1,0:T(8,128)S(1)}, bf16[64,3200]{1,0:T(8,128)(2,1)S(1)}) custom-call(bf16[64,3200]{1,0:T(8,128)(2,1)S(1)} %get-tuple-element.30.own, bf16[64,3200]{1,0:T(8,128)(2,1)S(1)} %pad_maximum_fusion.1.other, bf16[64,3328]{1,0:T(8,128)(2,1)S(1)} %get-tuple-element.16.after, bf16[576,3200]{1,0:T(8,128)(2,1)S(1)} %bitcast.14, ...), custom_call_target="tpu_custom_call" | custom-call | flops 1415577600 | bytes 11059200 | tf_op jit(solution)/shard_map/forward_expert/pallas_call | solution.py:219
  48.4 1.0 collective-permute-start.15
  49.4 4.7 %collective-permute-done.13 = bf16[64,3328]{1,0:T(8,128)(2,1)S(1)} collective-permute-done((bf16[64,3328]{1,0:T(8,128)(2,1)S(1)}, bf16[64,3328]{1,0:T(8,128)(2,1)S(1)}, u32[]{:S(2)}, u32[]{:S(2)}) %collective-permute-start.13) | collective-permute-done | bytes 426016 | tf_op jit(solution)/shard_map/ppermute | solution.py:27
  54.2 8.3 %collective-permute-done.15 = bf16[64,3200]{1,0:T(8,128)(2,1)S(1)} collective-permute-done((bf16[64,3200]{1,0:T(8,128)(2,1)S(1)}, bf16[64,3200]{1,0:T(8,128)(2,1)S(1)}, u32[]{:S(2)}, u32[]{:S(2)}) %collective-permute-start.15) | collective-permute-done | bytes 409632 | tf_op jit(solution)/shard_map/ppermute | solution.py:27
  62.4 0.1 convert_add_fusion.1
  62.6 0.1 fusion
  62.7 4.9 %collective-permute-start.16 = (bf16[8,16384]{1,0:T(8,128)(2,1)S(1)}, bf16[8,16384]{1,0:T(8,128)(2,1)S(1)}, u32[]{:S(2)}, u32[]{:S(2)}) collective-permute-start(bf16[8,16384]{1,0:T(8,128)(2,1)S(1)} %pad_maximum_fusion.3), channel_id=1, source_target_pairs={{0,2},{1,3},{2,4},{3,5},{4,6},{5,7},{6,8},{7,9},{8,10},{9,11},{10,... | collective-permute-start | bytes 786440 | tf_op jit(solution)/shard_map/ppermute | solution.py:22
  67.7 0.1 collective-permute-start.17
  67.8 6.5 %collective-permute-start.21 = (bf16[64,3328]{1,0:T(8,128)(2,1)S(1)}, bf16[64,3328]{1,0:T(8,128)(2,1)S(1)}, u32[]{:S(2)}, u32[]{:S(2)}) collective-permute-start(bf16[64,3328]{1,0:T(8,128)(2,1)S(1)} %copy-done.6), channel_id=1, source_target_pairs={{0,16},{1,17},{2,18},{3,19},{4,20},{5,21},{6,22},{7,23},{8,24},{9,... | collective-permute-start | bytes 1277960 | tf_op jit(solution)/shard_map/ppermute | solution.py:37
  74.4 0.1 fusion.4
  74.5 6.2 %collective-permute-start.20 = (bf16[8,3200]{1,0:T(8,128)(2,1)S(1)}, bf16[8,3200]{1,0:T(8,128)(2,1)S(1)}, u32[]{:S(2)}, u32[]{:S(2)}) collective-permute-start(bf16[8,3200]{1,0:T(8,128)(2,1)S(1)} %fusion.10), channel_id=1, source_target_pairs={{0,26},{1,27},{2,28},{3,29},{4,30},{5,31},{6,16},{7,17},{8,18},{9,... | collective-permute-start | bytes 153608 | tf_op jit(solution)/shard_map/ppermute | solution.py:37
  80.7 0.3 collective-permute-start.19
  81.0 5.9 %collective-permute-start.18 = (bf16[8,3200]{1,0:T(8,128)(2,1)S(1)}, bf16[8,3200]{1,0:T(8,128)(2,1)S(1)}, u32[]{:S(2)}, u32[]{:S(2)}) collective-permute-start(bf16[8,3200]{1,0:T(8,128)(2,1)S(1)} %slice.232), channel_id=1, source_target_pairs={{0,16},{1,17},{2,18},{3,19},{4,20},{5,21},{6,22},{7,23},{8,24},{9,... | collective-permute-start | bytes 153608 | tf_op jit(solution)/shard_map/ppermute | solution.py:37
  86.9 0.9 collective-permute-start.24
  87.8 1.4 %collective-permute-done.19 = bf16[8,3200]{1,0:T(8,128)(2,1)S(1)} collective-permute-done((bf16[8,3200]{1,0:T(8,128)(2,1)S(1)}, bf16[8,3200]{1,0:T(8,128)(2,1)S(1)}, u32[]{:S(2)}, u32[]{:S(2)}) %collective-permute-start.19) | collective-permute-done | bytes 51232 | tf_op jit(solution)/shard_map/ppermute | solution.py:37
  89.2 2.4 %collective-permute-start.23 = (bf16[8,3328]{1,0:T(8,128)(2,1)S(1)}, bf16[8,3328]{1,0:T(8,128)(2,1)S(1)}, u32[]{:S(2)}, u32[]{:S(2)}) collective-permute-start(bf16[8,3328]{1,0:T(8,128)(2,1)S(1)} %fusion.9), channel_id=1, source_target_pairs={{0,246},{1,247},{2,248},{3,249},{4,250},{5,251},{6,252},{7,253},{8... | collective-permute-start | bytes 159752 | tf_op jit(solution)/shard_map/ppermute | solution.py:37
  91.7 0.4 collective-permute-start.22
  92.1 1.3 %forward_finish.1 = bf16[64,3200]{1,0:T(8,128)(2,1)} custom-call(f32[8,3200]{1,0:T(8,128)S(1)} %convert_add_fusion.3.refs_0_, bf16[64,3328]{1,0:T(8,128)(2,1)S(1)} %collective-permute-done.21.refs_1_), custom_call_target="tpu_custom_call" | custom-call | tf_op jit(solution)/shard_map/forward_finish/pallas_call | solution.py:323
  93.4 4.9 %collective-permute-done.24 = bf16[8,3328]{1,0:T(8,128)(2,1)S(1)} collective-permute-done((bf16[8,3328]{1,0:T(8,128)(2,1)S(1)}, bf16[8,3328]{1,0:T(8,128)(2,1)S(1)}, u32[]{:S(2)}, u32[]{:S(2)}) %collective-permute-start.24) | collective-permute-done | bytes 53280 | tf_op jit(solution)/shard_map/ppermute | solution.py:37
  98.3 3.9 %collective-permute-done.23 = bf16[8,3328]{1,0:T(8,128)(2,1)S(1)} collective-permute-done((bf16[8,3328]{1,0:T(8,128)(2,1)S(1)}, bf16[8,3328]{1,0:T(8,128)(2,1)S(1)}, u32[]{:S(2)}, u32[]{:S(2)}) %collective-permute-start.23) | collective-permute-done | bytes 53280 | tf_op jit(solution)/shard_map/ppermute | solution.py:37
  102.2 1.4 %backward_finish.1 = bf16[64,3200]{1,0:T(8,128)(2,1)} custom-call(f32[8,3328]{1,0:T(8,128)S(1)} %convert_add_fusion.2.refs_0_, bf16[80,3328]{1,0:T(8,128)(2,1)S(1)} %collective-permute-done.25.refs_1_), custom_call_target="tpu_custom_call" | custom-call | tf_op jit(solution)/shard_map/backward_finish/pallas_call | solution.py:323
  (74 shorter events, 0.7 us)
Async XLA Ops:
  5.0 11.2 %collective-permute-start.2 = (bf16[24,3200]{1,0:T(8,128)(2,1)}, bf16[24,3200]{1,0:T(8,128)(2,1)S(1)}, u32[]{:S(2)}, u32[]{:S(2)}) collective-permute-start(bf16[24,3200]{1,0:T(8,128)(2,1)} %get-tuple-element.12), channel_id=1, source_target_pairs={{0,4},{1,5},{2,6},{3,7},{4,8},{5,9},{6,10},{7,11},{8,12},{9,13},{1... | collective-permute-start | bytes 460808 | tf_op jit(solution)/shard_map/ppermute | solution.py:22
  9.3 12.3 %collective-permute-start = (bf16[24,3200]{1,0:T(8,128)(2,1)}, bf16[24,3200]{1,0:T(8,128)(2,1)S(1)}, u32[]{:S(2)}, u32[]{:S(2)}) collective-permute-start(bf16[24,3200]{1,0:T(8,128)(2,1)} %get-tuple-element.12), channel_id=1, source_target_pairs={{0,2},{1,3},{2,4},{3,5},{4,6},{5,7},{6,8},{7,9},{8,10},{9,11},{10,... | collective-permute-start | bytes 460808 | tf_op jit(solution)/shard_map/ppermute | solution.py:22
  10.0 12.9 %collective-permute-start.1 = (bf16[24,3200]{1,0:T(8,128)(2,1)}, bf16[24,3200]{1,0:T(8,128)(2,1)S(1)}, u32[]{:S(2)}, u32[]{:S(2)}) collective-permute-start(bf16[24,3200]{1,0:T(8,128)(2,1)} %get-tuple-element.12), channel_id=1, source_target_pairs={{0,14},{1,15},{2,0},{3,1},{4,2},{5,3},{6,4},{7,5},{8,6},{9,7},{10,... | collective-permute-start | bytes 460808 | tf_op jit(solution)/shard_map/ppermute | solution.py:22
  10.7 10.4 %collective-permute-start.3 = (bf16[24,3200]{1,0:T(8,128)(2,1)}, bf16[24,3200]{1,0:T(8,128)(2,1)S(1)}, u32[]{:S(2)}, u32[]{:S(2)}) collective-permute-start(bf16[24,3200]{1,0:T(8,128)(2,1)} %get-tuple-element.12), channel_id=1, source_target_pairs={{0,12},{1,13},{2,14},{3,15},{4,0},{5,1},{6,2},{7,3},{8,4},{9,5},{1... | collective-permute-start | bytes 460808 | tf_op jit(solution)/shard_map/ppermute | solution.py:22
  10.7 13.3 %collective-permute-start.8 = (bf16[24,3200]{1,0:T(8,128)(2,1)}, bf16[24,3200]{1,0:T(8,128)(2,1)S(1)}, u32[]{:S(2)}, u32[]{:S(2)}) collective-permute-start(bf16[24,3200]{1,0:T(8,128)(2,1)} %get-tuple-element.12), channel_id=1, source_target_pairs={{0,1},{1,0},{2,3},{3,2},{4,5},{5,4},{6,7},{7,6},{8,9},{9,8},{10,11... | collective-permute-start | bytes 460808 | tf_op jit(solution)/shard_map/ppermute | solution.py:27
  16.2 8.5 %collective-permute-start.6 = (bf16[24,1536]{1,0:T(8,128)(2,1)S(1)}, bf16[24,1536]{1,0:T(8,128)(2,1)S(1)}, u32[]{:S(2)}, u32[]{:S(2)}) collective-permute-start(bf16[24,1536]{1,0:T(8,128)(2,1)S(1)} %slice.206), channel_id=1, source_target_pairs={{0,4},{1,5},{2,6},{3,7},{4,8},{5,9},{6,10},{7,11},{8,12},{9,13},{1... | collective-permute-start | bytes 221192 | tf_op jit(solution)/shard_map/ppermute | solution.py:22
  21.1 5.6 %collective-permute-start.7 = (bf16[24,1664]{1,0:T(8,128)(2,1)S(1)}, bf16[24,1664]{1,0:T(8,128)(2,1)S(1)}, u32[]{:S(2)}, u32[]{:S(2)}) collective-permute-start(bf16[24,1664]{1,0:T(8,128)(2,1)S(1)} %slice.207), channel_id=1, source_target_pairs={{0,12},{1,13},{2,14},{3,15},{4,0},{5,1},{6,2},{7,3},{8,4},{9,5},{1... | collective-permute-start | bytes 239624 | tf_op jit(solution)/shard_map/ppermute | solution.py:22
  21.5 9.2 %copy-start = (bf16[1,3200,576]{1,2,0:T(8,128)(2,1)S(1)}, bf16[1,3200,576]{1,2,0:T(8,128)(2,1)}, u32[]{:S(2)}) copy-start(bf16[1,3200,576]{1,2,0:T(8,128)(2,1)} %param.21) | copy-start | bytes 11059204
  21.6 15.1 %collective-permute-start.11 = (bf16[32,3200]{1,0:T(8,128)(2,1)S(1)}, bf16[32,3200]{1,0:T(8,128)(2,1)S(1)}, u32[]{:S(2)}, u32[]{:S(2)}) collective-permute-start(bf16[32,3200]{1,0:T(8,128)(2,1)S(1)} %pad_maximum_fusion.6.refs_2_), channel_id=1, source_target_pairs={{0,1},{1,0},{2,3},{3,2},{4,5},{5,4},{6,7},{7,6},{8,9},{9,8},{10,11... | collective-permute-start | bytes 614408 | tf_op jit(solution)/shard_map/ppermute | solution.py:27
  22.9 6.7 %collective-permute-start.4 = (bf16[24,3200]{1,0:T(8,128)(2,1)S(1)}, bf16[24,3200]{1,0:T(8,128)(2,1)S(1)}, u32[]{:S(2)}, u32[]{:S(2)}) collective-permute-start(bf16[24,3200]{1,0:T(8,128)(2,1)S(1)} %collective-permute-done.2), channel_id=1, source_target_pairs={{0,2},{1,3},{2,4},{3,5},{4,6},{5,7},{6,8},{7,9},{8,10},{9,11},{10,... | collective-permute-start | bytes 460808 | tf_op jit(solution)/shard_map/ppermute | solution.py:22
  24.0 5.6 %collective-permute-start.5 = (bf16[24,3200]{1,0:T(8,128)(2,1)S(1)}, bf16[24,3200]{1,0:T(8,128)(2,1)S(1)}, u32[]{:S(2)}, u32[]{:S(2)}) collective-permute-start(bf16[24,3200]{1,0:T(8,128)(2,1)S(1)} %collective-permute-done.3), channel_id=1, source_target_pairs={{0,14},{1,15},{2,0},{3,1},{4,2},{5,3},{6,4},{7,5},{8,6},{9,7},{10,... | collective-permute-start | bytes 460808 | tf_op jit(solution)/shard_map/ppermute | solution.py:22
  24.7 10.2 %collective-permute-start.10 = (bf16[24,3200]{1,0:T(8,128)(2,1)S(1)}, bf16[24,3200]{1,0:T(8,128)(2,1)S(1)}, u32[]{:S(2)}, u32[]{:S(2)}) collective-permute-start(bf16[24,3200]{1,0:T(8,128)(2,1)S(1)} %collective-permute-done.8), channel_id=1, source_target_pairs={{0,14},{1,15},{2,0},{3,1},{4,2},{5,3},{6,4},{7,5},{8,6},{9,7},{10,... | collective-permute-start | bytes 460808 | tf_op jit(solution)/shard_map/ppermute | solution.py:22
  26.7 8.1 %collective-permute-start.9 = (bf16[24,3200]{1,0:T(8,128)(2,1)S(1)}, bf16[24,3200]{1,0:T(8,128)(2,1)S(1)}, u32[]{:S(2)}, u32[]{:S(2)}) collective-permute-start(bf16[24,3200]{1,0:T(8,128)(2,1)S(1)} %collective-permute-done.8), channel_id=1, source_target_pairs={{0,2},{1,3},{2,4},{3,5},{4,6},{5,7},{6,8},{7,9},{8,10},{9,11},{10,... | collective-permute-start | bytes 460808 | tf_op jit(solution)/shard_map/ppermute | solution.py:22
  29.7 6.1 %collective-permute-start.12 = (bf16[48,3200]{1,0:T(8,128)(2,1)S(1)}, bf16[48,3200]{1,0:T(8,128)(2,1)S(1)}, u32[]{:S(2)}, u32[]{:S(2)}) collective-permute-start(bf16[48,3200]{1,0:T(8,128)(2,1)S(1)} %pad_maximum_fusion.2.refs_0_.refs_3_), channel_id=1, source_target_pairs={{0,1},{1,0},{2,3},{3,2},{4,5},{5,4},{6,7},{7,6},{8,9},{9,8},{10,11... | collective-permute-start | bytes 921608 | tf_op jit(solution)/shard_map/ppermute | solution.py:27
  30.7 2.0 %copy-start.1 = (bf16[1,3200,576]{1,2,0:T(8,128)(2,1)S(1)}, bf16[1,3200,576]{1,2,0:T(8,128)(2,1)}, u32[]{:S(2)}) copy-start(bf16[1,3200,576]{1,2,0:T(8,128)(2,1)} %param.22) | copy-start | bytes 11059204
  32.8 2.0 %copy-start.3 = (bf16[1,576,3200]{2,1,0:T(8,128)(2,1)S(1)}, bf16[1,576,3200]{2,1,0:T(8,128)(2,1)}, u32[]{:S(2)}) copy-start(bf16[1,576,3200]{2,1,0:T(8,128)(2,1)} %param.23) | copy-start | bytes 11059204
  34.8 2.0 %copy-start.2 = (bf16[1,3200,576]{1,2,0:T(8,128)(2,1)S(1)}, bf16[1,3200,576]{1,2,0:T(8,128)(2,1)}, u32[]{:S(2)}) copy-start(bf16[1,3200,576]{1,2,0:T(8,128)(2,1)} %param.22) | copy-start | bytes 11059204
  34.8 3.2 %copy-start.4 = (bf16[1,576,3200]{2,1,0:T(8,128)(2,1)S(1)}, bf16[1,576,3200]{2,1,0:T(8,128)(2,1)}, u32[]{:S(2)}) copy-start(bf16[1,576,3200]{2,1,0:T(8,128)(2,1)} %param.23) | copy-start | bytes 11059204
  35.8 9.2 %collective-permute-start.14 = (bf16[40,3200]{1,0:T(8,128)(2,1)S(1)}, bf16[40,3200]{1,0:T(8,128)(2,1)S(1)}, u32[]{:S(2)}, u32[]{:S(2)}) collective-permute-start(bf16[40,3200]{1,0:T(8,128)(2,1)S(1)} %get-tuple-element.17), channel_id=1, source_target_pairs={{0,1},{1,0},{2,3},{3,2},{4,5},{5,4},{6,7},{7,6},{8,9},{9,8},{10,11... | collective-permute-start | bytes 768008 | tf_op jit(solution)/shard_map/ppermute | solution.py:27
  44.3 9.8 %collective-permute-start.13 = (bf16[64,3328]{1,0:T(8,128)(2,1)S(1)}, bf16[64,3328]{1,0:T(8,128)(2,1)S(1)}, u32[]{:S(2)}, u32[]{:S(2)}) collective-permute-start(bf16[64,3328]{1,0:T(8,128)(2,1)S(1)} %get-tuple-element.16.after), channel_id=1, source_target_pairs={{0,1},{1,0},{2,3},{3,2},{4,5},{5,4},{6,7},{7,6},{8,9},{9,8},{10,11... | collective-permute-start | bytes 1277960 | tf_op jit(solution)/shard_map/ppermute | solution.py:27
  48.4 14.0 %collective-permute-start.15 = (bf16[64,3200]{1,0:T(8,128)(2,1)S(1)}, bf16[64,3200]{1,0:T(8,128)(2,1)S(1)}, u32[]{:S(2)}, u32[]{:S(2)}) collective-permute-start(bf16[64,3200]{1,0:T(8,128)(2,1)S(1)} %get-tuple-element.19), channel_id=1, source_target_pairs={{0,1},{1,0},{2,3},{3,2},{4,5},{5,4},{6,7},{7,6},{8,9},{9,8},{10,11... | collective-permute-start | bytes 1228808 | tf_op jit(solution)/shard_map/ppermute | solution.py:27
  62.5 5.2 %copy-start.6 = (bf16[64,3328]{1,0:T(8,128)(2,1)S(1)}, bf16[64,3328]{1,0:T(8,128)(2,1)}, u32[]{:S(2)}) copy-start(bf16[64,3328]{1,0:T(8,128)(2,1)} %get-tuple-element.20) | copy-start | bytes 1277956
  62.6 11.7 %copy-start.5 = (bf16[80,3328]{1,0:T(8,128)(2,1)S(1)}, bf16[80,3328]{1,0:T(8,128)(2,1)}, u32[]{:S(2)}) copy-start(bf16[80,3328]{1,0:T(8,128)(2,1)} %get-tuple-element.21) | copy-start | bytes 1597444
  62.7 11.6 %collective-permute-start.16 = (bf16[8,16384]{1,0:T(8,128)(2,1)S(1)}, bf16[8,16384]{1,0:T(8,128)(2,1)S(1)}, u32[]{:S(2)}, u32[]{:S(2)}) collective-permute-start(bf16[8,16384]{1,0:T(8,128)(2,1)S(1)} %pad_maximum_fusion.3), channel_id=1, source_target_pairs={{0,2},{1,3},{2,4},{3,5},{4,6},{5,7},{6,8},{7,9},{8,10},{9,11},{10,... | collective-permute-start | bytes 786440 | tf_op jit(solution)/shard_map/ppermute | solution.py:22
  67.7 6.6 %collective-permute-start.17 = (bf16[8,16256]{1,0:T(8,128)(2,1)S(1)}, bf16[8,16256]{1,0:T(8,128)(2,1)S(1)}, u32[]{:S(2)}, u32[]{:S(2)}) collective-permute-start(bf16[8,16256]{1,0:T(8,128)(2,1)S(1)} %pad_maximum_fusion.4), channel_id=1, source_target_pairs={{0,14},{1,15},{2,0},{3,1},{4,2},{5,3},{6,4},{7,5},{8,6},{9,7},{10,... | collective-permute-start | bytes 780296 | tf_op jit(solution)/shard_map/ppermute | solution.py:22
  67.8 24.3 %collective-permute-start.21 = (bf16[64,3328]{1,0:T(8,128)(2,1)S(1)}, bf16[64,3328]{1,0:T(8,128)(2,1)S(1)}, u32[]{:S(2)}, u32[]{:S(2)}) collective-permute-start(bf16[64,3328]{1,0:T(8,128)(2,1)S(1)} %copy-done.6), channel_id=1, source_target_pairs={{0,16},{1,17},{2,18},{3,19},{4,20},{5,21},{6,22},{7,23},{8,24},{9,... | collective-permute-start | bytes 1277960 | tf_op jit(solution)/shard_map/ppermute | solution.py:37
  74.3 28.0 %collective-permute-start.25 = (bf16[80,3328]{1,0:T(8,128)(2,1)S(1)}, bf16[80,3328]{1,0:T(8,128)(2,1)S(1)}, u32[]{:S(2)}, u32[]{:S(2)}) collective-permute-start(bf16[80,3328]{1,0:T(8,128)(2,1)S(1)} %copy-done.5), channel_id=1, source_target_pairs={{0,240},{1,241},{2,242},{3,243},{4,244},{5,245},{6,246},{7,247},{8... | collective-permute-start | bytes 1597448 | tf_op jit(solution)/shard_map/ppermute | solution.py:37
  74.5 12.4 %collective-permute-start.20 = (bf16[8,3200]{1,0:T(8,128)(2,1)S(1)}, bf16[8,3200]{1,0:T(8,128)(2,1)S(1)}, u32[]{:S(2)}, u32[]{:S(2)}) collective-permute-start(bf16[8,3200]{1,0:T(8,128)(2,1)S(1)} %fusion.10), channel_id=1, source_target_pairs={{0,26},{1,27},{2,28},{3,29},{4,30},{5,31},{6,16},{7,17},{8,18},{9,... | collective-permute-start | bytes 153608 | tf_op jit(solution)/shard_map/ppermute | solution.py:37
  80.7 8.6 %collective-permute-start.19 = (bf16[8,3200]{1,0:T(8,128)(2,1)S(1)}, bf16[8,3200]{1,0:T(8,128)(2,1)S(1)}, u32[]{:S(2)}, u32[]{:S(2)}) collective-permute-start(bf16[8,3200]{1,0:T(8,128)(2,1)S(1)} %slice.305), channel_id=1, source_target_pairs={{0,22},{1,23},{2,24},{3,25},{4,26},{5,27},{6,28},{7,29},{8,30},{9,... | collective-permute-start | bytes 153608 | tf_op jit(solution)/shard_map/ppermute | solution.py:37
  81.0 10.7 %collective-permute-start.18 = (bf16[8,3200]{1,0:T(8,128)(2,1)S(1)}, bf16[8,3200]{1,0:T(8,128)(2,1)S(1)}, u32[]{:S(2)}, u32[]{:S(2)}) collective-permute-start(bf16[8,3200]{1,0:T(8,128)(2,1)S(1)} %slice.232), channel_id=1, source_target_pairs={{0,16},{1,17},{2,18},{3,19},{4,20},{5,21},{6,22},{7,23},{8,24},{9,... | collective-permute-start | bytes 153608 | tf_op jit(solution)/shard_map/ppermute | solution.py:37
  86.9 11.3 %collective-permute-start.24 = (bf16[8,3328]{1,0:T(8,128)(2,1)S(1)}, bf16[8,3328]{1,0:T(8,128)(2,1)S(1)}, u32[]{:S(2)}, u32[]{:S(2)}) collective-permute-start(bf16[8,3328]{1,0:T(8,128)(2,1)S(1)} %slice.303), channel_id=1, source_target_pairs={{0,250},{1,251},{2,252},{3,253},{4,254},{5,255},{6,240},{7,241},{8... | collective-permute-start | bytes 159752 | tf_op jit(solution)/shard_map/ppermute | solution.py:37
  89.2 13.0 %collective-permute-start.23 = (bf16[8,3328]{1,0:T(8,128)(2,1)S(1)}, bf16[8,3328]{1,0:T(8,128)(2,1)S(1)}, u32[]{:S(2)}, u32[]{:S(2)}) collective-permute-start(bf16[8,3328]{1,0:T(8,128)(2,1)S(1)} %fusion.9), channel_id=1, source_target_pairs={{0,246},{1,247},{2,248},{3,249},{4,250},{5,251},{6,252},{7,253},{8... | collective-permute-start | bytes 159752 | tf_op jit(solution)/shard_map/ppermute | solution.py:37
  91.7 10.5 %collective-permute-start.22 = (bf16[8,3328]{1,0:T(8,128)(2,1)S(1)}, bf16[8,3328]{1,0:T(8,128)(2,1)S(1)}, u32[]{:S(2)}, u32[]{:S(2)}) collective-permute-start(bf16[8,3328]{1,0:T(8,128)(2,1)S(1)} %slice.242), channel_id=1, source_target_pairs={{0,240},{1,241},{2,242},{3,243},{4,244},{5,245},{6,246},{7,247},{8... | collective-permute-start | bytes 159752 | tf_op jit(solution)/shard_map/ppermute | solution.py:37

commit v5 on v4

--- a/solution.py
+++ b/solution.py
@@ -344,7 +344,7 @@
     return [own], [below1, above1], [below2, above2], [below3, above3, far]
 
 
-def sum_columns(b_total, f_total, capacity):
+def sum_columns(b_total, f_total, capacity, packs):
     width = b_total.shape[1]
     low, full = jnp.bfloat16, jnp.float32
     total = jnp.concatenate([b_total, f_total], axis=1)
@@ -352,8 +352,10 @@
         total[at * capacity : (at + 1) * capacity] for at in range(total.shape[0] // capacity)
     ]
     both = total.shape[1]
-    up = along_z(jnp.concatenate([above1, below2, far[:, :width]], axis=1).astype(low), 1).astype(full)
-    down = along_z(jnp.concatenate([below1, above2, far[:, width:]], axis=1).astype(low), -1).astype(full)
+    up = along_z(jnp.concatenate([above1, below2, far[:, :width]], axis=1).astype(low), 1)
+    down = along_z(jnp.concatenate([below1, above2, far[:, width:]], axis=1).astype(low), -1)
+    up, down, *packs = lax.optimization_barrier((up, down, *packs))
+    up, down = up.astype(full), down.astype(full)
     near = own + up[:, :both] + down[:, :both]
     above3 = above3 + down[:, both : 2 * both]
     below3 = below3 + up[:, both : 2 * both]
@@ -367,7 +369,7 @@
     def add(parts):
         return sum(part.astype(full) for part in parts)
 
-    return add((b_near, b_up, b_down)), add((f_near, f_up, f_down))
+    return add((b_near, b_up, b_down)), add((f_near, f_up, f_down)), *packs
 
 
 def body(
@@ -391,8 +393,6 @@
     rows, f_pack, b_pack = head(
         capacity, fwd_ids, bwd_ids, fwd_lengths, bwd_lengths, fwd_in[0], bwd_in[0], bwd_grad[0], norm_gain, router
     )
-    f_pack = across(f_pack, 1, 0)
-    b_pack = across(b_pack, -1, 0)
     column = gather_column(rows)
     other = swap_x(rows)
     other_near = [along_z(other, 1), along_z(other, -1)]
@@ -406,17 +406,21 @@
 
     own, near, two, far = column
     groups = [of_backward(blocks) for blocks in column]
-    others = [of_backward([other]), of_backward(other_near), swap_x(groups[2]), swap_x(groups[3])]
+    other_two = swap_x(jnp.concatenate(two, axis=0))
+    other_two = [other_two[: 3 * capacity], other_two[3 * capacity :]]
+    others = [of_backward([other]), of_backward(other_near), of_backward(other_two), swap_x(groups[3])]
     f_own = of_forward(own + near + two + far)
     loaded = hold((groups[3],), weights)
-    f_rest, others[3], loaded = lax.optimization_barrier((of_forward(two + far), others[3], loaded))
-    f_other = jnp.concatenate([of_forward([other] + other_near), swap_x(f_rest)], axis=0)
+    f_far, others[3], loaded = lax.optimization_barrier((of_forward(far), others[3], loaded))
+    f_other = jnp.concatenate([of_forward([other] + other_near + other_two), swap_x(f_far)], axis=0)
 
     b_mine, b_theirs = backward_expert(capacity, groups + others, loaded, weights)
     f_mine, f_theirs = forward_expert(f_own, f_other, b_theirs, weights)
-    b_total = b_mine + swap_x(b_theirs).astype(jnp.float32)
+    b_got, f_pack, b_pack = lax.optimization_barrier((swap_x(b_theirs), f_pack, b_pack))
+    packs = (across(f_pack, 1, 0), across(b_pack, -1, 0))
+    b_total = b_mine + b_got.astype(jnp.float32)
     f_total = f_mine + swap_x(f_theirs).astype(jnp.float32)
-    b_sums, f_sums = sum_columns(b_total, f_total, capacity)
+    b_sums, f_sums, f_pack, b_pack = sum_columns(b_total, f_total, capacity, packs)
     bwd_out = finish(backward_finish_kernel, "backward_finish", capacity, b_sums, b_pack, tok_count)
     fwd_out = finish(forward_finish_kernel, "forward_finish", capacity, f_sums, f_pack, tok_count)
     return (fwd_out[None], bwd_out[None])

time: 104 us -> 101 us (0.971)
  the two profiles are of different devices: /device:TPU:89 before, /device:TPU:57 now
where the time goes in v5:
time: 101 us
  starting transfers between devices  51 us (50%)
  waiting for transfers between devices  26.5 us (26%)
  Pallas kernels  15.6 us (15%)
  local copies, waits for them, and re-layouts  5.09 us (5%)
  between operations  2.32 us (2%)
    ppermute x8, starting transfers between devices, across(): return lax.ppermute(value, ('pipe', 'dp'), pairs)  27 us
    ppermute x12, starting transfers between devices, along_z(): return lax.ppermute(value, 'dp', pairs)  18.1 us
    ppermute x12, waiting for transfers between devices, along_z(): return lax.ppermute(value, 'dp', pairs)  15.7 us
    pallas_call x2, Pallas kernels, expert_call(): pl.pallas_call(kernel, out_shape=(jax.ShapeDtypeStruct((half, width + ext...  9.72 us
    ppermute x8, waiting for transfers between devices, across(): return lax.ppermute(value, ('pipe', 'dp'), pairs)  8.01 us
    ppermute x6, starting transfers between devices, swap_x(): lax.ppermute(value, 'dp', [(source, source ^ 1) for source in range(count)])  5.81 us
    unnamed x25, local copies, waits for them, and re-layouts  3.96 us
    pallas_call x1, Pallas kernels, head(): pl.pallas_call(lambda *refs: fetched_head_kernel(capacity, *refs), out_sh...  3.2 us
  transfers between devices with their start and end apart: 26, of which 9 were waited for; matrix products, arithmetic and copies ran while one was open for 3% of the time, Pallas kernels for 11%

profile of v5, /device:TPU:57, one launch (start us, length us, event | category | flops | bytes accessed | tf_op | source)
XLA Modules:
  0.0 101.2 jit_solution(2665817605843283782)
XLA Ops:
  1.9 3.2 %head.1 = (bf16[24,3200]{1,0:T(8,128)(2,1)}, bf16[64,3328]{1,0:T(8,128)(2,1)}, bf16[80,3328]{1,0:T(8,128)(2,1)}) custom-call(s32[1,1]{1,0:T(1,128)S(6)} %copy.27.refs_0_, s32[1,1]{1,0:T(1,128)S(6)} %copy.28.refs_1_, s32[1,64]{1,0:T(1,128)} %refs_2_.1, s32[1,64]{1,0:T(1,128)} %refs_3_.1, bf16[64,3200]{1,0:T(8,128)(2,1)} %bitcast.23, ...), custom_call_target="tpu_custom_call" | custom-call | tf_op jit(solution)/shard_map/head/pallas_call | solution.py:127
  5.1 1.7 %collective-permute-start = (bf16[24,3200]{1,0:T(8,128)(2,1)}, bf16[24,3200]{1,0:T(8,128)(2,1)S(1)}, u32[]{:S(2)}, u32[]{:S(2)}) collective-permute-start(bf16[24,3200]{1,0:T(8,128)(2,1)} %get-tuple-element.19), channel_id=1, source_target_pairs={{0,2},{1,3},{2,4},{3,5},{4,6},{5,7},{6,8},{7,9},{8,10},{9,11},{10,... | collective-permute-start | bytes 460808 | tf_op jit(solution)/shard_map/ppermute | solution.py:22
  6.9 4.2 %collective-permute-start.2 = (bf16[24,3200]{1,0:T(8,128)(2,1)}, bf16[24,3200]{1,0:T(8,128)(2,1)S(1)}, u32[]{:S(2)}, u32[]{:S(2)}) collective-permute-start(bf16[24,3200]{1,0:T(8,128)(2,1)} %get-tuple-element.19), channel_id=1, source_target_pairs={{0,4},{1,5},{2,6},{3,7},{4,8},{5,9},{6,10},{7,11},{8,12},{9,13},{1... | collective-permute-start | bytes 460808 | tf_op jit(solution)/shard_map/ppermute | solution.py:22
  11.1 0.7 collective-permute-start.3
  11.8 1.2 %collective-permute-start.8 = (bf16[24,3200]{1,0:T(8,128)(2,1)}, bf16[24,3200]{1,0:T(8,128)(2,1)S(1)}, u32[]{:S(2)}, u32[]{:S(2)}) collective-permute-start(bf16[24,3200]{1,0:T(8,128)(2,1)} %get-tuple-element.19), channel_id=1, source_target_pairs={{0,1},{1,0},{2,3},{3,2},{4,5},{5,4},{6,7},{7,6},{8,9},{9,8},{10,11... | collective-permute-start | bytes 460808 | tf_op jit(solution)/shard_map/ppermute | solution.py:27
  13.0 0.8 slice_dynamic-update-slice_fusion.9
  13.9 0.9 slice.171.refs_0_
  14.8 5.0 %collective-permute-done.2 = bf16[24,3200]{1,0:T(8,128)(2,1)S(1)} collective-permute-done((bf16[24,3200]{1,0:T(8,128)(2,1)}, bf16[24,3200]{1,0:T(8,128)(2,1)S(1)}, u32[]{:S(2)}, u32[]{:S(2)}) %collective-permute-start.2) | collective-permute-done | bytes 153632 | tf_op jit(solution)/shard_map/ppermute | solution.py:22
  19.7 1.0 %collective-permute-start.6 = (bf16[24,1536]{1,0:T(8,128)(2,1)S(1)}, bf16[24,1536]{1,0:T(8,128)(2,1)S(1)}, u32[]{:S(2)}, u32[]{:S(2)}) collective-permute-start(bf16[24,1536]{1,0:T(8,128)(2,1)S(1)} %slice.226), channel_id=1, source_target_pairs={{0,4},{1,5},{2,6},{3,7},{4,8},{5,9},{6,10},{7,11},{8,12},{9,13},{1... | collective-permute-start | bytes 221192 | tf_op jit(solution)/shard_map/ppermute | solution.py:22
  20.8 2.6 %collective-permute-start.7 = (bf16[24,1664]{1,0:T(8,128)(2,1)S(1)}, bf16[24,1664]{1,0:T(8,128)(2,1)S(1)}, u32[]{:S(2)}, u32[]{:S(2)}) collective-permute-start(bf16[24,1664]{1,0:T(8,128)(2,1)S(1)} %slice.227), channel_id=1, source_target_pairs={{0,12},{1,13},{2,14},{3,15},{4,0},{5,1},{6,2},{7,3},{8,4},{9,5},{1... | collective-permute-start | bytes 239624 | tf_op jit(solution)/shard_map/ppermute | solution.py:22
  23.4 1.3 %collective-permute-start.11 = (bf16[48,3200]{1,0:T(8,128)(2,1)S(1)}, bf16[48,3200]{1,0:T(8,128)(2,1)S(1)}, u32[]{:S(2)}, u32[]{:S(2)}) collective-permute-start(bf16[48,3200]{1,0:T(8,128)(2,1)S(1)} %pad_maximum_fusion.2), channel_id=1, source_target_pairs={{0,1},{1,0},{2,3},{3,2},{4,5},{5,4},{6,7},{7,6},{8,9},{9,8},{10,11... | collective-permute-start | bytes 921608 | tf_op jit(solution)/shard_map/ppermute | solution.py:27
  24.8 1.6 %collective-permute-start.4 = (bf16[24,3200]{1,0:T(8,128)(2,1)S(1)}, bf16[24,3200]{1,0:T(8,128)(2,1)S(1)}, u32[]{:S(2)}, u32[]{:S(2)}) collective-permute-start(bf16[24,3200]{1,0:T(8,128)(2,1)S(1)} %collective-permute-done.2), channel_id=1, source_target_pairs={{0,2},{1,3},{2,4},{3,5},{4,6},{5,7},{6,8},{7,9},{8,10},{9,11},{10,... | collective-permute-start | bytes 460808 | tf_op jit(solution)/shard_map/ppermute | solution.py:22
  26.5 0.0 copy-start
  26.6 0.1 collective-permute-start.5
  26.7 1.5 %collective-permute-start.9 = (bf16[24,3200]{1,0:T(8,128)(2,1)S(1)}, bf16[24,3200]{1,0:T(8,128)(2,1)S(1)}, u32[]{:S(2)}, u32[]{:S(2)}) collective-permute-start(bf16[24,3200]{1,0:T(8,128)(2,1)S(1)} %collective-permute-done.8), channel_id=1, source_target_pairs={{0,2},{1,3},{2,4},{3,5},{4,6},{5,7},{6,8},{7,9},{8,10},{9,11},{10,... | collective-permute-start | bytes 460808 | tf_op jit(solution)/shard_map/ppermute | solution.py:22
  28.2 1.3 %collective-permute-start.10 = (bf16[24,3200]{1,0:T(8,128)(2,1)S(1)}, bf16[24,3200]{1,0:T(8,128)(2,1)S(1)}, u32[]{:S(2)}, u32[]{:S(2)}) collective-permute-start(bf16[24,3200]{1,0:T(8,128)(2,1)S(1)} %collective-permute-done.8), channel_id=1, source_target_pairs={{0,14},{1,15},{2,0},{3,1},{4,2},{5,3},{6,4},{7,5},{8,6},{9,7},{10,... | collective-permute-start | bytes 460808 | tf_op jit(solution)/shard_map/ppermute | solution.py:22
  29.5 0.4 collective-permute-done.4
  29.9 1.1 %collective-permute-done.5 = bf16[24,3200]{1,0:T(8,128)(2,1)S(1)} collective-permute-done((bf16[24,3200]{1,0:T(8,128)(2,1)S(1)}, bf16[24,3200]{1,0:T(8,128)(2,1)S(1)}, u32[]{:S(2)}, u32[]{:S(2)}) %collective-permute-start.5) | collective-permute-done | bytes 153632 | tf_op jit(solution)/shard_map/ppermute | solution.py:22
  31.1 0.7 collective-permute-start.12
  31.8 1.4 %collective-permute-done.9 = bf16[24,3200]{1,0:T(8,128)(2,1)S(1)} collective-permute-done((bf16[24,3200]{1,0:T(8,128)(2,1)S(1)}, bf16[24,3200]{1,0:T(8,128)(2,1)S(1)}, u32[]{:S(2)}, u32[]{:S(2)}) %collective-permute-start.9) | collective-permute-done | bytes 153632 | tf_op jit(solution)/shard_map/ppermute | solution.py:22
  33.3 1.9 %collective-permute-done.10 = bf16[24,3200]{1,0:T(8,128)(2,1)S(1)} collective-permute-done((bf16[24,3200]{1,0:T(8,128)(2,1)S(1)}, bf16[24,3200]{1,0:T(8,128)(2,1)S(1)}, u32[]{:S(2)}, u32[]{:S(2)}) %collective-permute-start.10) | collective-permute-done | bytes 153632 | tf_op jit(solution)/shard_map/ppermute | solution.py:22
  35.2 2.0 %copy-done.2 = bf16[1,576,3200]{2,1,0:T(8,128)(2,1)S(1)} copy-done((bf16[1,576,3200]{2,1,0:T(8,128)(2,1)S(1)}, bf16[1,576,3200]{2,1,0:T(8,128)(2,1)}, u32[]{:S(2)}) %copy-start.2) | copy-done | bytes 3686424
  37.4 1.0 collective-permute-start.14
  38.3 0.9 copy-done.3
  39.3 6.3 %backward_expert.1 = (f32[64,3328]{1,0:T(8,128)S(1)}, bf16[64,3328]{1,0:T(8,128)(2,1)S(1)}) custom-call(bf16[16,3200]{1,0:T(8,128)(2,1)S(1)} %slice.171.refs_0_, bf16[32,3200]{1,0:T(8,128)(2,1)S(1)} %pad_maximum_fusion.5.refs_1_, bf16[32,3200]{1,0:T(8,128)(2,1)S(1)} %pad_maximum_fusion.6.refs_2_, bf16[48,3200]{1,0:T(8,128)(2,1)S(1)} %pad_maximum_fusion.1.refs_0_.refs_3_, ...), custom_call_target="tpu_custom_call" | custom-call | flops 2359296000 | bytes 11059200 | tf_op jit(solution)/shard_map/backward_expert/pallas_call | solution.py:219
  45.5 0.8 collective-permute-start.13
  46.3 3.5 %forward_expert.1 = (f32[64,3200]{1,0:T(8,128)S(1)}, bf16[64,3200]{1,0:T(8,128)(2,1)S(1)}) custom-call(bf16[64,3200]{1,0:T(8,128)(2,1)S(1)} %get-tuple-element.45.own, bf16[64,3200]{1,0:T(8,128)(2,1)S(1)} %constant_dynamic-update-slice_fusion.5.other, bf16[64,3328]{1,0:T(8,128)(2,1)S(1)} %get-tuple-element.23.after, bf16[576,3200]{1,0:T(8,128)(2,1)S(1)} %bitcast.14, ...), custom_call_target="tpu_custom_call" | custom-call | flops 1415577600 | bytes 11059200 | tf_op jit(solution)/shard_map/forward_expert/pallas_call | solution.py:219
  49.8 0.8 collective-permute-start.15
  50.6 2.7 %collective-permute-done.13 = bf16[64,3328]{1,0:T(8,128)(2,1)S(1)} collective-permute-done((bf16[64,3328]{1,0:T(8,128)(2,1)S(1)}, bf16[64,3328]{1,0:T(8,128)(2,1)S(1)}, u32[]{:S(2)}, u32[]{:S(2)}) %collective-permute-start.13) | collective-permute-done | bytes 426016 | tf_op jit(solution)/shard_map/ppermute | solution.py:27
  53.4 0.1 convert_add_fusion
  53.5 8.6 %collective-permute-start.19 = (bf16[80,3328]{1,0:T(8,128)(2,1)S(1)}, bf16[80,3328]{1,0:T(8,128)(2,1)S(1)}, u32[]{:S(2)}, u32[]{:S(2)}) collective-permute-start(bf16[80,3328]{1,0:T(8,128)(2,1)S(1)} %copy-done.4), channel_id=1, source_target_pairs={{0,240},{1,241},{2,242},{3,243},{4,244},{5,245},{6,246},{7,247},{8... | collective-permute-start | bytes 1597448 | tf_op jit(solution)/shard_map/ppermute | solution.py:37
  62.1 2.2 %collective-permute-start.18 = (bf16[64,3328]{1,0:T(8,128)(2,1)S(1)}, bf16[64,3328]{1,0:T(8,128)(2,1)S(1)}, u32[]{:S(2)}, u32[]{:S(2)}) collective-permute-start(bf16[64,3328]{1,0:T(8,128)(2,1)S(1)} %copy-done.5), channel_id=1, source_target_pairs={{0,16},{1,17},{2,18},{3,19},{4,20},{5,21},{6,22},{7,23},{8,24},{9,... | collective-permute-start | bytes 1277960 | tf_op jit(solution)/shard_map/ppermute | solution.py:37
  64.3 0.1 convert_add_fusion.1
  64.4 0.1 fusion
  64.6 3.2 %collective-permute-start.16 = (bf16[8,16384]{1,0:T(8,128)(2,1)S(1)}, bf16[8,16384]{1,0:T(8,128)(2,1)S(1)}, u32[]{:S(2)}, u32[]{:S(2)}) collective-permute-start(bf16[8,16384]{1,0:T(8,128)(2,1)S(1)} %pad_maximum_fusion.3), channel_id=1, source_target_pairs={{0,2},{1,3},{2,4},{3,5},{4,6},{5,7},{6,8},{7,9},{8,10},{9,11},{10,... | collective-permute-start | bytes 786440 | tf_op jit(solution)/shard_map/ppermute | solution.py:22
  67.8 0.1 collective-permute-start.17
  67.9 6.0 %collective-permute-done.17 = bf16[8,16256]{1,0:T(8,128)(2,1)S(1)} collective-permute-done((bf16[8,16256]{1,0:T(8,128)(2,1)S(1)}, bf16[8,16256]{1,0:T(8,128)(2,1)S(1)}, u32[]{:S(2)}, u32[]{:S(2)}) %collective-permute-start.17) | collective-permute-done | bytes 260128 | tf_op jit(solution)/shard_map/ppermute | solution.py:22
  74.0 0.1 fusion.4
  74.2 5.3 %collective-permute-start.20 = (bf16[8,3200]{1,0:T(8,128)(2,1)S(1)}, bf16[8,3200]{1,0:T(8,128)(2,1)S(1)}, u32[]{:S(2)}, u32[]{:S(2)}) collective-permute-start(bf16[8,3200]{1,0:T(8,128)(2,1)S(1)} %slice.256), channel_id=1, source_target_pairs={{0,16},{1,17},{2,18},{3,19},{4,20},{5,21},{6,22},{7,23},{8,24},{9,... | collective-permute-start | bytes 153608 | tf_op jit(solution)/shard_map/ppermute | solution.py:37
  79.5 1.8 %collective-permute-start.21 = (bf16[8,3200]{1,0:T(8,128)(2,1)S(1)}, bf16[8,3200]{1,0:T(8,128)(2,1)S(1)}, u32[]{:S(2)}, u32[]{:S(2)}) collective-permute-start(bf16[8,3200]{1,0:T(8,128)(2,1)S(1)} %slice.329), channel_id=1, source_target_pairs={{0,22},{1,23},{2,24},{3,25},{4,26},{5,27},{6,28},{7,29},{8,30},{9,... | collective-permute-start | bytes 153608 | tf_op jit(solution)/shard_map/ppermute | solution.py:37
  81.3 4.4 %collective-permute-start.22 = (bf16[8,3200]{1,0:T(8,128)(2,1)S(1)}, bf16[8,3200]{1,0:T(8,128)(2,1)S(1)}, u32[]{:S(2)}, u32[]{:S(2)}) collective-permute-start(bf16[8,3200]{1,0:T(8,128)(2,1)S(1)} %fusion.10), channel_id=1, source_target_pairs={{0,26},{1,27},{2,28},{3,29},{4,30},{5,31},{6,16},{7,17},{8,18},{9,... | collective-permute-start | bytes 153608 | tf_op jit(solution)/shard_map/ppermute | solution.py:37
  85.7 0.5 collective-permute-start.24
  86.3 1.6 %collective-permute-start.23 = (bf16[8,3328]{1,0:T(8,128)(2,1)S(1)}, bf16[8,3328]{1,0:T(8,128)(2,1)S(1)}, u32[]{:S(2)}, u32[]{:S(2)}) collective-permute-start(bf16[8,3328]{1,0:T(8,128)(2,1)S(1)} %slice.266), channel_id=1, source_target_pairs={{0,240},{1,241},{2,242},{3,243},{4,244},{5,245},{6,246},{7,247},{8... | collective-permute-start | bytes 159752 | tf_op jit(solution)/shard_map/ppermute | solution.py:37
  87.8 2.6 %collective-permute-start.25 = (bf16[8,3328]{1,0:T(8,128)(2,1)S(1)}, bf16[8,3328]{1,0:T(8,128)(2,1)S(1)}, u32[]{:S(2)}, u32[]{:S(2)}) collective-permute-start(bf16[8,3328]{1,0:T(8,128)(2,1)S(1)} %slice.327), channel_id=1, source_target_pairs={{0,250},{1,251},{2,252},{3,253},{4,254},{5,255},{6,240},{7,241},{8... | collective-permute-start | bytes 159752 | tf_op jit(solution)/shard_map/ppermute | solution.py:37
  90.5 1.3 %forward_finish.1 = bf16[64,3200]{1,0:T(8,128)(2,1)} custom-call(f32[8,3200]{1,0:T(8,128)S(1)} %convert_add_fusion.3.refs_0_, bf16[64,3328]{1,0:T(8,128)(2,1)S(1)} %collective-permute-done.18.refs_1_), custom_call_target="tpu_custom_call" | custom-call | tf_op jit(solution)/shard_map/forward_finish/pallas_call | solution.py:323
  91.7 5.3 %collective-permute-done.24 = bf16[8,3328]{1,0:T(8,128)(2,1)S(1)} collective-permute-done((bf16[8,3328]{1,0:T(8,128)(2,1)S(1)}, bf16[8,3328]{1,0:T(8,128)(2,1)S(1)}, u32[]{:S(2)}, u32[]{:S(2)}) %collective-permute-start.24) | collective-permute-done | bytes 53280 | tf_op jit(solution)/shard_map/ppermute | solution.py:37
  97.0 2.7 %collective-permute-done.25 = bf16[8,3328]{1,0:T(8,128)(2,1)S(1)} collective-permute-done((bf16[8,3328]{1,0:T(8,128)(2,1)S(1)}, bf16[8,3328]{1,0:T(8,128)(2,1)S(1)}, u32[]{:S(2)}, u32[]{:S(2)}) %collective-permute-start.25) | collective-permute-done | bytes 53280 | tf_op jit(solution)/shard_map/ppermute | solution.py:37
  99.8 1.4 %backward_finish.1 = bf16[64,3200]{1,0:T(8,128)(2,1)} custom-call(f32[8,3328]{1,0:T(8,128)S(1)} %convert_add_fusion.2.refs_0_, bf16[80,3328]{1,0:T(8,128)(2,1)S(1)} %collective-permute-done.19.refs_1_), custom_call_target="tpu_custom_call" | custom-call | tf_op jit(solution)/shard_map/backward_finish/pallas_call | solution.py:323
  (78 shorter events, 0.8 us)
Async XLA Ops:
  1.9 33.2 %copy-start.1 = (bf16[1,3200,576]{1,2,0:T(8,128)(2,1)S(1)}, bf16[1,3200,576]{1,2,0:T(8,128)(2,1)}, u32[]{:S(2)}) copy-start(bf16[1,3200,576]{1,2,0:T(8,128)(2,1)} %param.22) | copy-start | bytes 11059204
  5.1 18.3 %collective-permute-start = (bf16[24,3200]{1,0:T(8,128)(2,1)}, bf16[24,3200]{1,0:T(8,128)(2,1)S(1)}, u32[]{:S(2)}, u32[]{:S(2)}) collective-permute-start(bf16[24,3200]{1,0:T(8,128)(2,1)} %get-tuple-element.19), channel_id=1, source_target_pairs={{0,2},{1,3},{2,4},{3,5},{4,6},{5,7},{6,8},{7,9},{8,10},{9,11},{10,... | collective-permute-start | bytes 460808 | tf_op jit(solution)/shard_map/ppermute | solution.py:22
  6.9 17.9 %collective-permute-start.1 = (bf16[24,3200]{1,0:T(8,128)(2,1)}, bf16[24,3200]{1,0:T(8,128)(2,1)S(1)}, u32[]{:S(2)}, u32[]{:S(2)}) collective-permute-start(bf16[24,3200]{1,0:T(8,128)(2,1)} %get-tuple-element.19), channel_id=1, source_target_pairs={{0,14},{1,15},{2,0},{3,1},{4,2},{5,3},{6,4},{7,5},{8,6},{9,7},{10,... | collective-permute-start | bytes 460808 | tf_op jit(solution)/shard_map/ppermute | solution.py:22
  6.9 12.9 %collective-permute-start.2 = (bf16[24,3200]{1,0:T(8,128)(2,1)}, bf16[24,3200]{1,0:T(8,128)(2,1)S(1)}, u32[]{:S(2)}, u32[]{:S(2)}) collective-permute-start(bf16[24,3200]{1,0:T(8,128)(2,1)} %get-tuple-element.19), channel_id=1, source_target_pairs={{0,4},{1,5},{2,6},{3,7},{4,8},{5,9},{6,10},{7,11},{8,12},{9,13},{1... | collective-permute-start | bytes 460808 | tf_op jit(solution)/shard_map/ppermute | solution.py:22
  11.1 9.7 %collective-permute-start.3 = (bf16[24,3200]{1,0:T(8,128)(2,1)}, bf16[24,3200]{1,0:T(8,128)(2,1)S(1)}, u32[]{:S(2)}, u32[]{:S(2)}) collective-permute-start(bf16[24,3200]{1,0:T(8,128)(2,1)} %get-tuple-element.19), channel_id=1, source_target_pairs={{0,12},{1,13},{2,14},{3,15},{4,0},{5,1},{6,2},{7,3},{8,4},{9,5},{1... | collective-permute-start | bytes 460808 | tf_op jit(solution)/shard_map/ppermute | solution.py:22
  11.8 14.7 %collective-permute-start.8 = (bf16[24,3200]{1,0:T(8,128)(2,1)}, bf16[24,3200]{1,0:T(8,128)(2,1)S(1)}, u32[]{:S(2)}, u32[]{:S(2)}) collective-permute-start(bf16[24,3200]{1,0:T(8,128)(2,1)} %get-tuple-element.19), channel_id=1, source_target_pairs={{0,1},{1,0},{2,3},{3,2},{4,5},{5,4},{6,7},{7,6},{8,9},{9,8},{10,11... | collective-permute-start | bytes 460808 | tf_op jit(solution)/shard_map/ppermute | solution.py:27
  19.7 6.9 %collective-permute-start.6 = (bf16[24,1536]{1,0:T(8,128)(2,1)S(1)}, bf16[24,1536]{1,0:T(8,128)(2,1)S(1)}, u32[]{:S(2)}, u32[]{:S(2)}) collective-permute-start(bf16[24,1536]{1,0:T(8,128)(2,1)S(1)} %slice.226), channel_id=1, source_target_pairs={{0,4},{1,5},{2,6},{3,7},{4,8},{5,9},{6,10},{7,11},{8,12},{9,13},{1... | collective-permute-start | bytes 221192 | tf_op jit(solution)/shard_map/ppermute | solution.py:22
  20.8 7.4 %collective-permute-start.7 = (bf16[24,1664]{1,0:T(8,128)(2,1)S(1)}, bf16[24,1664]{1,0:T(8,128)(2,1)S(1)}, u32[]{:S(2)}, u32[]{:S(2)}) collective-permute-start(bf16[24,1664]{1,0:T(8,128)(2,1)S(1)} %slice.227), channel_id=1, source_target_pairs={{0,12},{1,13},{2,14},{3,15},{4,0},{5,1},{6,2},{7,3},{8,4},{9,5},{1... | collective-permute-start | bytes 239624 | tf_op jit(solution)/shard_map/ppermute | solution.py:22
  23.4 13.8 %collective-permute-start.11 = (bf16[48,3200]{1,0:T(8,128)(2,1)S(1)}, bf16[48,3200]{1,0:T(8,128)(2,1)S(1)}, u32[]{:S(2)}, u32[]{:S(2)}) collective-permute-start(bf16[48,3200]{1,0:T(8,128)(2,1)S(1)} %pad_maximum_fusion.2), channel_id=1, source_target_pairs={{0,1},{1,0},{2,3},{3,2},{4,5},{5,4},{6,7},{7,6},{8,9},{9,8},{10,11... | collective-permute-start | bytes 921608 | tf_op jit(solution)/shard_map/ppermute | solution.py:27
  24.8 5.1 %collective-permute-start.4 = (bf16[24,3200]{1,0:T(8,128)(2,1)S(1)}, bf16[24,3200]{1,0:T(8,128)(2,1)S(1)}, u32[]{:S(2)}, u32[]{:S(2)}) collective-permute-start(bf16[24,3200]{1,0:T(8,128)(2,1)S(1)} %collective-permute-done.2), channel_id=1, source_target_pairs={{0,2},{1,3},{2,4},{3,5},{4,6},{5,7},{6,8},{7,9},{8,10},{9,11},{10,... | collective-permute-start | bytes 460808 | tf_op jit(solution)/shard_map/ppermute | solution.py:22
  26.5 8.7 %copy-start = (bf16[1,3200,576]{1,2,0:T(8,128)(2,1)S(1)}, bf16[1,3200,576]{1,2,0:T(8,128)(2,1)}, u32[]{:S(2)}) copy-start(bf16[1,3200,576]{1,2,0:T(8,128)(2,1)} %param.21) | copy-start | bytes 11059204
  26.6 4.4 %collective-permute-start.5 = (bf16[24,3200]{1,0:T(8,128)(2,1)S(1)}, bf16[24,3200]{1,0:T(8,128)(2,1)S(1)}, u32[]{:S(2)}, u32[]{:S(2)}) collective-permute-start(bf16[24,3200]{1,0:T(8,128)(2,1)S(1)} %collective-permute-done.3), channel_id=1, source_target_pairs={{0,14},{1,15},{2,0},{3,1},{4,2},{5,3},{6,4},{7,5},{8,6},{9,7},{10,... | collective-permute-start | bytes 460808 | tf_op jit(solution)/shard_map/ppermute | solution.py:22
  26.7 6.6 %collective-permute-start.9 = (bf16[24,3200]{1,0:T(8,128)(2,1)S(1)}, bf16[24,3200]{1,0:T(8,128)(2,1)S(1)}, u32[]{:S(2)}, u32[]{:S(2)}) collective-permute-start(bf16[24,3200]{1,0:T(8,128)(2,1)S(1)} %collective-permute-done.8), channel_id=1, source_target_pairs={{0,2},{1,3},{2,4},{3,5},{4,6},{5,7},{6,8},{7,9},{8,10},{9,11},{10,... | collective-permute-start | bytes 460808 | tf_op jit(solution)/shard_map/ppermute | solution.py:22
  28.2 6.9 %collective-permute-start.10 = (bf16[24,3200]{1,0:T(8,128)(2,1)S(1)}, bf16[24,3200]{1,0:T(8,128)(2,1)S(1)}, u32[]{:S(2)}, u32[]{:S(2)}) collective-permute-start(bf16[24,3200]{1,0:T(8,128)(2,1)S(1)} %collective-permute-done.8), channel_id=1, source_target_pairs={{0,14},{1,15},{2,0},{3,1},{4,2},{5,3},{6,4},{7,5},{8,6},{9,7},{10,... | collective-permute-start | bytes 460808 | tf_op jit(solution)/shard_map/ppermute | solution.py:22
  31.1 6.3 %collective-permute-start.12 = (bf16[48,3200]{1,0:T(8,128)(2,1)S(1)}, bf16[48,3200]{1,0:T(8,128)(2,1)S(1)}, u32[]{:S(2)}, u32[]{:S(2)}) collective-permute-start(bf16[48,3200]{1,0:T(8,128)(2,1)S(1)} %pad_maximum_fusion.1.refs_0_.refs_3_), channel_id=1, source_target_pairs={{0,1},{1,0},{2,3},{3,2},{4,5},{5,4},{6,7},{7,6},{8,9},{9,8},{10,11... | collective-permute-start | bytes 921608 | tf_op jit(solution)/shard_map/ppermute | solution.py:27
  35.2 2.0 %copy-start.2 = (bf16[1,576,3200]{2,1,0:T(8,128)(2,1)S(1)}, bf16[1,576,3200]{2,1,0:T(8,128)(2,1)}, u32[]{:S(2)}) copy-start(bf16[1,576,3200]{2,1,0:T(8,128)(2,1)} %param.23) | copy-start | bytes 11059204
  37.2 2.0 %copy-start.3 = (bf16[1,576,3200]{2,1,0:T(8,128)(2,1)S(1)}, bf16[1,576,3200]{2,1,0:T(8,128)(2,1)}, u32[]{:S(2)}) copy-start(bf16[1,576,3200]{2,1,0:T(8,128)(2,1)} %param.23) | copy-start | bytes 11059204
  37.4 8.9 %collective-permute-start.14 = (bf16[24,3200]{1,0:T(8,128)(2,1)S(1)}, bf16[24,3200]{1,0:T(8,128)(2,1)S(1)}, u32[]{:S(2)}, u32[]{:S(2)}) collective-permute-start(bf16[24,3200]{1,0:T(8,128)(2,1)S(1)} %pad_maximum_fusion.9), channel_id=1, source_target_pairs={{0,1},{1,0},{2,3},{3,2},{4,5},{5,4},{6,7},{7,6},{8,9},{9,8},{10,11... | collective-permute-start | bytes 460808 | tf_op jit(solution)/shard_map/ppermute | solution.py:27
  45.5 7.8 %collective-permute-start.13 = (bf16[64,3328]{1,0:T(8,128)(2,1)S(1)}, bf16[64,3328]{1,0:T(8,128)(2,1)S(1)}, u32[]{:S(2)}, u32[]{:S(2)}) collective-permute-start(bf16[64,3328]{1,0:T(8,128)(2,1)S(1)} %get-tuple-element.23.after), channel_id=1, source_target_pairs={{0,1},{1,0},{2,3},{3,2},{4,5},{5,4},{6,7},{7,6},{8,9},{9,8},{10,11... | collective-permute-start | bytes 1277960 | tf_op jit(solution)/shard_map/ppermute | solution.py:27
  49.8 3.7 %copy-start.4 = (bf16[80,3328]{1,0:T(8,128)(2,1)S(1)}, bf16[80,3328]{1,0:T(8,128)(2,1)}, u32[]{:S(2)}) copy-start(bf16[80,3328]{1,0:T(8,128)(2,1)} %get-tuple-element.31) | copy-start | bytes 1597444
  49.8 12.3 %copy-start.5 = (bf16[64,3328]{1,0:T(8,128)(2,1)S(1)}, bf16[64,3328]{1,0:T(8,128)(2,1)}, u32[]{:S(2)}) copy-start(bf16[64,3328]{1,0:T(8,128)(2,1)} %get-tuple-element.30) | copy-start | bytes 1277956
  49.8 14.5 %collective-permute-start.15 = (bf16[64,3200]{1,0:T(8,128)(2,1)S(1)}, bf16[64,3200]{1,0:T(8,128)(2,1)S(1)}, u32[]{:S(2)}, u32[]{:S(2)}) collective-permute-start(bf16[64,3200]{1,0:T(8,128)(2,1)S(1)} %get-tuple-element.29), channel_id=1, source_target_pairs={{0,1},{1,0},{2,3},{3,2},{4,5},{5,4},{6,7},{7,6},{8,9},{9,8},{10,11... | collective-permute-start | bytes 1228808 | tf_op jit(solution)/shard_map/ppermute | solution.py:27
  53.5 20.5 %collective-permute-start.19 = (bf16[80,3328]{1,0:T(8,128)(2,1)S(1)}, bf16[80,3328]{1,0:T(8,128)(2,1)S(1)}, u32[]{:S(2)}, u32[]{:S(2)}) collective-permute-start(bf16[80,3328]{1,0:T(8,128)(2,1)S(1)} %copy-done.4), channel_id=1, source_target_pairs={{0,240},{1,241},{2,242},{3,243},{4,244},{5,245},{6,246},{7,247},{8... | collective-permute-start | bytes 1597448 | tf_op jit(solution)/shard_map/ppermute | solution.py:37
  62.1 11.8 %collective-permute-start.18 = (bf16[64,3328]{1,0:T(8,128)(2,1)S(1)}, bf16[64,3328]{1,0:T(8,128)(2,1)S(1)}, u32[]{:S(2)}, u32[]{:S(2)}) collective-permute-start(bf16[64,3328]{1,0:T(8,128)(2,1)S(1)} %copy-done.5), channel_id=1, source_target_pairs={{0,16},{1,17},{2,18},{3,19},{4,20},{5,21},{6,22},{7,23},{8,24},{9,... | collective-permute-start | bytes 1277960 | tf_op jit(solution)/shard_map/ppermute | solution.py:37
  64.6 9.3 %collective-permute-start.16 = (bf16[8,16384]{1,0:T(8,128)(2,1)S(1)}, bf16[8,16384]{1,0:T(8,128)(2,1)S(1)}, u32[]{:S(2)}, u32[]{:S(2)}) collective-permute-start(bf16[8,16384]{1,0:T(8,128)(2,1)S(1)} %pad_maximum_fusion.3), channel_id=1, source_target_pairs={{0,2},{1,3},{2,4},{3,5},{4,6},{5,7},{6,8},{7,9},{8,10},{9,11},{10,... | collective-permute-start | bytes 786440 | tf_op jit(solution)/shard_map/ppermute | solution.py:22
  67.8 6.1 %collective-permute-start.17 = (bf16[8,16256]{1,0:T(8,128)(2,1)S(1)}, bf16[8,16256]{1,0:T(8,128)(2,1)S(1)}, u32[]{:S(2)}, u32[]{:S(2)}) collective-permute-start(bf16[8,16256]{1,0:T(8,128)(2,1)S(1)} %pad_maximum_fusion.4), channel_id=1, source_target_pairs={{0,14},{1,15},{2,0},{3,1},{4,2},{5,3},{6,4},{7,5},{8,6},{9,7},{10,... | collective-permute-start | bytes 780296 | tf_op jit(solution)/shard_map/ppermute | solution.py:22
  74.2 13.6 %collective-permute-start.20 = (bf16[8,3200]{1,0:T(8,128)(2,1)S(1)}, bf16[8,3200]{1,0:T(8,128)(2,1)S(1)}, u32[]{:S(2)}, u32[]{:S(2)}) collective-permute-start(bf16[8,3200]{1,0:T(8,128)(2,1)S(1)} %slice.256), channel_id=1, source_target_pairs={{0,16},{1,17},{2,18},{3,19},{4,20},{5,21},{6,22},{7,23},{8,24},{9,... | collective-permute-start | bytes 153608 | tf_op jit(solution)/shard_map/ppermute | solution.py:37
  79.5 10.9 %collective-permute-start.21 = (bf16[8,3200]{1,0:T(8,128)(2,1)S(1)}, bf16[8,3200]{1,0:T(8,128)(2,1)S(1)}, u32[]{:S(2)}, u32[]{:S(2)}) collective-permute-start(bf16[8,3200]{1,0:T(8,128)(2,1)S(1)} %slice.329), channel_id=1, source_target_pairs={{0,22},{1,23},{2,24},{3,25},{4,26},{5,27},{6,28},{7,29},{8,30},{9,... | collective-permute-start | bytes 153608 | tf_op jit(solution)/shard_map/ppermute | solution.py:37
  81.3 9.1 %collective-permute-start.22 = (bf16[8,3200]{1,0:T(8,128)(2,1)S(1)}, bf16[8,3200]{1,0:T(8,128)(2,1)S(1)}, u32[]{:S(2)}, u32[]{:S(2)}) collective-permute-start(bf16[8,3200]{1,0:T(8,128)(2,1)S(1)} %fusion.10), channel_id=1, source_target_pairs={{0,26},{1,27},{2,28},{3,29},{4,30},{5,31},{6,16},{7,17},{8,18},{9,... | collective-permute-start | bytes 153608 | tf_op jit(solution)/shard_map/ppermute | solution.py:37
  85.7 11.3 %collective-permute-start.24 = (bf16[8,3328]{1,0:T(8,128)(2,1)S(1)}, bf16[8,3328]{1,0:T(8,128)(2,1)S(1)}, u32[]{:S(2)}, u32[]{:S(2)}) collective-permute-start(bf16[8,3328]{1,0:T(8,128)(2,1)S(1)} %fusion.9), channel_id=1, source_target_pairs={{0,246},{1,247},{2,248},{3,249},{4,250},{5,251},{6,252},{7,253},{8... | collective-permute-start | bytes 159752 | tf_op jit(solution)/shard_map/ppermute | solution.py:37
  86.3 10.8 %collective-permute-start.23 = (bf16[8,3328]{1,0:T(8,128)(2,1)S(1)}, bf16[8,3328]{1,0:T(8,128)(2,1)S(1)}, u32[]{:S(2)}, u32[]{:S(2)}) collective-permute-start(bf16[8,3328]{1,0:T(8,128)(2,1)S(1)} %slice.266), channel_id=1, source_target_pairs={{0,240},{1,241},{2,242},{3,243},{4,244},{5,245},{6,246},{7,247},{8... | collective-permute-start | bytes 159752 | tf_op jit(solution)/shard_map/ppermute | solution.py:37
  87.8 11.9 %collective-permute-start.25 = (bf16[8,3328]{1,0:T(8,128)(2,1)S(1)}, bf16[8,3328]{1,0:T(8,128)(2,1)S(1)}, u32[]{:S(2)}, u32[]{:S(2)}) collective-permute-start(bf16[8,3328]{1,0:T(8,128)(2,1)S(1)} %slice.327), channel_id=1, source_target_pairs={{0,250},{1,251},{2,252},{3,253},{4,254},{5,255},{6,240},{7,241},{8... | collective-permute-start | bytes 159752 | tf_op jit(solution)/shard_map/ppermute | solution.py:37

commit v6 on v5

v6 whole, which is shorter than its diff:
```python
import jax
import jax.numpy as jnp
from jax import lax
from jax.experimental import pallas as pl
from jax.experimental.pallas import tpu as pltpu
from jax.sharding import PartitionSpec as P

EXPERTS = 16
EPS = 1e-05
LANES = 128
CHUNKS = 1
VMEM_LIMIT = 20 * 1024 * 1024
VMEM = pl.BlockSpec(memory_space=pltpu.VMEM)
SMEM = pl.BlockSpec(memory_space=pltpu.SMEM)
NT = (((1,), (1,)), ((), ()))
TN = (((0,), (0,)), ((), ()))


def along_z(value, steps):
    count = lax.axis_size("dp")
    pairs = [(source, (source + 2 * steps) % count) for source in range(count)]
    return lax.ppermute(value, "dp", pairs)


def swap_x(value):
    count = lax.axis_size("dp")
    return lax.ppermute(value, "dp", [(source, source ^ 1) for source in range(count)])


def across(value, stages, steps):
    n_pipe, n_dp = lax.axis_size("pipe"), lax.axis_size("dp")
    pairs = [
        (p * n_dp + d, (p + stages) % n_pipe * n_dp + (d + 2 * steps) % n_dp)
        for p in range(n_pipe)
        for d in range(n_dp)
    ]
    return lax.ppermute(value, ("pipe", "dp"), pairs)


def columns(parts, rows):
    lane = lax.broadcasted_iota(jnp.int32, (rows, LANES), 1)
    out = jnp.zeros((rows, LANES), jnp.float32)
    for at, part in parts:
        out = jnp.where(lane == at, part, out)
    return out


def place(ids, capacity):
    tok_count = ids.shape[1]
    chosen = jnp.broadcast_to(jnp.where(ids == 0, 1.0, 0.0), (capacity, tok_count))
    before = lax.broadcasted_iota(jnp.int32, (tok_count, tok_count), 0)
    after = lax.broadcasted_iota(jnp.int32, (tok_count, tok_count), 1)
    upto = jnp.where(before <= after, 1.0, 0.0).astype(jnp.bfloat16)
    rank = dot(chosen.astype(jnp.bfloat16), upto)
    slot = lax.broadcasted_iota(jnp.int32, (capacity, tok_count), 0).astype(jnp.float32)
    return jnp.where((rank - 1.0 == slot) & (chosen > 0.0), 1.0, 0.0)


def slot_mask(placing, length):
    position = lax.broadcasted_iota(jnp.int32, placing.shape, 1)
    return jnp.sum(jnp.where(position < length, placing, 0.0), axis=1, keepdims=True)


def normalize(placing, tokens, gain):
    values = dot(placing.astype(jnp.bfloat16), tokens)
    inv = lax.rsqrt(jnp.mean(values * values, axis=1, keepdims=True) + EPS)
    return values, inv, (values * inv * gain).astype(jnp.bfloat16).astype(jnp.float32)


def head_kernel(capacity, f_len, b_len, *refs):
    sources, (rows, f_side, b_side), held, arrived = refs[:7], refs[7:10], refs[10:17], refs[17]
    copies = [
        pltpu.make_async_copy(source, target, arrived.at[at])
        for at, (source, target) in enumerate(zip(sources, held))
    ]
    for copy in copies:
        copy.start()
    for copy in copies:
        copy.wait()
    f_ids, b_ids, gain, router, f_in, b_in, grad = [ref[...] for ref in held]
    router = router.astype(jnp.float32)
    tok_count, width = f_in.shape

    def side(ids, length, tokens):
        placing = place(ids, capacity)
        values, inv, normed = normalize(placing, tokens, gain)
        prob = sigmoid(jnp.sum(normed * router, axis=1, keepdims=True))
        return placing, slot_mask(placing, length[0, 0]), values, inv, normed, prob

    def lanes_of(placing, scalars):
        wide = jnp.concatenate([placing, jnp.zeros((capacity, LANES - tok_count), jnp.float32)], axis=1)
        return wide + columns([(tok_count + at, scalar) for at, scalar in enumerate(scalars)], capacity)

    placing, mask, values, inv, normed, prob = side(b_ids, b_len, b_in)
    grads = dot(placing.astype(jnp.bfloat16), grad)
    b_rows = [normed, grads * mask]
    b_side[:capacity, :width] = values
    b_side[capacity : 2 * capacity, :width] = grads
    b_side[2 * capacity :, :width] = jnp.concatenate(
        [gain, router, jnp.zeros((capacity - 2, width), jnp.float32)], axis=0
    )
    b_side[:capacity, width:] = lanes_of(placing, (prob, inv, mask * prob * (1.0 - prob)))
    b_side[capacity:, width:] = jnp.zeros((2 * capacity, LANES), jnp.float32)
    placing, mask, values, inv, normed, prob = side(f_ids, f_len, f_in)
    rows[...] = jnp.concatenate(b_rows + [normed], axis=0).astype(jnp.bfloat16)
    f_side[:, :width] = values
    f_side[:, width:] = lanes_of(placing, (mask * prob,))


def head(capacity, f_len, b_len, *sources):
    width = sources[-1].shape[1]
    return pl.pallas_call(
        lambda *refs: head_kernel(capacity, *refs),
        out_shape=(
            jax.ShapeDtypeStruct((3 * capacity, width), jnp.bfloat16),
            jax.ShapeDtypeStruct((capacity, width + LANES), jnp.float32),
            jax.ShapeDtypeStruct((3 * capacity, width + LANES), jnp.float32),
        ),
        in_specs=[SMEM, SMEM] + [pl.BlockSpec(memory_space=pl.ANY)] * len(sources),
        out_specs=(VMEM,) * 3,
        scratch_shapes=[pltpu.VMEM(source.shape, source.dtype) for source in sources]
        + [pltpu.SemaphoreType.DMA((len(sources),))],
        compiler_params=pltpu.CompilerParams(vmem_limit_bytes=56 * 1024 * 1024),
        name="head",
    )(f_len, b_len, *sources)


def sigmoid(value):
    return 1.0 / (1.0 + jnp.exp(-value))


def dot_t(left, right):
    return lax.dot_general(left, right, NT, preferred_element_type=jnp.float32)


def dot(left, right):
    return jnp.dot(left, right, preferred_element_type=jnp.float32)


def chunk_of(step, weights):
    part = weights[0].shape[0] // CHUNKS
    return [weight[step * part : (step + 1) * part] for weight in weights]


def forward_kernel(own, other, after, gate_w, up_w, down_w, mine, theirs, rows, total):
    half = own.shape[0]
    rows[:half] = own[...]
    rows[half:] = other[...]
    for step in range(CHUNKS):
        gate, up, down = chunk_of(step, (gate_w, up_w, down_w))
        gate_pre = dot_t(rows[...], gate)
        up_pre = dot_t(rows[...], up)
        hidden = (gate_pre * sigmoid(gate_pre) * up_pre).astype(jnp.bfloat16)
        if step == 0 and CHUNKS > 1:
            total[...] = dot(hidden, down)
        elif step < CHUNKS - 1:
            total[...] += dot(hidden, down)
        else:
            part = (total[...] if step else 0.0) + dot(hidden, down)
            mine[...] = part[:half]
            theirs[...] = part[half:].astype(jnp.bfloat16)


def backward_kernel(capacity, groups, after, gate_w, up_w, down_w, mine, theirs, rows, grads, total):
    half, width = mine.shape[0], rows.shape[1]
    pair = 2 * capacity
    blocks = [(ref, at) for ref in groups for at in range(0, ref.shape[0], pair)]
    for at in range(0, len(blocks), 2):
        low, high = [ref[start : start + pair].astype(jnp.float32) for ref, start in blocks[at : at + 2]]
        place = slice(at * capacity, at * capacity + pair)
        rows[place] = jnp.concatenate([low[:capacity], high[:capacity]], axis=0).astype(jnp.bfloat16)
        grads[place] = jnp.concatenate([low[capacity:], high[capacity:]], axis=0).astype(jnp.bfloat16)

    dots = jnp.zeros((2 * half, 1), jnp.float32)
    for step in range(CHUNKS):
        gate, up, down = chunk_of(step, (gate_w, up_w, down_w))
        gate_pre = dot_t(rows[...], gate)
        up_pre = dot_t(rows[...], up)
        d_hidden = dot_t(grads[...], down)
        gate_sig = sigmoid(gate_pre)
        silu = gate_pre * gate_sig
        hidden = (silu * up_pre).astype(jnp.bfloat16).astype(jnp.float32)
        dots += jnp.sum(hidden * d_hidden, axis=1, keepdims=True)
        d_gate = (d_hidden * up_pre * gate_sig * (1.0 + gate_pre * (1.0 - gate_sig))).astype(jnp.bfloat16)
        d_up = (d_hidden * silu).astype(jnp.bfloat16)
        part = dot(d_gate, gate) + dot(d_up, up)
        if step == 0 and CHUNKS > 1:
            total[...] = part
        elif step < CHUNKS - 1:
            total[...] += part
        else:
            part += total[...] if step else 0.0
            mine[:, :width] = part[:half]
            theirs[:, :width] = part[half:].astype(jnp.bfloat16)
    high = dots.astype(jnp.bfloat16).astype(jnp.float32)
    tail = columns([(0, high), (1, dots - high)], 2 * half)
    mine[:, width:] = tail[:half]
    theirs[:, width:] = tail[half:].astype(jnp.bfloat16)


def expert_call(kernel, name, operands, weights, extra, count, spaces, products, scratch):
    hidden, width = weights[0].shape
    half = count // 2
    return pl.pallas_call(
        kernel,
        out_shape=(
            jax.ShapeDtypeStruct((half, width + extra), jnp.float32),
            jax.ShapeDtypeStruct((half, width + extra), jnp.bfloat16),
        ),
        in_specs=spaces + [VMEM] * 3,
        out_specs=(VMEM, VMEM),
        scratch_shapes=[pltpu.VMEM((count, width), jnp.bfloat16)] * scratch
        + [pltpu.VMEM((count, width), jnp.float32)],
        compiler_params=pltpu.CompilerParams(vmem_limit_bytes=VMEM_LIMIT),
        cost_estimate=pl.CostEstimate(
            flops=products * 2 * count * hidden * width, bytes_accessed=6 * hidden * width, transcendentals=0
        ),
        name=name,
    )(*operands, *weights)


def hold(after, weights):
    def kernel(*refs):
        held = refs[-1]
        held[...] = jnp.zeros_like(held)

    return pl.pallas_call(
        kernel,
        out_shape=jax.ShapeDtypeStruct((8, LANES), jnp.float32),
        in_specs=[pl.BlockSpec(memory_space=pl.ANY)] * len(after) + [VMEM] * 3,
        out_specs=VMEM,
        compiler_params=pltpu.CompilerParams(vmem_limit_bytes=2 * 1024 * 1024),
        cost_estimate=pl.CostEstimate(
            flops=0, bytes_accessed=6 * weights[0].shape[0] * weights[0].shape[1], transcendentals=0
        ),
        name="hold",
    )(*after, *weights)


def forward_expert(own, other, after, weights):
    spaces = [VMEM, VMEM, pl.BlockSpec(memory_space=pl.ANY)]
    return expert_call(
        forward_kernel, "forward_expert", (own, other, after), weights, 0, 2 * own.shape[0], spaces, 3, 1
    )


def backward_expert(capacity, groups, after, weights):
    count = sum(group.shape[0] for group in groups) // 2

    def kernel(*refs):
        backward_kernel(capacity, refs[: len(groups)], *refs[len(groups) :])

    return expert_call(
        kernel,
        "backward_expert",
        groups + [after],
        weights,
        LANES,
        count,
        [VMEM] * len(groups) + [pl.BlockSpec(memory_space=pl.ANY)],
        5,
        2,
    )


def overlay(placing, rows, tokens, out):
    place16 = placing.astype(jnp.bfloat16)
    placed = lax.dot_general(place16, rows.astype(jnp.bfloat16), TN, preferred_element_type=jnp.float32)
    ones = jnp.ones((placing.shape[0], LANES), jnp.bfloat16)
    chosen = lax.dot_general(place16, ones, TN, preferred_element_type=jnp.float32)
    out[...] = jnp.where(chosen[:, :1] > 0.0, placed, tokens[...].astype(jnp.float32)).astype(jnp.bfloat16)


def rows_kernel(tok_count, near, up, down, f_side, b_side, f_out, b_out):
    capacity, width = near.shape[0], f_side.shape[1] - LANES
    total = near[...] + up[...].astype(jnp.float32) + down[...].astype(jnp.float32)
    d_rows = total[:, :width].astype(jnp.bfloat16).astype(jnp.float32)
    row_dot = total[:, width : width + 1] + total[:, width + 1 : width + 2]
    result = total[:, width + LANES :].astype(jnp.bfloat16).astype(jnp.float32)
    values, grads = b_side[:capacity, :width], b_side[capacity : 2 * capacity, :width]
    gain = b_side[2 * capacity : 2 * capacity + 1, :width]
    router = b_side[2 * capacity + 1 : 2 * capacity + 2, :width]
    lanes = b_side[:capacity, width:]
    prob, inv, slope = [lanes[:, tok_count + at : tok_count + at + 1] for at in range(3)]
    weighted = gain * (prob * d_rows + (slope * row_dot) * router)
    inner = jnp.mean(weighted * values, axis=1, keepdims=True)
    b_out[:, :width] = (grads + inv * weighted - values * inv * inv * inv * inner).astype(jnp.bfloat16)
    b_out[:, width:] = lanes.astype(jnp.bfloat16)
    scale = f_side[:, width + tok_count : width + tok_count + 1]
    f_out[:, :width] = (f_side[:, :width] + scale * result).astype(jnp.bfloat16)
    f_out[:, width:] = f_side[:, width:].astype(jnp.bfloat16)


def finished_rows(tok_count, near, up, down, f_side, b_side):
    return pl.pallas_call(
        lambda *refs: rows_kernel(tok_count, *refs),
        out_shape=(jax.ShapeDtypeStruct(f_side.shape, jnp.bfloat16),) * 2,
        in_specs=[VMEM] * 5,
        out_specs=(VMEM, VMEM),
        compiler_params=pltpu.CompilerParams(vmem_limit_bytes=8 * 1024 * 1024),
        name="rows",
    )(near, up, down, f_side, b_side)


def finish_kernel(moved, tokens, out):
    tok_count, width = tokens.shape
    overlay(moved[:, width : width + tok_count].astype(jnp.float32), moved[:, :width], tokens[...], out)


def finish(moved, tokens):
    return pl.pallas_call(
        finish_kernel,
        out_shape=jax.ShapeDtypeStruct(tokens.shape, tokens.dtype),
        in_specs=[VMEM, VMEM],
        out_specs=VMEM,
        compiler_params=pltpu.CompilerParams(vmem_limit_bytes=8 * 1024 * 1024),
        name="finish",
    )(moved, tokens)


def gather_column(own):
    half = own.shape[1] // (2 * LANES) * LANES
    below2 = along_z(own, 2)
    above2 = along_z(own, -2)
    below1 = along_z(own, 1)
    above1 = along_z(own, -1)
    below3 = along_z(below2, 1)
    above3 = along_z(above2, -1)
    far_low = along_z(below2[:, :half], 2)
    far_high = along_z(above2[:, half:], -2)
    far = jnp.concatenate([far_low, far_high], axis=1)
    return [own], [below1, above1], [below2, above2], [below3, above3, far]


def sum_columns(b_total, f_total, capacity, tokens):
    width = b_total.shape[1]
    low, full = jnp.bfloat16, jnp.float32
    total = jnp.concatenate([b_total, f_total], axis=1)
    own, below1, above1, below2, above2, below3, above3, far = [
        total[at * capacity : (at + 1) * capacity] for at in range(total.shape[0] // capacity)
    ]
    both = total.shape[1]
    up = along_z(jnp.concatenate([above1, below2, far[:, :width]], axis=1).astype(low), 1)
    down = along_z(jnp.concatenate([below1, above2, far[:, width:]], axis=1).astype(low), -1)
    up, down = up.astype(full), down.astype(full)
    near = own + up[:, :both] + down[:, :both]
    above3 = above3 + down[:, both : 2 * both]
    below3 = below3 + up[:, both : 2 * both]
    above3 = jnp.concatenate([above3[:, :width] + up[:, 2 * both :], above3[:, width:]], axis=1)
    below3 = jnp.concatenate([below3[:, :width], below3[:, width:] + down[:, 2 * both :]], axis=1)
    return (near, along_z(above3.astype(low), 3), along_z(below3.astype(low), -3)), tokens


def body(
    fwd_in,
    fwd_ids,
    fwd_lengths,
    bwd_in,
    bwd_grad,
    bwd_ids,
    bwd_lengths,
    norm_gain,
    router,
    w_gate,
    w_up,
    w_down,
):
    tok_count = fwd_in.shape[1]
    capacity = max(2, 2 * tok_count // EXPERTS)
    weights = (w_gate[0].T, w_up[0].T, w_down[0])

    rows, f_side, b_side = head(
        capacity, fwd_lengths, bwd_lengths, fwd_ids, bwd_ids, norm_gain, router, fwd_in[0], bwd_in[0], bwd_grad[0]
    )
    column = gather_column(rows)
    other = swap_x(rows)
    other_near = [along_z(other, 1), along_z(other, -1)]
    pair = 2 * capacity

    def of_backward(blocks):
        return jnp.concatenate([block[:pair] for block in blocks], axis=0)

    def of_forward(blocks):
        return jnp.concatenate([block[pair:] for block in blocks], axis=0)

    own, near, two, far = column
    groups = [of_backward(blocks) for blocks in column]
    other_two = swap_x(jnp.concatenate(two, axis=0))
    other_two = [other_two[: 3 * capacity], other_two[3 * capacity :]]
    others = [of_backward([other]), of_backward(other_near), of_backward(other_two), swap_x(groups[3])]
    f_own = of_forward(own + near + two + far)
    loaded = hold((groups[3],), weights)
    f_far, others[3], loaded = lax.optimization_barrier((of_forward(far), others[3], loaded))
    f_other = jnp.concatenate([of_forward([other] + other_near + other_two), swap_x(f_far)], axis=0)

    b_mine, b_theirs = backward_expert(capacity, groups + others, loaded, weights)
    f_mine, f_theirs = forward_expert(f_own, f_other, b_theirs, weights)
    b_got = swap_x(b_theirs)
    b_total = b_mine + b_got.astype(jnp.float32)
    f_got, f_tokens, b_tokens = lax.optimization_barrier((swap_x(f_theirs), fwd_in[0], bwd_grad[0]))
    tokens = (across(f_tokens, 1, 0), across(b_tokens, -1, 0))
    f_total = f_mine + f_got.astype(jnp.float32)
    parts, (f_tokens, b_tokens) = sum_columns(b_total, f_total, capacity, tokens)
    f_done, b_done = finished_rows(tok_count, *parts, f_side, b_side)
    bwd_out = finish(across(b_done, -1, 0), b_tokens)
    fwd_out = finish(across(f_done, 1, 0), f_tokens)
    return (fwd_out[None], bwd_out[None])


def solution(mesh):
    in_specs = (
        P("pipe", "dp", None),
        P("pipe", "dp"),
        P("pipe", "dp"),
        P("pipe", "dp", None),
        P("pipe", "dp", None),
        P("pipe", "dp"),
        P("pipe", "dp"),
        P("pipe", None),
        P("pipe", None),
        P("pipe", None, "dp"),
        P("pipe", None, "dp"),
        P("pipe", "dp", None),
    )
    out_specs = (P("pipe", "dp", None), P("pipe", "dp", None))
    return jax.shard_map(body, mesh=mesh, in_specs=in_specs, out_specs=out_specs, check_vma=False)
```

time: 101 us -> 100 us (0.990)
  the two profiles are of different devices: /device:TPU:57 before, /device:TPU:4 now
where the time goes in v6:
time: 100 us; the launch traced here: 98.5 us
  starting transfers between devices  39.7 us (40%)
  waiting for transfers between devices  36.9 us (37%)
  Pallas kernels  14.8 us (15%)
  local copies, waits for them, and re-layouts  4.16 us (4%)
  between operations  2.36 us (2%)
    ppermute x14, starting transfers between devices, along_z(): return lax.ppermute(value, 'dp', pairs)  31.4 us
    ppermute x14, waiting for transfers between devices, along_z(): return lax.ppermute(value, 'dp', pairs)  16.1 us
    ppermute x6, waiting for transfers between devices, swap_x(): lax.ppermute(value, 'dp', [(source, source ^ 1) for source in range(count)])  15.2 us
    pallas_call x2, Pallas kernels, expert_call(): pl.pallas_call(kernel, out_shape=(jax.ShapeDtypeStruct((half, width + ext...  9.08 us
    ppermute x6, starting transfers between devices, swap_x(): lax.ppermute(value, 'dp', [(source, source ^ 1) for source in range(count)])  7.17 us
    ppermute x4, waiting for transfers between devices, across(): return lax.ppermute(value, ('pipe', 'dp'), pairs)  5.58 us
    unnamed x29, local copies, waits for them, and re-layouts  3.04 us
    pallas_call x1, Pallas kernels, head(): pl.pallas_call(lambda *refs: head_kernel(capacity, *refs), out_shape=(jax...  3.03 us
  transfers between devices with their start and end apart: 24, of which 13 were waited for; matrix products, arithmetic and copies ran while one was open for 3% of the time, Pallas kernels for 11%

profile of v6, /device:TPU:4, one launch (start us, length us, event | category | flops | bytes accessed | tf_op | source)
XLA Modules:
  0.0 98.5 jit_solution(3550877083179255457)
XLA Ops:
  1.9 3.0 %head.1 = (bf16[24,3200]{1,0:T(8,128)(2,1)}, f32[8,3328]{1,0:T(8,128)}, f32[24,3328]{1,0:T(8,128)}) custom-call(s32[1,1]{1,0:T(1,128)S(6)} %copy.27.refs_0_, s32[1,1]{1,0:T(1,128)S(6)} %copy.28.refs_1_, s32[1,64]{1,0:T(1,128)} %refs_2_.1, s32[1,64]{1,0:T(1,128)} %refs_3_.1, f32[1,3200]{1,0:T(1,128)} %refs_4_.1, bf16[1,3200]{1,0:T(2,128)(2,1)} %refs_5_.1, ...), custom_call_target="tpu_custom_call" | custom-call | tf_op jit(solution)/shard_map/head/pallas_call | solution.py:112
  5.0 2.0 %collective-permute-start = (bf16[24,3200]{1,0:T(8,128)(2,1)}, bf16[24,3200]{1,0:T(8,128)(2,1)S(1)}, u32[]{:S(2)}, u32[]{:S(2)}) collective-permute-start(bf16[24,3200]{1,0:T(8,128)(2,1)} %get-tuple-element.17), channel_id=1, source_target_pairs={{0,2},{1,3},{2,4},{3,5},{4,6},{5,7},{6,8},{7,9},{8,10},{9,11},{10,... | collective-permute-start | bytes 460808 | tf_op jit(solution)/shard_map/ppermute | solution.py:22
  7.0 4.0 %collective-permute-start.1 = (bf16[24,3200]{1,0:T(8,128)(2,1)}, bf16[24,3200]{1,0:T(8,128)(2,1)S(1)}, u32[]{:S(2)}, u32[]{:S(2)}) collective-permute-start(bf16[24,3200]{1,0:T(8,128)(2,1)} %get-tuple-element.17), channel_id=1, source_target_pairs={{0,14},{1,15},{2,0},{3,1},{4,2},{5,3},{6,4},{7,5},{8,6},{9,7},{10,... | collective-permute-start | bytes 460808 | tf_op jit(solution)/shard_map/ppermute | solution.py:22
  11.0 4.1 %collective-permute-start.3 = (bf16[24,3200]{1,0:T(8,128)(2,1)}, bf16[24,3200]{1,0:T(8,128)(2,1)S(1)}, u32[]{:S(2)}, u32[]{:S(2)}) collective-permute-start(bf16[24,3200]{1,0:T(8,128)(2,1)} %get-tuple-element.17), channel_id=1, source_target_pairs={{0,12},{1,13},{2,14},{3,15},{4,0},{5,1},{6,2},{7,3},{8,4},{9,5},{1... | collective-permute-start | bytes 460808 | tf_op jit(solution)/shard_map/ppermute | solution.py:22
  15.1 1.2 %collective-permute-start.8 = (bf16[24,3200]{1,0:T(8,128)(2,1)}, bf16[24,3200]{1,0:T(8,128)(2,1)S(1)}, u32[]{:S(2)}, u32[]{:S(2)}) collective-permute-start(bf16[24,3200]{1,0:T(8,128)(2,1)} %get-tuple-element.17), channel_id=1, source_target_pairs={{0,1},{1,0},{2,3},{3,2},{4,5},{5,4},{6,7},{7,6},{8,9},{9,8},{10,11... | collective-permute-start | bytes 460808 | tf_op jit(solution)/shard_map/ppermute | solution.py:27
  16.3 0.8 slice_dynamic-update-slice_fusion.9
  17.2 0.9 slice.163.refs_0_
  18.1 3.1 %collective-permute-done.2 = bf16[24,3200]{1,0:T(8,128)(2,1)S(1)} collective-permute-done((bf16[24,3200]{1,0:T(8,128)(2,1)}, bf16[24,3200]{1,0:T(8,128)(2,1)S(1)}, u32[]{:S(2)}, u32[]{:S(2)}) %collective-permute-start.2) | collective-permute-done | bytes 153632 | tf_op jit(solution)/shard_map/ppermute | solution.py:22
  21.2 1.1 %collective-permute-start.6 = (bf16[24,1536]{1,0:T(8,128)(2,1)S(1)}, bf16[24,1536]{1,0:T(8,128)(2,1)S(1)}, u32[]{:S(2)}, u32[]{:S(2)}) collective-permute-start(bf16[24,1536]{1,0:T(8,128)(2,1)S(1)} %slice.216), channel_id=1, source_target_pairs={{0,4},{1,5},{2,6},{3,7},{4,8},{5,9},{6,10},{7,11},{8,12},{9,13},{1... | collective-permute-start | bytes 221192 | tf_op jit(solution)/shard_map/ppermute | solution.py:22
  22.2 0.3 collective-permute-done.3
  22.6 3.1 %collective-permute-start.7 = (bf16[24,1664]{1,0:T(8,128)(2,1)S(1)}, bf16[24,1664]{1,0:T(8,128)(2,1)S(1)}, u32[]{:S(2)}, u32[]{:S(2)}) collective-permute-start(bf16[24,1664]{1,0:T(8,128)(2,1)S(1)} %slice.217), channel_id=1, source_target_pairs={{0,12},{1,13},{2,14},{3,15},{4,0},{5,1},{6,2},{7,3},{8,4},{9,5},{1... | collective-permute-start | bytes 239624 | tf_op jit(solution)/shard_map/ppermute | solution.py:22
  25.7 1.3 %collective-permute-start.11 = (bf16[48,3200]{1,0:T(8,128)(2,1)S(1)}, bf16[48,3200]{1,0:T(8,128)(2,1)S(1)}, u32[]{:S(2)}, u32[]{:S(2)}) collective-permute-start(bf16[48,3200]{1,0:T(8,128)(2,1)S(1)} %pad_maximum_fusion.2), channel_id=1, source_target_pairs={{0,1},{1,0},{2,3},{3,2},{4,5},{5,4},{6,7},{7,6},{8,9},{9,8},{10,11... | collective-permute-start | bytes 921608 | tf_op jit(solution)/shard_map/ppermute | solution.py:27
  27.1 1.8 %collective-permute-start.4 = (bf16[24,3200]{1,0:T(8,128)(2,1)S(1)}, bf16[24,3200]{1,0:T(8,128)(2,1)S(1)}, u32[]{:S(2)}, u32[]{:S(2)}) collective-permute-start(bf16[24,3200]{1,0:T(8,128)(2,1)S(1)} %collective-permute-done.2), channel_id=1, source_target_pairs={{0,2},{1,3},{2,4},{3,5},{4,6},{5,7},{6,8},{7,9},{8,10},{9,11},{10,... | collective-permute-start | bytes 460808 | tf_op jit(solution)/shard_map/ppermute | solution.py:22
  29.0 1.6 %collective-permute-start.5 = (bf16[24,3200]{1,0:T(8,128)(2,1)S(1)}, bf16[24,3200]{1,0:T(8,128)(2,1)S(1)}, u32[]{:S(2)}, u32[]{:S(2)}) collective-permute-start(bf16[24,3200]{1,0:T(8,128)(2,1)S(1)} %collective-permute-done.3), channel_id=1, source_target_pairs={{0,14},{1,15},{2,0},{3,1},{4,2},{5,3},{6,4},{7,5},{8,6},{9,7},{10,... | collective-permute-start | bytes 460808 | tf_op jit(solution)/shard_map/ppermute | solution.py:22
  30.6 0.5 collective-permute-start.9
  31.2 2.9 %collective-permute-start.10 = (bf16[24,3200]{1,0:T(8,128)(2,1)S(1)}, bf16[24,3200]{1,0:T(8,128)(2,1)S(1)}, u32[]{:S(2)}, u32[]{:S(2)}) collective-permute-start(bf16[24,3200]{1,0:T(8,128)(2,1)S(1)} %collective-permute-done.8), channel_id=1, source_target_pairs={{0,14},{1,15},{2,0},{3,1},{4,2},{5,3},{6,4},{7,5},{8,6},{9,7},{10,... | collective-permute-start | bytes 460808 | tf_op jit(solution)/shard_map/ppermute | solution.py:22
  34.1 0.4 collective-permute-done.4
  34.5 0.9 collective-permute-done.5
  35.5 1.3 %collective-permute-start.12 = (bf16[48,3200]{1,0:T(8,128)(2,1)S(1)}, bf16[48,3200]{1,0:T(8,128)(2,1)S(1)}, u32[]{:S(2)}, u32[]{:S(2)}) collective-permute-start(bf16[48,3200]{1,0:T(8,128)(2,1)S(1)} %pad_maximum_fusion.1.refs_0_.refs_3_), channel_id=1, source_target_pairs={{0,1},{1,0},{2,3},{3,2},{4,5},{5,4},{6,7},{7,6},{8,9},{9,8},{10,11... | collective-permute-start | bytes 921608 | tf_op jit(solution)/shard_map/ppermute | solution.py:27
  36.8 0.3 collective-permute-done.9
  37.2 2.0 %copy-done.2 = bf16[1,576,3200]{2,1,0:T(8,128)(2,1)S(1)} copy-done((bf16[1,576,3200]{2,1,0:T(8,128)(2,1)S(1)}, bf16[1,576,3200]{2,1,0:T(8,128)(2,1)}, u32[]{:S(2)}) %copy-start.2) | copy-done | bytes 3686424
  39.4 4.7 %collective-permute-done.12.refs_7_ = bf16[48,3200]{1,0:T(8,128)(2,1)S(1)} collective-permute-done((bf16[48,3200]{1,0:T(8,128)(2,1)S(1)}, bf16[48,3200]{1,0:T(8,128)(2,1)S(1)}, u32[]{:S(2)}, u32[]{:S(2)}) %collective-permute-start.12) | collective-permute-done | bytes 307232 | tf_op jit(solution)/shard_map/ppermute | solution.py:27
  44.1 1.2 %collective-permute-start.14 = (bf16[24,3200]{1,0:T(8,128)(2,1)S(1)}, bf16[24,3200]{1,0:T(8,128)(2,1)S(1)}, u32[]{:S(2)}, u32[]{:S(2)}) collective-permute-start(bf16[24,3200]{1,0:T(8,128)(2,1)S(1)} %pad_maximum_fusion.9), channel_id=1, source_target_pairs={{0,1},{1,0},{2,3},{3,2},{4,5},{5,4},{6,7},{7,6},{8,9},{9,8},{10,11... | collective-permute-start | bytes 460808 | tf_op jit(solution)/shard_map/ppermute | solution.py:27
  45.3 5.9 %backward_expert.1 = (f32[64,3328]{1,0:T(8,128)S(1)}, bf16[64,3328]{1,0:T(8,128)(2,1)S(1)}) custom-call(bf16[16,3200]{1,0:T(8,128)(2,1)S(1)} %slice.163.refs_0_, bf16[32,3200]{1,0:T(8,128)(2,1)S(1)} %pad_maximum_fusion.5.refs_1_, bf16[32,3200]{1,0:T(8,128)(2,1)S(1)} %pad_maximum_fusion.6.refs_2_, bf16[48,3200]{1,0:T(8,128)(2,1)S(1)} %pad_maximum_fusion.1.refs_0_.refs_3_, ...), custom_call_target="tpu_custom_call" | custom-call | flops 2359296000 | bytes 11059200 | tf_op jit(solution)/shard_map/backward_expert/pallas_call | solution.py:204
  51.2 0.9 collective-permute-start.13
  52.1 3.2 %forward_expert.1 = (f32[64,3200]{1,0:T(8,128)S(1)}, bf16[64,3200]{1,0:T(8,128)(2,1)S(1)}) custom-call(bf16[64,3200]{1,0:T(8,128)(2,1)S(1)} %get-tuple-element.41.own, bf16[64,3200]{1,0:T(8,128)(2,1)S(1)} %constant_dynamic-update-slice_fusion.5.other, bf16[64,3328]{1,0:T(8,128)(2,1)S(1)} %get-tuple-element.21.after, bf16[576,3200]{1,0:T(8,128)(2,1)S(1)} %bitcast.14, ...), custom_call_target="tpu_custom_call" | custom-call | flops 1415577600 | bytes 11059200 | tf_op jit(solution)/shard_map/forward_expert/pallas_call | solution.py:204
  55.4 1.3 %collective-permute-start.15 = (bf16[64,3200]{1,0:T(8,128)(2,1)S(1)}, bf16[64,3200]{1,0:T(8,128)(2,1)S(1)}, u32[]{:S(2)}, u32[]{:S(2)}) collective-permute-start(bf16[64,3200]{1,0:T(8,128)(2,1)S(1)} %get-tuple-element.24), channel_id=1, source_target_pairs={{0,1},{1,0},{2,3},{3,2},{4,5},{5,4},{6,7},{7,6},{8,9},{9,8},{10,11... | collective-permute-start | bytes 1228808 | tf_op jit(solution)/shard_map/ppermute | solution.py:27
  56.7 6.2 %collective-permute-done.13 = bf16[64,3328]{1,0:T(8,128)(2,1)S(1)} collective-permute-done((bf16[64,3328]{1,0:T(8,128)(2,1)S(1)}, bf16[64,3328]{1,0:T(8,128)(2,1)S(1)}, u32[]{:S(2)}, u32[]{:S(2)}) %collective-permute-start.13) | collective-permute-done | bytes 426016 | tf_op jit(solution)/shard_map/ppermute | solution.py:27
  62.9 0.1 convert_add_fusion
  62.9 4.3 %collective-permute-done.15 = bf16[64,3200]{1,0:T(8,128)(2,1)S(1)} collective-permute-done((bf16[64,3200]{1,0:T(8,128)(2,1)S(1)}, bf16[64,3200]{1,0:T(8,128)(2,1)S(1)}, u32[]{:S(2)}, u32[]{:S(2)}) %collective-permute-start.15) | collective-permute-done | bytes 409632 | tf_op jit(solution)/shard_map/ppermute | solution.py:27
  67.2 0.1 convert_add_fusion.1
  67.4 0.1 fusion
  67.6 0.1 collective-permute-start.16
  67.7 3.3 %collective-permute-start.17 = (bf16[8,16256]{1,0:T(8,128)(2,1)S(1)}, bf16[8,16256]{1,0:T(8,128)(2,1)S(1)}, u32[]{:S(2)}, u32[]{:S(2)}) collective-permute-start(bf16[8,16256]{1,0:T(8,128)(2,1)S(1)} %pad_maximum_fusion.4), channel_id=1, source_target_pairs={{0,14},{1,15},{2,0},{3,1},{4,2},{5,3},{6,4},{7,5},{8,6},{9,7},{10,... | collective-permute-start | bytes 780296 | tf_op jit(solution)/shard_map/ppermute | solution.py:22
  71.0 0.5 collective-permute-start.21
  71.5 4.1 %collective-permute-done.17 = bf16[8,16256]{1,0:T(8,128)(2,1)S(1)} collective-permute-done((bf16[8,16256]{1,0:T(8,128)(2,1)S(1)}, bf16[8,16256]{1,0:T(8,128)(2,1)S(1)}, u32[]{:S(2)}, u32[]{:S(2)}) %collective-permute-start.17) | collective-permute-done | bytes 260128 | tf_op jit(solution)/shard_map/ppermute | solution.py:22
  75.7 0.1 fusion.7
  75.9 2.4 %collective-permute-start.19 = (bf16[8,6528]{1,0:T(8,128)(2,1)S(1)}, bf16[8,6528]{1,0:T(8,128)(2,1)S(1)}, u32[]{:S(2)}, u32[]{:S(2)}) collective-permute-start(bf16[8,6528]{1,0:T(8,128)(2,1)S(1)} %pad_maximum_fusion.11), channel_id=1, source_target_pairs={{0,10},{1,11},{2,12},{3,13},{4,14},{5,15},{6,0},{7,1},{8,2},{9,3},... | collective-permute-start | bytes 313352 | tf_op jit(solution)/shard_map/ppermute | solution.py:22
  78.3 4.5 %collective-permute-start.18 = (bf16[8,6528]{1,0:T(8,128)(2,1)S(1)}, bf16[8,6528]{1,0:T(8,128)(2,1)S(1)}, u32[]{:S(2)}, u32[]{:S(2)}) collective-permute-start(bf16[8,6528]{1,0:T(8,128)(2,1)S(1)} %pad_maximum_fusion.10), channel_id=1, source_target_pairs={{0,6},{1,7},{2,8},{3,9},{4,10},{5,11},{6,12},{7,13},{8,14},{9,15},... | collective-permute-start | bytes 313352 | tf_op jit(solution)/shard_map/ppermute | solution.py:22
  82.8 3.8 %collective-permute-done.19.refs_2_ = bf16[8,6528]{1,0:T(8,128)(2,1)S(1)} collective-permute-done((bf16[8,6528]{1,0:T(8,128)(2,1)S(1)}, bf16[8,6528]{1,0:T(8,128)(2,1)S(1)}, u32[]{:S(2)}, u32[]{:S(2)}) %collective-permute-start.19) | collective-permute-done | bytes 104480 | tf_op jit(solution)/shard_map/ppermute | solution.py:22
  86.5 3.1 %collective-permute-done.18.refs_1_ = bf16[8,6528]{1,0:T(8,128)(2,1)S(1)} collective-permute-done((bf16[8,6528]{1,0:T(8,128)(2,1)S(1)}, bf16[8,6528]{1,0:T(8,128)(2,1)S(1)}, u32[]{:S(2)}, u32[]{:S(2)}) %collective-permute-start.18) | collective-permute-done | bytes 104480 | tf_op jit(solution)/shard_map/ppermute | solution.py:22
  89.6 0.3 rows.1
  90.0 0.1 collective-permute-start.22
  90.1 0.5 collective-permute-start.20
  90.6 1.3 %collective-permute-done.22.moved = bf16[8,3328]{1,0:T(8,128)(2,1)S(1)} collective-permute-done((bf16[8,3328]{1,0:T(8,128)(2,1)S(1)}, bf16[8,3328]{1,0:T(8,128)(2,1)S(1)}, u32[]{:S(2)}, u32[]{:S(2)}) %collective-permute-start.22) | collective-permute-done | bytes 53280 | tf_op jit(solution)/shard_map/ppermute | solution.py:37
  91.9 1.2 %finish.3 = bf16[64,3200]{1,0:T(8,128)(2,1)} custom-call(bf16[8,3328]{1,0:T(8,128)(2,1)S(1)} %collective-permute-done.22.moved, bf16[64,3200]{1,0:T(8,128)(2,1)S(1)} %collective-permute-done.23.tokens), custom_call_target="tpu_custom_call" | custom-call | tf_op jit(solution)/shard_map/finish/pallas_call | solution.py:311
  93.0 4.3 %collective-permute-done.20.moved = bf16[8,3328]{1,0:T(8,128)(2,1)S(1)} collective-permute-done((bf16[8,3328]{1,0:T(8,128)(2,1)S(1)}, bf16[8,3328]{1,0:T(8,128)(2,1)S(1)}, u32[]{:S(2)}, u32[]{:S(2)}) %collective-permute-start.20) | collective-permute-done | bytes 53280 | tf_op jit(solution)/shard_map/ppermute | solution.py:37
  97.3 1.2 %finish.2 = bf16[64,3200]{1,0:T(8,128)(2,1)} custom-call(bf16[8,3328]{1,0:T(8,128)(2,1)S(1)} %collective-permute-done.20.moved, bf16[64,3200]{1,0:T(8,128)(2,1)S(1)} %collective-permute-done.21.tokens), custom_call_target="tpu_custom_call" | custom-call | tf_op jit(solution)/shard_map/finish/pallas_call | solution.py:311
  (77 shorter events, 0.7 us)
Async XLA Ops:
  1.9 35.3 %copy-start.1 = (bf16[1,3200,576]{1,2,0:T(8,128)(2,1)S(1)}, bf16[1,3200,576]{1,2,0:T(8,128)(2,1)}, u32[]{:S(2)}) copy-start(bf16[1,3200,576]{1,2,0:T(8,128)(2,1)} %param.22) | copy-start | bytes 11059204
  5.0 20.8 %collective-permute-start = (bf16[24,3200]{1,0:T(8,128)(2,1)}, bf16[24,3200]{1,0:T(8,128)(2,1)S(1)}, u32[]{:S(2)}, u32[]{:S(2)}) collective-permute-start(bf16[24,3200]{1,0:T(8,128)(2,1)} %get-tuple-element.17), channel_id=1, source_target_pairs={{0,2},{1,3},{2,4},{3,5},{4,6},{5,7},{6,8},{7,9},{8,10},{9,11},{10,... | collective-permute-start | bytes 460808 | tf_op jit(solution)/shard_map/ppermute | solution.py:22
  7.0 20.1 %collective-permute-start.1 = (bf16[24,3200]{1,0:T(8,128)(2,1)}, bf16[24,3200]{1,0:T(8,128)(2,1)S(1)}, u32[]{:S(2)}, u32[]{:S(2)}) collective-permute-start(bf16[24,3200]{1,0:T(8,128)(2,1)} %get-tuple-element.17), channel_id=1, source_target_pairs={{0,14},{1,15},{2,0},{3,1},{4,2},{5,3},{6,4},{7,5},{8,6},{9,7},{10,... | collective-permute-start | bytes 460808 | tf_op jit(solution)/shard_map/ppermute | solution.py:22
  11.0 10.2 %collective-permute-start.2 = (bf16[24,3200]{1,0:T(8,128)(2,1)}, bf16[24,3200]{1,0:T(8,128)(2,1)S(1)}, u32[]{:S(2)}, u32[]{:S(2)}) collective-permute-start(bf16[24,3200]{1,0:T(8,128)(2,1)} %get-tuple-element.17), channel_id=1, source_target_pairs={{0,4},{1,5},{2,6},{3,7},{4,8},{5,9},{6,10},{7,11},{8,12},{9,13},{1... | collective-permute-start | bytes 460808 | tf_op jit(solution)/shard_map/ppermute | solution.py:22
  11.0 11.6 %collective-permute-start.3 = (bf16[24,3200]{1,0:T(8,128)(2,1)}, bf16[24,3200]{1,0:T(8,128)(2,1)S(1)}, u32[]{:S(2)}, u32[]{:S(2)}) collective-permute-start(bf16[24,3200]{1,0:T(8,128)(2,1)} %get-tuple-element.17), channel_id=1, source_target_pairs={{0,12},{1,13},{2,14},{3,15},{4,0},{5,1},{6,2},{7,3},{8,4},{9,5},{1... | collective-permute-start | bytes 460808 | tf_op jit(solution)/shard_map/ppermute | solution.py:22
  15.1 13.8 %collective-permute-start.8 = (bf16[24,3200]{1,0:T(8,128)(2,1)}, bf16[24,3200]{1,0:T(8,128)(2,1)S(1)}, u32[]{:S(2)}, u32[]{:S(2)}) collective-permute-start(bf16[24,3200]{1,0:T(8,128)(2,1)} %get-tuple-element.17), channel_id=1, source_target_pairs={{0,1},{1,0},{2,3},{3,2},{4,5},{5,4},{6,7},{7,6},{8,9},{9,8},{10,11... | collective-permute-start | bytes 460808 | tf_op jit(solution)/shard_map/ppermute | solution.py:27
  21.2 9.4 %collective-permute-start.6 = (bf16[24,1536]{1,0:T(8,128)(2,1)S(1)}, bf16[24,1536]{1,0:T(8,128)(2,1)S(1)}, u32[]{:S(2)}, u32[]{:S(2)}) collective-permute-start(bf16[24,1536]{1,0:T(8,128)(2,1)S(1)} %slice.216), channel_id=1, source_target_pairs={{0,4},{1,5},{2,6},{3,7},{4,8},{5,9},{6,10},{7,11},{8,12},{9,13},{1... | collective-permute-start | bytes 221192 | tf_op jit(solution)/shard_map/ppermute | solution.py:22
  22.6 8.6 %collective-permute-start.7 = (bf16[24,1664]{1,0:T(8,128)(2,1)S(1)}, bf16[24,1664]{1,0:T(8,128)(2,1)S(1)}, u32[]{:S(2)}, u32[]{:S(2)}) collective-permute-start(bf16[24,1664]{1,0:T(8,128)(2,1)S(1)} %slice.217), channel_id=1, source_target_pairs={{0,12},{1,13},{2,14},{3,15},{4,0},{5,1},{6,2},{7,3},{8,4},{9,5},{1... | collective-permute-start | bytes 239624 | tf_op jit(solution)/shard_map/ppermute | solution.py:22
  25.7 13.6 %collective-permute-start.11 = (bf16[48,3200]{1,0:T(8,128)(2,1)S(1)}, bf16[48,3200]{1,0:T(8,128)(2,1)S(1)}, u32[]{:S(2)}, u32[]{:S(2)}) collective-permute-start(bf16[48,3200]{1,0:T(8,128)(2,1)S(1)} %pad_maximum_fusion.2), channel_id=1, source_target_pairs={{0,1},{1,0},{2,3},{3,2},{4,5},{5,4},{6,7},{7,6},{8,9},{9,8},{10,11... | collective-permute-start | bytes 921608 | tf_op jit(solution)/shard_map/ppermute | solution.py:27
  27.1 7.4 %collective-permute-start.4 = (bf16[24,3200]{1,0:T(8,128)(2,1)S(1)}, bf16[24,3200]{1,0:T(8,128)(2,1)S(1)}, u32[]{:S(2)}, u32[]{:S(2)}) collective-permute-start(bf16[24,3200]{1,0:T(8,128)(2,1)S(1)} %collective-permute-done.2), channel_id=1, source_target_pairs={{0,2},{1,3},{2,4},{3,5},{4,6},{5,7},{6,8},{7,9},{8,10},{9,11},{10,... | collective-permute-start | bytes 460808 | tf_op jit(solution)/shard_map/ppermute | solution.py:22
  28.9 8.3 %copy-start = (bf16[1,3200,576]{1,2,0:T(8,128)(2,1)S(1)}, bf16[1,3200,576]{1,2,0:T(8,128)(2,1)}, u32[]{:S(2)}) copy-start(bf16[1,3200,576]{1,2,0:T(8,128)(2,1)} %param.21) | copy-start | bytes 11059204
  29.0 6.5 %collective-permute-start.5 = (bf16[24,3200]{1,0:T(8,128)(2,1)S(1)}, bf16[24,3200]{1,0:T(8,128)(2,1)S(1)}, u32[]{:S(2)}, u32[]{:S(2)}) collective-permute-start(bf16[24,3200]{1,0:T(8,128)(2,1)S(1)} %collective-permute-done.3), channel_id=1, source_target_pairs={{0,14},{1,15},{2,0},{3,1},{4,2},{5,3},{6,4},{7,5},{8,6},{9,7},{10,... | collective-permute-start | bytes 460808 | tf_op jit(solution)/shard_map/ppermute | solution.py:22
  30.6 6.5 %collective-permute-start.9 = (bf16[24,3200]{1,0:T(8,128)(2,1)S(1)}, bf16[24,3200]{1,0:T(8,128)(2,1)S(1)}, u32[]{:S(2)}, u32[]{:S(2)}) collective-permute-start(bf16[24,3200]{1,0:T(8,128)(2,1)S(1)} %collective-permute-done.8), channel_id=1, source_target_pairs={{0,2},{1,3},{2,4},{3,5},{4,6},{5,7},{6,8},{7,9},{8,10},{9,11},{10,... | collective-permute-start | bytes 460808 | tf_op jit(solution)/shard_map/ppermute | solution.py:22
  31.2 6.0 %collective-permute-start.10 = (bf16[24,3200]{1,0:T(8,128)(2,1)S(1)}, bf16[24,3200]{1,0:T(8,128)(2,1)S(1)}, u32[]{:S(2)}, u32[]{:S(2)}) collective-permute-start(bf16[24,3200]{1,0:T(8,128)(2,1)S(1)} %collective-permute-done.8), channel_id=1, source_target_pairs={{0,14},{1,15},{2,0},{3,1},{4,2},{5,3},{6,4},{7,5},{8,6},{9,7},{10,... | collective-permute-start | bytes 460808 | tf_op jit(solution)/shard_map/ppermute | solution.py:22
  35.5 8.6 %collective-permute-start.12 = (bf16[48,3200]{1,0:T(8,128)(2,1)S(1)}, bf16[48,3200]{1,0:T(8,128)(2,1)S(1)}, u32[]{:S(2)}, u32[]{:S(2)}) collective-permute-start(bf16[48,3200]{1,0:T(8,128)(2,1)S(1)} %pad_maximum_fusion.1.refs_0_.refs_3_), channel_id=1, source_target_pairs={{0,1},{1,0},{2,3},{3,2},{4,5},{5,4},{6,7},{7,6},{8,9},{9,8},{10,11... | collective-permute-start | bytes 921608 | tf_op jit(solution)/shard_map/ppermute | solution.py:27
  37.2 2.0 %copy-start.2 = (bf16[1,576,3200]{2,1,0:T(8,128)(2,1)S(1)}, bf16[1,576,3200]{2,1,0:T(8,128)(2,1)}, u32[]{:S(2)}) copy-start(bf16[1,576,3200]{2,1,0:T(8,128)(2,1)} %param.23) | copy-start | bytes 11059204
  39.2 6.1 %copy-start.3 = (bf16[1,576,3200]{2,1,0:T(8,128)(2,1)S(1)}, bf16[1,576,3200]{2,1,0:T(8,128)(2,1)}, u32[]{:S(2)}) copy-start(bf16[1,576,3200]{2,1,0:T(8,128)(2,1)} %param.23) | copy-start | bytes 11059204
  44.1 8.0 %collective-permute-start.14 = (bf16[24,3200]{1,0:T(8,128)(2,1)S(1)}, bf16[24,3200]{1,0:T(8,128)(2,1)S(1)}, u32[]{:S(2)}, u32[]{:S(2)}) collective-permute-start(bf16[24,3200]{1,0:T(8,128)(2,1)S(1)} %pad_maximum_fusion.9), channel_id=1, source_target_pairs={{0,1},{1,0},{2,3},{3,2},{4,5},{5,4},{6,7},{7,6},{8,9},{9,8},{10,11... | collective-permute-start | bytes 460808 | tf_op jit(solution)/shard_map/ppermute | solution.py:27
  51.2 11.6 %collective-permute-start.13 = (bf16[64,3328]{1,0:T(8,128)(2,1)S(1)}, bf16[64,3328]{1,0:T(8,128)(2,1)S(1)}, u32[]{:S(2)}, u32[]{:S(2)}) collective-permute-start(bf16[64,3328]{1,0:T(8,128)(2,1)S(1)} %get-tuple-element.21.after), channel_id=1, source_target_pairs={{0,1},{1,0},{2,3},{3,2},{4,5},{5,4},{6,7},{7,6},{8,9},{9,8},{10,11... | collective-permute-start | bytes 1277960 | tf_op jit(solution)/shard_map/ppermute | solution.py:27
  55.4 11.9 %collective-permute-start.15 = (bf16[64,3200]{1,0:T(8,128)(2,1)S(1)}, bf16[64,3200]{1,0:T(8,128)(2,1)S(1)}, u32[]{:S(2)}, u32[]{:S(2)}) collective-permute-start(bf16[64,3200]{1,0:T(8,128)(2,1)S(1)} %get-tuple-element.24), channel_id=1, source_target_pairs={{0,1},{1,0},{2,3},{3,2},{4,5},{5,4},{6,7},{7,6},{8,9},{9,8},{10,11... | collective-permute-start | bytes 1228808 | tf_op jit(solution)/shard_map/ppermute | solution.py:27
  67.3 3.6 %copy-start.6 = (bf16[1,64,3200]{2,1,0:T(8,128)(2,1)S(1)}, bf16[1,64,3200]{2,1,0:T(8,128)(2,1)}, u32[]{:S(2)}) copy-start(bf16[1,64,3200]{2,1,0:T(8,128)(2,1)} %param.16) | copy-start | bytes 1228804
  67.4 3.6 %copy-start.7 = (bf16[1,64,3200]{2,1,0:T(8,128)(2,1)S(1)}, bf16[1,64,3200]{2,1,0:T(8,128)(2,1)}, u32[]{:S(2)}) copy-start(bf16[1,64,3200]{2,1,0:T(8,128)(2,1)} %param.12) | copy-start | bytes 1228804
  67.6 8.1 %collective-permute-start.16 = (bf16[8,16384]{1,0:T(8,128)(2,1)S(1)}, bf16[8,16384]{1,0:T(8,128)(2,1)S(1)}, u32[]{:S(2)}, u32[]{:S(2)}) collective-permute-start(bf16[8,16384]{1,0:T(8,128)(2,1)S(1)} %pad_maximum_fusion.3), channel_id=1, source_target_pairs={{0,2},{1,3},{2,4},{3,5},{4,6},{5,7},{6,8},{7,9},{8,10},{9,11},{10,... | collective-permute-start | bytes 786440 | tf_op jit(solution)/shard_map/ppermute | solution.py:22
  67.7 7.9 %collective-permute-start.17 = (bf16[8,16256]{1,0:T(8,128)(2,1)S(1)}, bf16[8,16256]{1,0:T(8,128)(2,1)S(1)}, u32[]{:S(2)}, u32[]{:S(2)}) collective-permute-start(bf16[8,16256]{1,0:T(8,128)(2,1)S(1)} %pad_maximum_fusion.4), channel_id=1, source_target_pairs={{0,14},{1,15},{2,0},{3,1},{4,2},{5,3},{6,4},{7,5},{8,6},{9,7},{10,... | collective-permute-start | bytes 780296 | tf_op jit(solution)/shard_map/ppermute | solution.py:22
  71.0 19.6 %collective-permute-start.23 = (bf16[64,3200]{1,0:T(8,128)(2,1)S(1)}, bf16[64,3200]{1,0:T(8,128)(2,1)S(1)}, u32[]{:S(2)}, u32[]{:S(2)}) collective-permute-start(bf16[64,3200]{1,0:T(8,128)(2,1)S(1)} %bitcast.25), channel_id=1, source_target_pairs={{0,240},{1,241},{2,242},{3,243},{4,244},{5,245},{6,246},{7,247},{8... | collective-permute-start | bytes 1228808 | tf_op jit(solution)/shard_map/ppermute | solution.py:37
  71.0 22.0 %collective-permute-start.21 = (bf16[64,3200]{1,0:T(8,128)(2,1)S(1)}, bf16[64,3200]{1,0:T(8,128)(2,1)S(1)}, u32[]{:S(2)}, u32[]{:S(2)}) collective-permute-start(bf16[64,3200]{1,0:T(8,128)(2,1)S(1)} %bitcast.27), channel_id=1, source_target_pairs={{0,16},{1,17},{2,18},{3,19},{4,20},{5,21},{6,22},{7,23},{8,24},{9,... | collective-permute-start | bytes 1228808 | tf_op jit(solution)/shard_map/ppermute | solution.py:37
  75.7 14.0 %copy-start.4 = (f32[24,3328]{1,0:T(8,128)S(1)}, f32[24,3328]{1,0:T(8,128)}, u32[]{:S(2)}) copy-start(f32[24,3328]{1,0:T(8,128)} %get-tuple-element.27.refs_4_) | copy-start | bytes 958468
  75.7 14.0 %copy-start.5 = (f32[8,3328]{1,0:T(8,128)S(1)}, f32[8,3328]{1,0:T(8,128)}, u32[]{:S(2)}) copy-start(f32[8,3328]{1,0:T(8,128)} %get-tuple-element.26.refs_3_) | copy-start | bytes 319492
  75.9 10.7 %collective-permute-start.19 = (bf16[8,6528]{1,0:T(8,128)(2,1)S(1)}, bf16[8,6528]{1,0:T(8,128)(2,1)S(1)}, u32[]{:S(2)}, u32[]{:S(2)}) collective-permute-start(bf16[8,6528]{1,0:T(8,128)(2,1)S(1)} %pad_maximum_fusion.11), channel_id=1, source_target_pairs={{0,10},{1,11},{2,12},{3,13},{4,14},{5,15},{6,0},{7,1},{8,2},{9,3},... | collective-permute-start | bytes 313352 | tf_op jit(solution)/shard_map/ppermute | solution.py:22
  78.3 11.4 %collective-permute-start.18 = (bf16[8,6528]{1,0:T(8,128)(2,1)S(1)}, bf16[8,6528]{1,0:T(8,128)(2,1)S(1)}, u32[]{:S(2)}, u32[]{:S(2)}) collective-permute-start(bf16[8,6528]{1,0:T(8,128)(2,1)S(1)} %pad_maximum_fusion.10), channel_id=1, source_target_pairs={{0,6},{1,7},{2,8},{3,9},{4,10},{5,11},{6,12},{7,13},{8,14},{9,15},... | collective-permute-start | bytes 313352 | tf_op jit(solution)/shard_map/ppermute | solution.py:22
  90.0 1.9 %collective-permute-start.22 = (bf16[8,3328]{1,0:T(8,128)(2,1)S(1)}, bf16[8,3328]{1,0:T(8,128)(2,1)S(1)}, u32[]{:S(2)}, u32[]{:S(2)}) collective-permute-start(bf16[8,3328]{1,0:T(8,128)(2,1)S(1)} %get-tuple-element.30), channel_id=1, source_target_pairs={{0,240},{1,241},{2,242},{3,243},{4,244},{5,245},{6,246},{7,247},{8... | collective-permute-start | bytes 159752 | tf_op jit(solution)/shard_map/ppermute | solution.py:37
  90.1 7.3 %collective-permute-start.20 = (bf16[8,3328]{1,0:T(8,128)(2,1)S(1)}, bf16[8,3328]{1,0:T(8,128)(2,1)S(1)}, u32[]{:S(2)}, u32[]{:S(2)}) collective-permute-start(bf16[8,3328]{1,0:T(8,128)(2,1)S(1)} %get-tuple-element.28), channel_id=1, source_target_pairs={{0,16},{1,17},{2,18},{3,19},{4,20},{5,21},{6,22},{7,23},{8,24},{9,... | collective-permute-start | bytes 159752 | tf_op jit(solution)/shard_map/ppermute | solution.py:37
